TPU v7x, 32 devices: a whole 2x2x4 slice. The times are simulated.
32 devices in a mesh: groups: 2 (over x), seq: 16 (over z, y, core).
Axes of the slice: x: 2, y: 2, z: 4, core: 2. Of those that a mesh axis runs over, the one named last changes fastest.
Arguments:
- tokens: bfloat16 [12288, 5120], P(('groups', 'seq')), parts along dimension 0, may hold values from -6 to 6
- token_adapter_index: int32 [12288], P(('groups', 'seq')), parts along dimension 0, may hold values from 0 to 7
- frozen_value_weight: bfloat16 [5120, 1024], P('seq'), may hold values from -0.078125 to 0.078125
- weight_block_scale: float32 [40, 8], replicated, may hold values from 0.5 to 2
- down_adapter_weight: bfloat16 [10240, 128], P('groups'), parts along dimension 0, may hold values from -0.078125 to 0.078125
- up_adapter_weight: bfloat16 [256, 1024], P('groups'), parts along dimension 0, may hold values from -1.5 to 1.5
- cotangent: bfloat16 [12288, 1024], P(('groups', 'seq')), parts along dimension 0, may hold values from -6 to 6
Outputs:
- values: bfloat16 [12288, 1024], P(('groups', 'seq')), parts along dimension 0
- activation_gradient: bfloat16 [12288, 5120], P(('groups', 'seq')), parts along dimension 0
- grad_a: float32 [10240, 128], P(('groups', 'seq')), parts along dimension 0
- grad_b: float32 [256, 1024], P('groups'), parts along dimension 0
There are 2 independent parts, one for each index of `groups`. A program takes and returns all parts, laid end to end along the dimension named above; an argument that names none is the same for every part. Nothing has to cross between parts.
All inputs are finite; a program needn't handle non-finite values.
Results may differ from a plain program's by a relative error of at most 0.005.
Values may be sent and summed in bfloat16 or wider, within the bound.
No kernel may reach another device: no remote copies, remote signals or barrier semaphores. Data moves between devices by JAX's collectives and lax.ppermute only.
A program may use at most 128 MiB of HBM per device.

v0:
```python
import jax
import jax.numpy as jnp
from jax import lax
from jax.sharding import PartitionSpec as P

BLOCK = 128
ADAPTER_RANK = 16


def dequant_rows(piece, scales):
    count = piece.shape[0]
    block_of = lax.iota(jnp.int32, count) // BLOCK
    select = (block_of[:, None] == lax.iota(jnp.int32, scales.shape[0])[None, :]).astype(
        jnp.float32
    )
    row_scales = jnp.dot(select, scales, precision=lax.Precision.HIGHEST)
    expanded = jnp.repeat(row_scales, BLOCK, axis=1)
    return (piece.astype(jnp.float32) * expanded).astype(jnp.bfloat16)


def reduce_over_rows(left, right):
    return lax.dot_general(
        left, right, (((1,), (1,)), ((), ())), preferred_element_type=jnp.float32
    )


def contract_tokens(left, right):
    return lax.dot_general(
        left, right, (((0,), (0,)), ((), ())), preferred_element_type=jnp.float32
    )


def on_device(
    tokens,
    token_adapter_index,
    frozen_value_weight,
    weight_block_scale,
    down_adapter_weight,
    up_adapter_weight,
    cotangent,
):
    token_adapter_mask = lax.iota(jnp.int32, down_adapter_weight.shape[1]) // ADAPTER_RANK
    adapter_choice_mask = (token_adapter_index[:, None] == token_adapter_mask[None, :]).astype(
        jnp.float32
    )
    down_projected = (
        jnp.dot(tokens, down_adapter_weight, preferred_element_type=jnp.float32)
        * adapter_choice_mask
    ).astype(jnp.bfloat16)
    adapter_output = 2.0 * jnp.dot(
        down_projected, up_adapter_weight, preferred_element_type=jnp.float32
    )
    expanded_rank_mask = (
        2.0 * reduce_over_rows(cotangent, up_adapter_weight) * adapter_choice_mask
    ).astype(jnp.bfloat16)
    adapter_backward = reduce_over_rows(expanded_rank_mask, down_adapter_weight)
    gathered = lax.all_gather(frozen_value_weight, "seq", axis=0, tiled=True)
    weight = dequant_rows(gathered, weight_block_scale)
    forward_pass = jnp.dot(tokens, weight, preferred_element_type=jnp.float32)
    backward_pass = reduce_over_rows(cotangent, weight)
    values = (forward_pass + adapter_output).astype(jnp.bfloat16)
    activation_gradient = (backward_pass + adapter_backward).astype(jnp.bfloat16)
    grad_a = lax.psum_scatter(
        contract_tokens(tokens, expanded_rank_mask), "seq", scatter_dimension=0, tiled=True
    )
    grad_b = lax.psum(2.0 * contract_tokens(down_projected, cotangent), "seq")
    return (values, activation_gradient, grad_a, grad_b)


def solution(mesh):
    return jax.shard_map(
        on_device,
        mesh=mesh,
        in_specs=(
            P(("groups", "seq"), None),
            P(("groups", "seq")),
            P("seq", None),
            P(),
            P("groups", None),
            P("groups", None),
            P(("groups", "seq"), None),
        ),
        out_specs=(
            P(("groups", "seq"), None),
            P(("groups", "seq"), None),
            P(("groups", "seq"), None),
            P("groups", None),
        ),
        check_vma=False,
    )
```

profile of v0, /device:TPU:0, one launch (start us, length us, event | category | flops | bytes accessed | tf_op | source)
XLA Modules:
  0.0 270.3 jit_solution(2155401548215772439)
XLA Ops:
  7.2 0.0 all-gather.2.cloned.1.call-start
  7.3 0.7 all-gather.2.cloned.1.call-update
  7.9 0.0 all-reduce.2.cloned.1.call-start
  8.0 0.7 copy-done
  8.7 3.3 %fusion.4 = bf16[384,128]{1,0:T(8,128)(2,1)S(1)} fusion(bf16[384,5120]{1,0:T(8,128)(2,1)} %param.7, bf16[5120,128]{1,0:T(8,128)(2,1)S(1)} %copy-done, s32[128]{0:T(128)S(1)} %and_select_fusion, s32[384]{0:T(512)} %param.8), kind=kOutput, calls=%fused_computation.11 | convolution fusion | flops 503463936 | bytes 5343232 | tf_op jit(solution)/shard_map/dot_general | solution.py:47
  12.0 1.1 convolution_multiply_fusion
  13.2 0.0 all-reduce.2.cloned.1.call-update
  13.2 0.0 reduce-scatter.4.cloned.1.call-start
  13.2 0.4 fusion.5
  13.6 4.5 %convolution_bitcast_fusion = f32[5120,128]{0,1:T(8,128)} fusion(bf16[384,128]{1,0:T(8,128)(2,1)S(1)} %fusion.5, bf16[384,5120]{1,0:T(8,128)(2,1)} %param.7), kind=kOutput, calls=%fused_computation.4 | convolution fusion | flops 503316480 | bytes 6651904 | tf_op jit(solution)/shard_map/dot_general | solution.py:28
  18.1 3.3 %copy.32 = f32[5120,128]{1,0:T(8,128)} copy(f32[5120,128]{0,1:T(8,128)} %convolution_bitcast_fusion) | data formatting | bytes 5242880
  21.4 0.0 reduce-scatter.4.cloned.1.call-update
  21.4 0.4 fusion.16
  21.8 3.0 %fusion.7 = f32[5120,8]{1,0:T(8,128)} fusion(f32[40,8]{0,1:T(8,128)S(1)} %copy-done.3, s32[5120]{0:T(1024)S(1)} %add_select_fusion), kind=kOutput, calls=%fused_computation.15 | convolution fusion | flops 20070400 | bytes 185600 | tf_op jit(solution)/shard_map/dot_general | solution.py:16
  24.8 76.2 %all-gather.2.cloned.1.call-done = bf16[5120,1024]{1,0:T(8,128)(2,1)} async-done(((bf16[320,1024]{1,0:T(8,128)(2,1)}), bf16[5120,1024]{1,0:T(8,128)(2,1)}) %all-gather.2.cloned.1.call-update) | async-done | bytes 10485776 | tf_op jit(solution)/shard_map/all_gather | solution.py:57
  100.9 11.5 %broadcast_in_dim.2 = f32[5120,8,128]{2,1,0:T(8,128)} broadcast(f32[5120,8]{1,0:T(8,128)} %fusion.7), dimensions={0,1} | broadcast | bytes 21135360 | tf_op jit(solution)/shard_map/broadcast_in_dim | solution.py:17
  112.4 20.0 %fusion.2 = bf16[384,1024]{0,1:T(8,128)(2,1)} fusion(f32[384,1024]{0,1:T(8,128)S(1)} %fusion.16, bf16[384,5120]{1,0:T(8,128)(2,1)} %param.7, f32[640,8,8,128]{3,2,1,0:T(8,128)} %bitcast.33, bf16[5120,1024]{1,0:T(8,128)(2,1)} %all-gather.2.cloned.1.call-done), kind=kOutput, calls=%fused_computation.6 | convolution fusion | flops 4043440128 | bytes 37748736 | tf_op jit(solution)/shard_map/dot_general | solution.py:59
  132.4 2.3 copy.26
  134.7 14.5 %fusion.13 = f32[5120,384]{1,0:T(8,128)S(1)} fusion(bf16[384,1024]{1,0:T(8,128)(2,1)} %param.13, f32[640,8,8,128]{3,2,1,0:T(8,128)} %bitcast.34, bf16[5120,1024]{1,0:T(8,128)(2,1)} %all-gather.2.cloned.1.call-done), kind=kOutput, calls=%fused_computation.28 | convolution fusion | flops 4042260480 | bytes 40108032 | tf_op jit(solution)/shard_map/dot_general | solution.py:22
  149.2 3.1 %fusion.1 = bf16[384,5120]{0,1:T(8,128)(2,1)} fusion(f32[5120,384]{1,0:T(8,128)S(1)} %fusion.13, bf16[384,128]{1,0:T(8,128)(2,1)S(1)} %fusion.5, bf16[5120,128]{1,0:T(8,128)(2,1)S(1)} %copy-done), kind=kOutput, calls=%fused_computation.3 | convolution fusion | flops 507248640 | bytes 13205504 | tf_op jit(solution)/shard_map/dot_general | solution.py:22
  152.3 6.3 %copy.27 = bf16[384,5120]{1,0:T(8,128)(2,1)} copy(bf16[384,5120]{0,1:T(8,128)(2,1)} %fusion.1) | data formatting | bytes 7864320
  158.6 34.6 %all-reduce.2.cloned.1.call-done = f32[128,1024]{1,0:T(8,128)} async-done(((f32[128,1024]{1,0:T(8,128)}), f32[128,1024]{1,0:T(8,128)}) %all-reduce.2.cloned.1.call-update) | async-done | bytes 524304 | tf_op jit(solution)/shard_map/psum | solution.py:66
  193.2 68.7 %reduce-scatter.4.cloned.1.call-done = f32[320,128]{1,0:T(8,128)} async-done(((f32[5120,128]{1,0:T(8,128)}), f32[320,128]{1,0:T(8,128)}) %reduce-scatter.4.cloned.1.call-update) | async-done | bytes 163856
  261.9 1.9 copy.39
  (11 shorter events, 0.0 us)
Async XLA Ops:
  7.2 1.6 copy-start
  7.2 6.0 %copy-start.4 = (s32[384]{0:T(512)S(1)}, s32[384]{0:T(512)}, u32[]{:S(2)}) copy-start(s32[384]{0:T(512)} %param.8) | copy-start | bytes 4612
  7.2 4.8 %copy-start.1 = (bf16[384,1024]{1,0:T(8,128)(2,1)S(1)}, bf16[384,1024]{1,0:T(8,128)(2,1)}, u32[]{:S(2)}) copy-start(bf16[384,1024]{1,0:T(8,128)(2,1)} %param.13) | copy-start | bytes 2359300
  7.2 6.0 %copy-start.2 = (bf16[128,1024]{1,0:T(8,128)(2,1)S(1)}, bf16[128,1024]{1,0:T(8,128)(2,1)}, u32[]{:S(2)}) copy-start(bf16[128,1024]{1,0:T(8,128)(2,1)} %param.12) | copy-start | bytes 786436
  7.2 93.7 %all-gather.2.cloned.1.call-start = ((), (), s32[]{:S(2)}) async-start(), calls=%async_computation.1 | async-start | bytes 11141120 | tf_op jit(solution)/shard_map/all_gather | solution.py:57
  7.9 185.3 %all-reduce.2.cloned.1.call-start = ((), (), s32[]{:S(2)}) async-start(), calls=%async_computation.2 | async-start | bytes 1048576 | tf_op jit(solution)/shard_map/psum | solution.py:66
  13.2 248.8 %reduce-scatter.4.cloned.1.call-start = ((), (), s32[]{:S(2)}) async-start(), calls=%async_computation.3 | async-start | bytes 2785280
  18.1 3.7 %copy-start.3 = (f32[40,8]{0,1:T(8,128)S(1)}, f32[40,8]{0,1:T(8,128)}, u32[]{:S(2)}) copy-start(f32[40,8]{0,1:T(8,128)} %param.10) | copy-start | bytes 3844
Sparse Core Ops, SparseCore 0:
  10.3 90.5 all-gather.1
  104.9 88.2 all-reduce.1
  197.6 64.3 reduce-scatter.3
where the time goes:
time: 271 us; the launch traced here: 270 us
  waiting for transfers between devices  180 us (66%)
  matrix products  50.2 us (19%)
  local copies, waits for them, and re-layouts  25.9 us (10%)
  between operations  13.9 us (5%)
    all_gather x1, waiting for transfers between devices, on_device(): gathered = lax.all_gather(frozen_value_weight, 'seq', axis=0, tiled=True)  76.2 us
    unnamed x4, waiting for transfers between devices  69.4 us
    psum x1, waiting for transfers between devices, on_device(): grad_b = lax.psum(2.0 * contract_tokens(down_projected, cotangent), 'seq')  34.6 us
    dot_general x1, matrix products, on_device(): forward_pass = jnp.dot(tokens, weight, preferred_element_type=jnp.float32)  20 us
    dot_general x3, matrix products, reduce_over_rows(): lax.dot_general(left, right, (((1,), (1,)), ((), ())), preferred_element_...  18 us
    unnamed x14, local copies, waits for them, and re-layouts  14.4 us
    broadcast_in_dim x1, local copies, waits for them, and re-layouts, dequant_rows(): expanded = jnp.repeat(row_scales, BLOCK, axis=1)  11.5 us
    dot_general x2, matrix products, contract_tokens(): lax.dot_general(left, right, (((0,), (0,)), ((), ())), preferred_element_...  5.61 us
  transfers between devices with their start and end apart: 3, of which 3 were waited for; matrix products, arithmetic and copies ran while one was open for 27% of the time, Pallas kernels for 0%

commit v1 on v0

v1 whole, which is shorter than its diff:
```python
import functools

import jax
import jax.numpy as jnp
from jax import lax
from jax.experimental import pallas as pl
from jax.experimental.pallas import tpu as pltpu
from jax.sharding import PartitionSpec as P

BLOCK = 128
ADAPTER_RANK = 16
STRIP = 64
VMEM_LIMIT = 48 * 1024 * 1024
F32 = jnp.float32
BF16 = jnp.bfloat16


def dequant_rows(piece, scales):
    count = piece.shape[0]
    block_of = lax.iota(jnp.int32, count) // BLOCK
    select = (block_of[:, None] == lax.iota(jnp.int32, scales.shape[0])[None, :]).astype(F32)
    row_scales = jnp.dot(select, scales, precision=lax.Precision.HIGHEST)
    expanded = jnp.repeat(row_scales, BLOCK, axis=1)
    return (piece.astype(F32) * expanded).astype(BF16)


def reduce_over_rows(left, right):
    return lax.dot_general(left, right, (((1,), (1,)), ((), ())), preferred_element_type=F32)


def contract_tokens(left, right):
    return lax.dot_general(left, right, (((0,), (0,)), ((), ())), preferred_element_type=F32)


def plain_path(tokens, token_adapter_index, frozen, scales, down, up, cotangent):
    rank_adapter = lax.iota(jnp.int32, down.shape[1]) // ADAPTER_RANK
    mask = (token_adapter_index[:, None] == rank_adapter[None, :]).astype(F32)
    shrink = (jnp.dot(tokens, down, preferred_element_type=F32) * mask).astype(BF16)
    spread = (2.0 * reduce_over_rows(cotangent, up) * mask).astype(BF16)
    weight = dequant_rows(lax.all_gather(frozen, "seq", axis=0, tiled=True), scales)
    values = jnp.dot(tokens, weight, preferred_element_type=F32)
    values = (values + 2.0 * jnp.dot(shrink, up, preferred_element_type=F32)).astype(BF16)
    act = reduce_over_rows(cotangent, weight) + reduce_over_rows(spread, down)
    grad_a = lax.psum_scatter(
        contract_tokens(tokens, spread), "seq", scatter_dimension=0, tiled=True
    )
    grad_b = lax.psum(2.0 * contract_tokens(shrink, cotangent), "seq")
    return values, act.astype(BF16), grad_a, grad_b


def call(body, name, grid, in_specs, out_specs, out_shape, scratch=(), alias=None, cost=None):
    return pl.pallas_call(
        body,
        name=name,
        grid_spec=pltpu.PrefetchScalarGridSpec(
            num_scalar_prefetch=1,
            grid=grid,
            in_specs=in_specs,
            out_specs=out_specs,
            scratch_shapes=scratch,
        ),
        out_shape=out_shape,
        input_output_aliases=alias or {},
        compiler_params=pltpu.CompilerParams(vmem_limit_bytes=VMEM_LIMIT),
        cost_estimate=cost,
    )


def whole(shape):
    return pl.BlockSpec(shape, lambda *_: (0,) * len(shape))


def struct(shape, dtype):
    return jax.ShapeDtypeStruct(shape, dtype)


def dequant_body(info, w, scales, shared, rest):
    z, y, c, x = info[0], info[1], info[2], info[3]
    strips = w.shape[0] // STRIP
    first = ((z * 2 + y) * 2 + c) * strips
    kept = rest.shape[0] // STRIP
    middle = strips - 2 * kept

    def scale_strip(out, at, source):
        block_row = lax.div((first + source) * STRIP, BLOCK)
        rows = pl.ds(pl.multiple_of(source * STRIP, STRIP), STRIP)
        for b in range(w.shape[1] // BLOCK):
            columns = pl.ds(b * BLOCK, BLOCK)
            value = w[rows, columns].astype(F32) * scales[block_row, b]
            out[pl.ds(at * STRIP, STRIP), columns] = value.astype(BF16)

    for i in range(kept):
        scale_strip(shared, i, x * (kept + middle) + i)
        scale_strip(rest, i, (1 - x) * (kept + middle) + i)
    for i in range(middle):
        scale_strip(shared, kept + i, kept + i)


def grads_body(steps, rows, info, tok, idx, down, up, cot, shrink, spread, send, keep, acc):
    j = pl.program_id(0)
    c = info[2]
    ranks = up.shape[0]
    rank_adapter = lax.broadcasted_iota(jnp.int32, (1, ranks), 1) // ADAPTER_RANK
    mask = (idx[...] == rank_adapter).astype(F32)

    @pl.when(j == 0)
    def _():
        spread[...] = (2.0 * reduce_over_rows(cot[...], up[...]) * mask).astype(BF16)
        acc[...] = jnp.zeros_like(acc)

    acc[...] += jnp.dot(tok[...], down[...], preferred_element_type=F32)
    part = contract_tokens(tok[...], spread[...])

    def place(own, other):
        for y in range(2):
            for core in range(2):
                at = (y * 2 + core) * rows
                out = (own, other)[core]
                out[j, y, pl.ds(0, rows), :] = part[at : at + rows]

    @pl.when(c == 0)
    def _():
        place(keep, send)

    @pl.when(c == 1)
    def _():
        place(send, keep)

    @pl.when(j == steps - 1)
    def _():
        shrink[...] = (acc[...] * mask).astype(BF16)
        grad_b = contract_tokens(shrink[...], cot[...])
        half = ranks // 2

        def place_b(own, other):
            for zz in range(steps):
                for y in range(2):
                    for core in range(2):
                        column = (zz * 2 + y) * ranks
                        piece = grad_b[core * half : (core + 1) * half, column : column + ranks]
                        (own, other)[core][zz, y, pl.ds(rows, half), :] = piece

        @pl.when(c == 0)
        def _():
            place_b(keep, send)

        @pl.when(c == 1)
        def _():
            place_b(send, keep)


def pair_body(info, keep, got, own, s1, s2, s3):
    j = pl.program_id(0)
    total = keep[0] + got[0]

    @pl.when(j == 0)
    def _():
        own[...] = total

    for step, out in ((1, s1), (2, s2), (3, s3)):

        @pl.when(j == step)
        def _(out=out):
            out[...] = total.astype(BF16)


def line_body(info, own, r1, r2, r3, mine, other):
    y = info[1]

    def total(at):
        return (
            own[at] + r1[at].astype(F32) + r2[at].astype(F32) + r3[at].astype(F32)
        )

    mine[...] = total(y)
    other[...] = total(1 - y).astype(BF16)


def last_body(info, mine, got, grad_a, piece_b):
    rows = grad_a.shape[0]
    total = mine[...] + got[...].astype(F32)
    grad_a[...] = total[:rows]
    piece_b[...] = 2.0 * total[rows:]


def place_b_body(info, own, other, out):
    z, y, c = info[0], info[1], info[2]
    half, ranks = own.shape[2:]
    for from_core, ref in ((c, own), (1 - c, other)):
        for i in range(2):
            yy = y if i == 0 else 1 - y
            for k in range(own.shape[1]):
                zz = lax.rem(z + 4 - k, 4)
                column = pl.multiple_of((zz * 2 + yy) * ranks, ranks)
                row = pl.multiple_of(from_core * half, half)
                out[pl.ds(row, half), pl.ds(column, ranks)] = ref[i, k]


def plane_body(first, last, rows, info, tok, cot, spread, down, *refs):
    pieces, refs = refs[:8], refs[8:]
    if first:
        shrink, up, act, acc, weight = refs
    else:
        total, _, act, acc, weight = refs
    y, c, x = info[1], info[2], info[3]
    for i, yy in enumerate((y, 1 - y)):
        for h, cc in enumerate((c, 1 - c)):
            shared, rest = pieces[h * 4 + i * 2], pieces[h * 4 + i * 2 + 1]
            base = (yy * 2 + cc) * rows
            kept = rest.shape[0]
            middle = shared.shape[0] - kept
            at = pl.multiple_of(base + x * (kept + middle), STRIP)
            weight[pl.ds(at, kept), :] = shared[:kept]
            at = pl.multiple_of(base + kept, STRIP)
            weight[pl.ds(at, middle), :] = shared[kept:]
            at = pl.multiple_of(base + (1 - x) * (kept + middle), STRIP)
            weight[pl.ds(at, kept), :] = rest[...]
    forward = jnp.dot(tok[...], weight[...], preferred_element_type=F32)
    if first:
        forward += 2.0 * jnp.dot(shrink[...], up[...], preferred_element_type=F32)
    else:
        forward += total[...]
    acc[...] = forward.astype(acc.dtype)
    back = reduce_over_rows(cot[...], weight[...]) + reduce_over_rows(spread[...], down[...])
    act[...] = back.astype(BF16)


def swap(n, move):
    pairs = []
    for s in range(n):
        z, y, c = move(s // 4, s // 2 % 2, s % 2)
        pairs.append((s, (z % (n // 4) * 2 + y) * 2 + c))
    return pairs


def block_path(tokens, token_adapter_index, frozen, scales, down, up, cotangent):
    n, planes = 16, 4
    count, width = tokens.shape
    rows, columns = frozen.shape
    ranks = up.shape[0]
    depth = width // planes
    kept = rows * 2 // 5 // STRIP * STRIP
    shared_rows = rows - kept
    half = ranks // 2
    piece_rows = rows + half

    s = lax.axis_index("seq").astype(jnp.int32)
    x = lax.axis_index("groups").astype(jnp.int32)
    info = jnp.stack([s // 4, s // 2 % 2, s % 2, x])

    def over_z(v, by=1):
        return lax.ppermute(v, "seq", swap(n, lambda z, y, c: (z + by, y, c)))

    def over_y(v):
        return lax.ppermute(v, "seq", swap(n, lambda z, y, c: (z, 1 - y, c)))

    def over_core(v):
        return lax.ppermute(v, "seq", swap(n, lambda z, y, c: (z, y, 1 - c)))

    def over_x(v):
        return lax.ppermute(v, "groups", [(0, 1), (1, 0)])

    shared, rest = call(
        dequant_body,
        "scale_rows",
        (1,),
        [whole((rows, columns)), pl.BlockSpec(memory_space=pltpu.SMEM)],
        [whole((shared_rows, columns)), whole((kept, columns))],
        [struct((shared_rows, columns), BF16), struct((kept, columns), BF16)],
    )(info, frozen, scales)

    near = [shared]
    for _ in range(1, planes):
        near.append(over_z(near[-1]))
    far = [over_y(v) for v in near]
    near_rest = [rest] + [over_x(v[:kept]) for v in near[1:]]
    far_rest = [over_x(v[:kept]) for v in far]

    piece = (planes, 2, piece_rows, ranks)
    shrink, spread, send, keep = call(
        functools.partial(grads_body, planes, rows),
        "gradient_shares",
        (planes,),
        [
            pl.BlockSpec((count, depth), lambda j, _: (0, j)),
            whole((count, 1)),
            pl.BlockSpec((depth, ranks), lambda j, _: (j, 0)),
            whole((ranks, columns)),
            whole((count, columns)),
        ],
        [whole((count, ranks)), whole((count, ranks)), whole(piece), whole(piece)],
        [
            struct((count, ranks), BF16),
            struct((count, ranks), BF16),
            struct(piece, F32),
            struct(piece, F32),
        ],
        scratch=[pltpu.VMEM((count, ranks), F32)],
    )(info, tokens, token_adapter_index[:, None], down, up, cotangent)

    pair = (2, piece_rows, ranks)
    block = pl.BlockSpec((1,) + pair, lambda j, info: (lax.rem(info[0] + j, 4), 0, 0, 0))
    own, s1, s2, s3 = call(
        pair_body,
        "add_core",
        (planes,),
        [block, block],
        [whole(pair)] * 4,
        [struct(pair, F32)] + [struct(pair, BF16)] * 3,
    )(info, keep, over_core(send))
    mine, other = call(
        line_body,
        "add_line",
        (1,),
        [whole(pair)] * 4,
        [whole(pair[1:])] * 2,
        [struct(pair[1:], F32), struct(pair[1:], BF16)],
    )(info, own, over_z(s1, 1), over_z(s2, 2), over_z(s3, 3))
    grad_a, piece_b = call(
        last_body,
        "add_side",
        (1,),
        [whole(pair[1:])] * 2,
        [whole((rows, ranks)), whole((half, ranks))],
        [struct((rows, ranks), F32), struct((half, ranks), F32)],
    )(info, mine, over_y(other))
    line_b = jnp.stack([piece_b] + [over_z(piece_b, k) for k in range(1, planes)])
    side_b = jnp.stack([line_b, over_y(line_b)])
    grad_b = call(
        place_b_body,
        "place_up_gradient",
        (1,),
        [whole(side_b.shape)] * 2,
        whole((ranks, columns)),
        struct((ranks, columns), F32),
    )(info, side_b, over_core(side_b))

    act = total = None
    for k in range(planes):
        mine_k = [near[k], near_rest[k], far[k], far_rest[k]]
        pieces = mine_k + [over_core(v) for v in mine_k]
        first, last = k == 0, k == planes - 1
        at = functools.partial(lambda k, j, info: lax.rem(info[0] + 4 - k, 4), k)
        in_specs = [
            pl.BlockSpec((count, depth), lambda j, info, at=at: (0, at(j, info))),
            whole((count, columns)),
            whole((count, ranks)),
            pl.BlockSpec((depth, ranks), lambda j, info, at=at: (at(j, info), 0)),
        ] + [whole(v.shape) for v in pieces]
        operands = [tokens, cotangent, spread, down] + pieces
        if first:
            in_specs += [whole((count, ranks)), whole((ranks, columns))]
            operands += [shrink, up]
            alias = None
        else:
            in_specs += [whole((count, columns)), pl.BlockSpec(memory_space=pl.ANY)]
            operands += [total, act]
            alias = {len(operands): 0}
        act, total = call(
            functools.partial(plane_body, first, last, rows),
            f"plane_{k}",
            (1,),
            in_specs,
            [in_specs[0], whole((count, columns))],
            [struct((count, width), BF16), struct((count, columns), BF16 if last else F32)],
            scratch=[pltpu.VMEM((depth, columns), BF16)],
            alias=alias,
            cost=pl.CostEstimate(
                flops=4 * count * depth * columns,
                bytes_accessed=8 * 1024 * 1024,
                transcendentals=0,
            ),
        )(info, *operands)
    return total, act, grad_a, grad_b


def solution(mesh):
    sizes = (mesh.shape["groups"], mesh.shape["seq"])

    def on_device(*operands):
        rows, columns = operands[2].shape
        ranks = operands[5].shape[0]
        fits = rows % STRIP == 0 and rows >= 5 * STRIP and columns == 8 * ranks
        path = block_path if sizes == (2, 16) and fits and ranks == BLOCK else plain_path
        return path(*operands)

    return jax.shard_map(
        on_device,
        mesh=mesh,
        in_specs=(
            P(("groups", "seq"), None),
            P(("groups", "seq")),
            P("seq", None),
            P(),
            P("groups", None),
            P("groups", None),
            P(("groups", "seq"), None),
        ),
        out_specs=(
            P(("groups", "seq"), None),
            P(("groups", "seq"), None),
            P(("groups", "seq"), None),
            P("groups", None),
        ),
        check_vma=False,
    )
```

time: 271 us -> 130 us (0.48)
  waiting for transfers between devices: 180 us -> 53.6 us
  matrix products: 50.2 us -> 0 us
  Pallas kernels: 0 us -> 36.2 us
  starting transfers between devices: 0.12 us -> 32.8 us
  local copies, waits for them, and re-layouts: 25.9 us -> 5.5 us
  between operations: 13.9 us -> 0.93 us
    all_gather x1 -> x0, waiting for transfers between devices: 76.2 us -> none  [on_device(): gathered = lax.all_gather(frozen_value_weight, 'seq', axis=0, tiled=True)]
    unnamed x4 -> x0, waiting for transfers between devices: 69.4 us -> none
    ppermute x0 -> x40, waiting for transfers between devices: none -> 53.6 us  [the longest x9 26.1 us: over_z(): return lax.ppermute(v, 'seq', swap(n, lambda z, y, c: (z + by, y, c)))]
    dot_general x9 -> x0, matrix products: 50.2 us -> none  [the longest x1 20 us: on_device(): forward_pass = jnp.dot(tokens, weight, preferred_element_type=jnp.float32)]
    pallas_call x0 -> x10, Pallas kernels: none -> 36.2 us  [the longest x4 23 us: block_path(): call(functools.partial(plane_body, first, last, rows), f'plane_{k}', (1,)...]
    psum x1 -> x0, waiting for transfers between devices: 34.6 us -> none  [on_device(): grad_b = lax.psum(2.0 * contract_tokens(down_projected, cotangent), 'seq')]
    ppermute x0 -> x40, starting transfers between devices: none -> 32.8 us  [the longest x9 12.2 us: over_z(): return lax.ppermute(v, 'seq', swap(n, lambda z, y, c: (z + by, y, c)))]
    broadcast_in_dim x1, local copies, waits for them, and re-layouts: 11.5 us -> 0.79 us  [block_path(): token_adapter_index[:, None]]
  transfers between devices with their start and end apart: 3 -> 40, of which waited for: 3 -> 11; matrix products, arithmetic and copies ran while one was open for 27% -> 0% of each run, Pallas kernels for 0% -> 21%
where the time goes in v1:
time: 130 us; the launch traced here: 129 us
  waiting for transfers between devices  53.6 us (41%)
  Pallas kernels  36.2 us (28%)
  starting transfers between devices  32.8 us (25%)
  local copies, waits for them, and re-layouts  5.5 us (4%)
    ppermute x9, waiting for transfers between devices, over_z(): return lax.ppermute(v, 'seq', swap(n, lambda z, y, c: (z + by, y, c)))  26.1 us
    pallas_call x4, Pallas kernels, block_path(): call(functools.partial(plane_body, first, last, rows), f'plane_{k}', (1,)...  23 us
    ppermute x6, waiting for transfers between devices, over_y(): return lax.ppermute(v, 'seq', swap(n, lambda z, y, c: (z, 1 - y, c)))  19 us
    ppermute x9, starting transfers between devices, over_z(): return lax.ppermute(v, 'seq', swap(n, lambda z, y, c: (z + by, y, c)))  12.2 us
    ppermute x7, starting transfers between devices, over_x(): return lax.ppermute(v, 'groups', [(0, 1), (1, 0)])  9.61 us
    ppermute x7, waiting for transfers between devices, over_x(): return lax.ppermute(v, 'groups', [(0, 1), (1, 0)])  8.4 us
    ppermute x6, starting transfers between devices, over_y(): return lax.ppermute(v, 'seq', swap(n, lambda z, y, c: (z, 1 - y, c)))  8.27 us
    pallas_call x1, Pallas kernels, block_path(): call(functools.partial(grads_body, planes, rows), 'gradient_shares', (pla...  7.45 us
  transfers between devices with their start and end apart: 40, of which 11 were waited for; matrix products, arithmetic and copies ran while one was open for 0% of the time, Pallas kernels for 21%

profile of v1, /device:TPU:0, one launch (start us, length us, event | category | flops | bytes accessed | tf_op | source)
XLA Modules:
  0.0 129.1 jit_solution(9696914005233131350)
XLA Ops:
  5.0 7.4 %gradient_shares.1 = (bf16[384,128]{1,0:T(8,128)(2,1)S(1)}, bf16[384,128]{1,0:T(8,128)(2,1)S(1)}, f32[4,2,384,128]{3,2,1,0:T(8,128)}, f32[4,2,384,128]{3,2,1,0:T(8,128)S(1)}) custom-call(s32[4]{0:T(128)S(1)} %pad_add_fusion.info, bf16[384,5120]{1,0:T(8,128)(2,1)} %tok.9, s32[384,1]{1,0:T(8,128)S(1)} %broadcast_in_dim.4.idx, bf16[5120,128]{1,0:T(8,128)(2,1)S(1)} %copy-done, ...), custom_call_target="tpu_custom_call" | custom-call | tf_op jit(solution)/shard_map/gradient_shares/pallas_call | solution.py:280
  14.1 1.6 %scale_rows.1 = (bf16[192,1024]{1,0:T(8,128)(2,1)S(1)}, bf16[128,1024]{1,0:T(8,128)(2,1)S(1)}) custom-call(s32[4]{0:T(128)S(1)} %pad_add_fusion.info, bf16[320,1024]{1,0:T(8,128)(2,1)S(1)} %copy-done.6, f32[40,8]{1,0:T(8,128)S(1)} %copy.16.scales), custom_call_target="tpu_custom_call" | custom-call | tf_op jit(solution)/shard_map/scale_rows/pallas_call | solution.py:263
  15.6 2.6 %collective-permute-start.24 = (bf16[192,1024]{1,0:T(8,128)(2,1)S(1)}, bf16[192,1024]{1,0:T(8,128)(2,1)S(1)}, u32[]{:S(2)}, u32[]{:S(2)}) collective-permute-start(bf16[192,1024]{1,0:T(8,128)(2,1)S(1)} %get-tuple-element.27.refs_0_), channel_id=1, source_target_pairs={{0,2},{1,3},{2,0},{3,1},{4,6},{5,7},{6,4},{7,5},{8,10},{9,11},{10,... | collective-permute-start | bytes 1179656 | tf_op jit(solution)/shard_map/ppermute | solution.py:255
  18.2 1.6 %collective-permute-start = (bf16[192,1024]{1,0:T(8,128)(2,1)S(1)}, bf16[192,1024]{1,0:T(8,128)(2,1)S(1)}, u32[]{:S(2)}, u32[]{:S(2)}) collective-permute-start(bf16[192,1024]{1,0:T(8,128)(2,1)S(1)} %get-tuple-element.27.refs_0_), channel_id=1, source_target_pairs={{0,4},{1,5},{2,6},{3,7},{4,8},{5,9},{6,10},{7,11},{8,12},{9,13},{1... | collective-permute-start | bytes 1179656 | tf_op jit(solution)/shard_map/ppermute | solution.py:252
  20.3 7.7 %collective-permute-done.24.refs_2_ = bf16[192,1024]{1,0:T(8,128)(2,1)S(1)} collective-permute-done((bf16[192,1024]{1,0:T(8,128)(2,1)S(1)}, bf16[192,1024]{1,0:T(8,128)(2,1)S(1)}, u32[]{:S(2)}, u32[]{:S(2)}) %collective-permute-start.24) | collective-permute-done | bytes 393248 | tf_op jit(solution)/shard_map/ppermute | solution.py:255
  28.0 1.8 %collective-permute-start.25 = (bf16[128,1024]{1,0:T(8,128)(2,1)S(1)}, bf16[128,1024]{1,0:T(8,128)(2,1)S(1)}, u32[]{:S(2)}, u32[]{:S(2)}) collective-permute-start(bf16[128,1024]{1,0:T(8,128)(2,1)S(1)} %slice.34), channel_id=1, source_target_pairs={{0,16},{16,0},{1,17},{17,1},{2,18},{18,2},{3,19},{19,3},{4,20},{20... | collective-permute-start | bytes 786440 | tf_op jit(solution)/shard_map/ppermute | solution.py:261
  31.3 1.6 %collective-permute-start.17 = (bf16[128,1024]{1,0:T(8,128)(2,1)S(1)}, bf16[128,1024]{1,0:T(8,128)(2,1)S(1)}, u32[]{:S(2)}, u32[]{:S(2)}) collective-permute-start(bf16[128,1024]{1,0:T(8,128)(2,1)S(1)} %slice.32), channel_id=1, source_target_pairs={{0,16},{16,0},{1,17},{17,1},{2,18},{18,2},{3,19},{19,3},{4,20},{20... | collective-permute-start | bytes 786440 | tf_op jit(solution)/shard_map/ppermute | solution.py:261
  33.4 3.8 %collective-permute-done.25.refs_3_ = bf16[128,1024]{1,0:T(8,128)(2,1)S(1)} collective-permute-done((bf16[128,1024]{1,0:T(8,128)(2,1)S(1)}, bf16[128,1024]{1,0:T(8,128)(2,1)S(1)}, u32[]{:S(2)}, u32[]{:S(2)}) %collective-permute-start.25) | collective-permute-done | bytes 262176 | tf_op jit(solution)/shard_map/ppermute | solution.py:261
  37.3 4.6 %collective-permute-done.17.refs_1_ = bf16[128,1024]{1,0:T(8,128)(2,1)S(1)} collective-permute-done((bf16[128,1024]{1,0:T(8,128)(2,1)S(1)}, bf16[128,1024]{1,0:T(8,128)(2,1)S(1)}, u32[]{:S(2)}, u32[]{:S(2)}) %collective-permute-start.17) | collective-permute-done | bytes 262176 | tf_op jit(solution)/shard_map/ppermute | solution.py:261
  41.8 1.6 %collective-permute-start.1 = (bf16[192,1024]{1,0:T(8,128)(2,1)S(1)}, bf16[192,1024]{1,0:T(8,128)(2,1)S(1)}, u32[]{:S(2)}, u32[]{:S(2)}) collective-permute-start(bf16[192,1024]{1,0:T(8,128)(2,1)S(1)} %collective-permute-done.refs_0_), channel_id=1, source_target_pairs={{0,4},{1,5},{2,6},{3,7},{4,8},{5,9},{6,10},{7,11},{8,12},{9,13},{1... | collective-permute-start | bytes 1179656 | tf_op jit(solution)/shard_map/ppermute | solution.py:252
  45.5 8.2 %collective-permute-done.1.refs_0_ = bf16[192,1024]{1,0:T(8,128)(2,1)S(1)} collective-permute-done((bf16[192,1024]{1,0:T(8,128)(2,1)S(1)}, bf16[192,1024]{1,0:T(8,128)(2,1)S(1)}, u32[]{:S(2)}, u32[]{:S(2)}) %collective-permute-start.1) | collective-permute-done | bytes 393248 | tf_op jit(solution)/shard_map/ppermute | solution.py:252
  57.4 3.1 %collective-permute-start.32 = (bf16[2,384,128]{2,1,0:T(8,128)(2,1)S(1)}, bf16[2,384,128]{2,1,0:T(8,128)(2,1)S(1)}, u32[]{:S(2)}, u32[]{:S(2)}) collective-permute-start(bf16[2,384,128]{2,1,0:T(8,128)(2,1)S(1)} %get-tuple-element.42), channel_id=1, source_target_pairs={{0,8},{1,9},{2,10},{3,11},{4,12},{5,13},{6,14},{7,15},{8,0},{9,1},... | collective-permute-start | bytes 589832 | tf_op jit(solution)/shard_map/ppermute | solution.py:252
  62.0 2.0 %collective-permute-start.33 = (bf16[2,384,128]{2,1,0:T(8,128)(2,1)S(1)}, bf16[2,384,128]{2,1,0:T(8,128)(2,1)S(1)}, u32[]{:S(2)}, u32[]{:S(2)}) collective-permute-start(bf16[2,384,128]{2,1,0:T(8,128)(2,1)S(1)} %get-tuple-element.43), channel_id=1, source_target_pairs={{0,12},{1,13},{2,14},{3,15},{4,0},{5,1},{6,2},{7,3},{8,4},{9,5},{1... | collective-permute-start | bytes 589832 | tf_op jit(solution)/shard_map/ppermute | solution.py:252
  64.0 3.7 %collective-permute-done.2.refs_0_ = bf16[192,1024]{1,0:T(8,128)(2,1)S(1)} collective-permute-done((bf16[192,1024]{1,0:T(8,128)(2,1)S(1)}, bf16[192,1024]{1,0:T(8,128)(2,1)S(1)}, u32[]{:S(2)}, u32[]{:S(2)}) %collective-permute-start.2) | collective-permute-done | bytes 393248 | tf_op jit(solution)/shard_map/ppermute | solution.py:252
  67.7 4.2 %collective-permute-done.31.r1 = bf16[2,384,128]{2,1,0:T(8,128)(2,1)S(1)} collective-permute-done((bf16[2,384,128]{2,1,0:T(8,128)(2,1)S(1)}, bf16[2,384,128]{2,1,0:T(8,128)(2,1)S(1)}, u32[]{:S(2)}, u32[]{:S(2)}) %collective-permute-start.31) | collective-permute-done | bytes 196640 | tf_op jit(solution)/shard_map/ppermute | solution.py:252
  71.9 5.5 %collective-permute-done.32.r2 = bf16[2,384,128]{2,1,0:T(8,128)(2,1)S(1)} collective-permute-done((bf16[2,384,128]{2,1,0:T(8,128)(2,1)S(1)}, bf16[2,384,128]{2,1,0:T(8,128)(2,1)S(1)}, u32[]{:S(2)}, u32[]{:S(2)}) %collective-permute-start.32) | collective-permute-done | bytes 196640 | tf_op jit(solution)/shard_map/ppermute | solution.py:252
  80.2 10.3 %collective-permute-done.34.got = bf16[384,128]{1,0:T(8,128)(2,1)S(1)} collective-permute-done((bf16[384,128]{1,0:T(8,128)(2,1)S(1)}, bf16[384,128]{1,0:T(8,128)(2,1)S(1)}, u32[]{:S(2)}, u32[]{:S(2)}) %collective-permute-start.34) | collective-permute-done | bytes 98336 | tf_op jit(solution)/shard_map/ppermute | solution.py:255
  94.7 2.9 %collective-permute-done.35 = f32[64,128]{1,0:T(8,128)S(1)} collective-permute-done((f32[64,128]{1,0:T(8,128)S(1)}, f32[64,128]{1,0:T(8,128)S(1)}, u32[]{:S(2)}, u32[]{:S(2)}) %collective-permute-start.35) | collective-permute-done | bytes 32800 | tf_op jit(solution)/shard_map/ppermute | solution.py:252
  98.8 1.6 %collective-permute-start.37 = (f32[64,128]{1,0:T(8,128)S(1)}, f32[64,128]{1,0:T(8,128)S(1)}, u32[]{:S(2)}, u32[]{:S(2)}) collective-permute-start(f32[64,128]{1,0:T(8,128)S(1)} %get-tuple-element.47), channel_id=1, source_target_pairs={{0,12},{1,13},{2,14},{3,15},{4,0},{5,1},{6,2},{7,3},{8,4},{9,5},{1... | collective-permute-start | bytes 98312 | tf_op jit(solution)/shard_map/ppermute | solution.py:252
  100.4 5.5 %plane_0.1 = (bf16[384,5120]{1,0:T(8,128)(2,1)}, f32[384,1024]{1,0:T(8,128)}) custom-call(s32[4]{0:T(128)S(1)} %pad_add_fusion.info, bf16[384,5120]{1,0:T(8,128)(2,1)} %tok.9, bf16[384,1024]{1,0:T(8,128)(2,1)S(1)} %copy-done.3, bf16[384,128]{1,0:T(8,128)(2,1)S(1)} %get-tuple-element.26.spread, bf16[5120,128]{1,0:T(8,128)(2,1)S(1)} %copy-done.1, ...), custom_call_target="tpu_custom_call" | custom-call | flops 2013265920 | bytes 8388608 | tf_op jit(solution)/shard_map/plane_0/pallas_call | solution.py:359
  107.8 1.5 %collective-permute-start.38 = (f32[4,64,128]{2,1,0:T(8,128)S(1)}, f32[4,64,128]{2,1,0:T(8,128)S(1)}, u32[]{:S(2)}, u32[]{:S(2)}) collective-permute-start(f32[4,64,128]{2,1,0:T(8,128)S(1)} %get-tuple-element.49), channel_id=1, source_target_pairs={{0,2},{1,3},{2,0},{3,1},{4,6},{5,7},{6,4},{7,5},{8,10},{9,11},{10,... | collective-permute-start | bytes 393224 | tf_op jit(solution)/shard_map/ppermute | solution.py:255
  109.4 5.8 %plane_1.1 = (bf16[384,5120]{1,0:T(8,128)(2,1)}, f32[384,1024]{1,0:T(8,128)}) custom-call(s32[4]{0:T(128)S(1)} %pad_add_fusion.info, bf16[384,5120]{1,0:T(8,128)(2,1)} %tok.9, bf16[384,1024]{1,0:T(8,128)(2,1)S(1)} %copy-done.3, bf16[384,128]{1,0:T(8,128)(2,1)S(1)} %get-tuple-element.26.spread, ...), custom_call_target="tpu_custom_call", output_to_operand_aliasing={{0}: (14, {})} | custom-call | flops 2013265920 | bytes 8388608 | tf_op jit(solution)/shard_map/plane_1/pallas_call | solution.py:359
  116.0 5.8 %plane_2.1 = (bf16[384,5120]{1,0:T(8,128)(2,1)}, f32[384,1024]{1,0:T(8,128)}) custom-call(s32[4]{0:T(128)S(1)} %pad_add_fusion.info, bf16[384,5120]{1,0:T(8,128)(2,1)} %tok.9, bf16[384,1024]{1,0:T(8,128)(2,1)S(1)} %copy-done.3, bf16[384,128]{1,0:T(8,128)(2,1)S(1)} %get-tuple-element.26.spread, ...), custom_call_target="tpu_custom_call", output_to_operand_aliasing={{0}: (14, {})} | custom-call | flops 2013265920 | bytes 8388608 | tf_op jit(solution)/shard_map/plane_2/pallas_call | solution.py:359
  121.9 5.8 %plane_3.1 = (bf16[384,5120]{1,0:T(8,128)(2,1)}, bf16[384,1024]{1,0:T(8,128)(2,1)}) custom-call(s32[4]{0:T(128)S(1)} %pad_add_fusion.info, bf16[384,5120]{1,0:T(8,128)(2,1)} %tok.9, bf16[384,1024]{1,0:T(8,128)(2,1)S(1)} %copy-done.3, bf16[384,128]{1,0:T(8,128)(2,1)S(1)} %get-tuple-element.26.spread, ...), custom_call_target="tpu_custom_call", output_to_operand_aliasing={{0}: (14, {})} | custom-call | flops 2013265920 | bytes 8388608 | tf_op jit(solution)/shard_map/plane_3/pallas_call | solution.py:359
  (94 shorter events, 28.0 us)
Async XLA Ops:
  12.4 41.3 %collective-permute-start.30 = (f32[4,2,384,128]{3,2,1,0:T(8,128)}, f32[4,2,384,128]{3,2,1,0:T(8,128)S(1)}, u32[]{:S(2)}, u32[]{:S(2)}) collective-permute-start(f32[4,2,384,128]{3,2,1,0:T(8,128)} %get-tuple-element.39), channel_id=1, source_target_pairs={{0,1},{1,0},{2,3},{3,2},{4,5},{5,4},{6,7},{7,6},{8,9},{9,8},{10,11... | collective-permute-start | bytes 4718600 | tf_op jit(solution)/shard_map/ppermute | solution.py:258
  15.6 12.3 %collective-permute-start.24 = (bf16[192,1024]{1,0:T(8,128)(2,1)S(1)}, bf16[192,1024]{1,0:T(8,128)(2,1)S(1)}, u32[]{:S(2)}, u32[]{:S(2)}) collective-permute-start(bf16[192,1024]{1,0:T(8,128)(2,1)S(1)} %get-tuple-element.27.refs_0_), channel_id=1, source_target_pairs={{0,2},{1,3},{2,0},{3,1},{4,6},{5,7},{6,4},{7,5},{8,10},{9,11},{10,... | collective-permute-start | bytes 1179656 | tf_op jit(solution)/shard_map/ppermute | solution.py:255
  18.2 13.1 %collective-permute-start = (bf16[192,1024]{1,0:T(8,128)(2,1)S(1)}, bf16[192,1024]{1,0:T(8,128)(2,1)S(1)}, u32[]{:S(2)}, u32[]{:S(2)}) collective-permute-start(bf16[192,1024]{1,0:T(8,128)(2,1)S(1)} %get-tuple-element.27.refs_0_), channel_id=1, source_target_pairs={{0,4},{1,5},{2,6},{3,7},{4,8},{5,9},{6,10},{7,11},{8,12},{9,13},{1... | collective-permute-start | bytes 1179656 | tf_op jit(solution)/shard_map/ppermute | solution.py:252
  19.7 13.1 %collective-permute-start.26 = (bf16[192,1024]{1,0:T(8,128)(2,1)S(1)}, bf16[192,1024]{1,0:T(8,128)(2,1)S(1)}, u32[]{:S(2)}, u32[]{:S(2)}) collective-permute-start(bf16[192,1024]{1,0:T(8,128)(2,1)S(1)} %get-tuple-element.27.refs_0_), channel_id=1, source_target_pairs={{0,1},{1,0},{2,3},{3,2},{4,5},{5,4},{6,7},{7,6},{8,9},{9,8},{10,11... | collective-permute-start | bytes 1179656 | tf_op jit(solution)/shard_map/ppermute | solution.py:258
  19.7 13.1 %collective-permute-start.27 = (bf16[128,1024]{1,0:T(8,128)(2,1)S(1)}, bf16[128,1024]{1,0:T(8,128)(2,1)S(1)}, u32[]{:S(2)}, u32[]{:S(2)}) collective-permute-start(bf16[128,1024]{1,0:T(8,128)(2,1)S(1)} %get-tuple-element.28.refs_1_), channel_id=1, source_target_pairs={{0,1},{1,0},{2,3},{3,2},{4,5},{5,4},{6,7},{7,6},{8,9},{9,8},{10,11... | collective-permute-start | bytes 786440 | tf_op jit(solution)/shard_map/ppermute | solution.py:258
  41.8 11.9 %collective-permute-start.1 = (bf16[192,1024]{1,0:T(8,128)(2,1)S(1)}, bf16[192,1024]{1,0:T(8,128)(2,1)S(1)}, u32[]{:S(2)}, u32[]{:S(2)}) collective-permute-start(bf16[192,1024]{1,0:T(8,128)(2,1)S(1)} %collective-permute-done.refs_0_), channel_id=1, source_target_pairs={{0,4},{1,5},{2,6},{3,7},{4,8},{5,9},{6,10},{7,11},{8,12},{9,13},{1... | collective-permute-start | bytes 1179656 | tf_op jit(solution)/shard_map/ppermute | solution.py:252
  43.4 12.7 %collective-permute-start.29 = (bf16[128,1024]{1,0:T(8,128)(2,1)S(1)}, bf16[128,1024]{1,0:T(8,128)(2,1)S(1)}, u32[]{:S(2)}, u32[]{:S(2)}) collective-permute-start(bf16[128,1024]{1,0:T(8,128)(2,1)S(1)} %collective-permute-done.25.refs_3_), channel_id=1, source_target_pairs={{0,1},{1,0},{2,3},{3,2},{4,5},{5,4},{6,7},{7,6},{8,9},{9,8},{10,11... | collective-permute-start | bytes 786440 | tf_op jit(solution)/shard_map/ppermute | solution.py:258
  44.4 13.0 %collective-permute-start.21 = (bf16[128,1024]{1,0:T(8,128)(2,1)S(1)}, bf16[128,1024]{1,0:T(8,128)(2,1)S(1)}, u32[]{:S(2)}, u32[]{:S(2)}) collective-permute-start(bf16[128,1024]{1,0:T(8,128)(2,1)S(1)} %collective-permute-done.17.refs_1_), channel_id=1, source_target_pairs={{0,1},{1,0},{2,3},{3,2},{4,5},{5,4},{6,7},{7,6},{8,9},{9,8},{10,11... | collective-permute-start | bytes 786440 | tf_op jit(solution)/shard_map/ppermute | solution.py:258
  44.4 16.1 %collective-permute-start.19 = (bf16[128,1024]{1,0:T(8,128)(2,1)S(1)}, bf16[128,1024]{1,0:T(8,128)(2,1)S(1)}, u32[]{:S(2)}, u32[]{:S(2)}) collective-permute-start(bf16[128,1024]{1,0:T(8,128)(2,1)S(1)} %slice.33), channel_id=1, source_target_pairs={{0,16},{16,0},{1,17},{17,1},{2,18},{18,2},{3,19},{19,3},{4,20},{20... | collective-permute-start | bytes 786440 | tf_op jit(solution)/shard_map/ppermute | solution.py:261
  53.7 14.0 %collective-permute-start.2 = (bf16[192,1024]{1,0:T(8,128)(2,1)S(1)}, bf16[192,1024]{1,0:T(8,128)(2,1)S(1)}, u32[]{:S(2)}, u32[]{:S(2)}) collective-permute-start(bf16[192,1024]{1,0:T(8,128)(2,1)S(1)} %collective-permute-done.1.refs_0_), channel_id=1, source_target_pairs={{0,4},{1,5},{2,6},{3,7},{4,8},{5,9},{6,10},{7,11},{8,12},{9,13},{1... | collective-permute-start | bytes 1179656 | tf_op jit(solution)/shard_map/ppermute | solution.py:252
  56.1 15.8 %collective-permute-start.31 = (bf16[2,384,128]{2,1,0:T(8,128)(2,1)S(1)}, bf16[2,384,128]{2,1,0:T(8,128)(2,1)S(1)}, u32[]{:S(2)}, u32[]{:S(2)}) collective-permute-start(bf16[2,384,128]{2,1,0:T(8,128)(2,1)S(1)} %get-tuple-element.41), channel_id=1, source_target_pairs={{0,4},{1,5},{2,6},{3,7},{4,8},{5,9},{6,10},{7,11},{8,12},{9,13},{1... | collective-permute-start | bytes 589832 | tf_op jit(solution)/shard_map/ppermute | solution.py:252
  57.4 20.0 %collective-permute-start.32 = (bf16[2,384,128]{2,1,0:T(8,128)(2,1)S(1)}, bf16[2,384,128]{2,1,0:T(8,128)(2,1)S(1)}, u32[]{:S(2)}, u32[]{:S(2)}) collective-permute-start(bf16[2,384,128]{2,1,0:T(8,128)(2,1)S(1)} %get-tuple-element.42), channel_id=1, source_target_pairs={{0,8},{1,9},{2,10},{3,11},{4,12},{5,13},{6,14},{7,15},{8,0},{9,1},... | collective-permute-start | bytes 589832 | tf_op jit(solution)/shard_map/ppermute | solution.py:252
  60.5 18.7 %collective-permute-start.11 = (bf16[192,1024]{1,0:T(8,128)(2,1)S(1)}, bf16[192,1024]{1,0:T(8,128)(2,1)S(1)}, u32[]{:S(2)}, u32[]{:S(2)}) collective-permute-start(bf16[192,1024]{1,0:T(8,128)(2,1)S(1)} %collective-permute-done.1.refs_0_), channel_id=1, source_target_pairs={{0,2},{1,3},{2,0},{3,1},{4,6},{5,7},{6,4},{7,5},{8,10},{9,11},{10,... | collective-permute-start | bytes 1179656 | tf_op jit(solution)/shard_map/ppermute | solution.py:255
  62.0 16.6 %collective-permute-start.33 = (bf16[2,384,128]{2,1,0:T(8,128)(2,1)S(1)}, bf16[2,384,128]{2,1,0:T(8,128)(2,1)S(1)}, u32[]{:S(2)}, u32[]{:S(2)}) collective-permute-start(bf16[2,384,128]{2,1,0:T(8,128)(2,1)S(1)} %get-tuple-element.43), channel_id=1, source_target_pairs={{0,12},{1,13},{2,14},{3,15},{4,0},{5,1},{6,2},{7,3},{8,4},{9,5},{1... | collective-permute-start | bytes 589832 | tf_op jit(solution)/shard_map/ppermute | solution.py:252
  67.7 24.0 %collective-permute-start.22 = (bf16[192,1024]{1,0:T(8,128)(2,1)S(1)}, bf16[192,1024]{1,0:T(8,128)(2,1)S(1)}, u32[]{:S(2)}, u32[]{:S(2)}) collective-permute-start(bf16[192,1024]{1,0:T(8,128)(2,1)S(1)} %collective-permute-done.18.refs_2_), channel_id=1, source_target_pairs={{0,1},{1,0},{2,3},{3,2},{4,5},{5,4},{6,7},{7,6},{8,9},{9,8},{10,11... | collective-permute-start | bytes 1179656 | tf_op jit(solution)/shard_map/ppermute | solution.py:258
  71.9 19.8 %collective-permute-start.13 = (bf16[192,1024]{1,0:T(8,128)(2,1)S(1)}, bf16[192,1024]{1,0:T(8,128)(2,1)S(1)}, u32[]{:S(2)}, u32[]{:S(2)}) collective-permute-start(bf16[192,1024]{1,0:T(8,128)(2,1)S(1)} %collective-permute-done.1.refs_0_), channel_id=1, source_target_pairs={{0,1},{1,0},{2,3},{3,2},{4,5},{5,4},{6,7},{7,6},{8,9},{9,8},{10,11... | collective-permute-start | bytes 1179656 | tf_op jit(solution)/shard_map/ppermute | solution.py:258
  77.5 15.8 %collective-permute-start.4 = (bf16[192,1024]{1,0:T(8,128)(2,1)S(1)}, bf16[192,1024]{1,0:T(8,128)(2,1)S(1)}, u32[]{:S(2)}, u32[]{:S(2)}) collective-permute-start(bf16[192,1024]{1,0:T(8,128)(2,1)S(1)} %collective-permute-done.2.refs_0_), channel_id=1, source_target_pairs={{0,2},{1,3},{2,0},{3,1},{4,6},{5,7},{6,4},{7,5},{8,10},{9,11},{10,... | collective-permute-start | bytes 1179656 | tf_op jit(solution)/shard_map/ppermute | solution.py:255
  78.6 14.3 %collective-permute-start.23 = (bf16[128,1024]{1,0:T(8,128)(2,1)S(1)}, bf16[128,1024]{1,0:T(8,128)(2,1)S(1)}, u32[]{:S(2)}, u32[]{:S(2)}) collective-permute-start(bf16[128,1024]{1,0:T(8,128)(2,1)S(1)} %collective-permute-done.19.refs_3_), channel_id=1, source_target_pairs={{0,1},{1,0},{2,3},{3,2},{4,5},{5,4},{6,7},{7,6},{8,9},{9,8},{10,11... | collective-permute-start | bytes 786440 | tf_op jit(solution)/shard_map/ppermute | solution.py:258
  90.5 17.3 %collective-permute-start.15 = (bf16[192,1024]{1,0:T(8,128)(2,1)S(1)}, bf16[192,1024]{1,0:T(8,128)(2,1)S(1)}, u32[]{:S(2)}, u32[]{:S(2)}) collective-permute-start(bf16[192,1024]{1,0:T(8,128)(2,1)S(1)} %collective-permute-done.11.refs_2_), channel_id=1, source_target_pairs={{0,1},{1,0},{2,3},{3,2},{4,5},{5,4},{6,7},{7,6},{8,9},{9,8},{10,11... | collective-permute-start | bytes 1179656 | tf_op jit(solution)/shard_map/ppermute | solution.py:258
  93.0 14.2 %collective-permute-start.14 = (bf16[128,1024]{1,0:T(8,128)(2,1)S(1)}, bf16[128,1024]{1,0:T(8,128)(2,1)S(1)}, u32[]{:S(2)}, u32[]{:S(2)}) collective-permute-start(bf16[128,1024]{1,0:T(8,128)(2,1)S(1)} %collective-permute-done.10.refs_1_), channel_id=1, source_target_pairs={{0,1},{1,0},{2,3},{3,2},{4,5},{5,4},{6,7},{7,6},{8,9},{9,8},{10,11... | collective-permute-start | bytes 786440 | tf_op jit(solution)/shard_map/ppermute | solution.py:258
  93.2 14.0 %collective-permute-start.12 = (bf16[128,1024]{1,0:T(8,128)(2,1)S(1)}, bf16[128,1024]{1,0:T(8,128)(2,1)S(1)}, u32[]{:S(2)}, u32[]{:S(2)}) collective-permute-start(bf16[128,1024]{1,0:T(8,128)(2,1)S(1)} %slice.31), channel_id=1, source_target_pairs={{0,16},{16,0},{1,17},{17,1},{2,18},{18,2},{3,19},{19,3},{4,20},{20... | collective-permute-start | bytes 786440 | tf_op jit(solution)/shard_map/ppermute | solution.py:261
  107.2 14.7 %collective-permute-start.6 = (bf16[192,1024]{1,0:T(8,128)(2,1)S(1)}, bf16[192,1024]{1,0:T(8,128)(2,1)S(1)}, u32[]{:S(2)}, u32[]{:S(2)}) collective-permute-start(bf16[192,1024]{1,0:T(8,128)(2,1)S(1)} %collective-permute-done.2.refs_0_), channel_id=1, source_target_pairs={{0,1},{1,0},{2,3},{3,2},{4,5},{5,4},{6,7},{7,6},{8,9},{9,8},{10,11... | collective-permute-start | bytes 1179656 | tf_op jit(solution)/shard_map/ppermute | solution.py:258
  107.7 14.1 %collective-permute-start.8 = (bf16[192,1024]{1,0:T(8,128)(2,1)S(1)}, bf16[192,1024]{1,0:T(8,128)(2,1)S(1)}, u32[]{:S(2)}, u32[]{:S(2)}) collective-permute-start(bf16[192,1024]{1,0:T(8,128)(2,1)S(1)} %collective-permute-done.4.refs_2_), channel_id=1, source_target_pairs={{0,1},{1,0},{2,3},{3,2},{4,5},{5,4},{6,7},{7,6},{8,9},{9,8},{10,11... | collective-permute-start | bytes 1179656 | tf_op jit(solution)/shard_map/ppermute | solution.py:258
  115.8 11.9 %collective-permute-start.39 = (f32[2,4,64,128]{3,2,1,0:T(8,128)S(1)}, f32[2,4,64,128]{3,2,1,0:T(8,128)S(1)}, u32[]{:S(2)}, u32[]{:S(2)}) collective-permute-start(f32[2,4,64,128]{3,2,1,0:T(8,128)S(1)} %pad_maximum_fusion.own), channel_id=1, source_target_pairs={{0,1},{1,0},{2,3},{3,2},{4,5},{5,4},{6,7},{7,6},{8,9},{9,8},{10,11... | collective-permute-start | bytes 786440 | tf_op jit(solution)/shard_map/ppermute | solution.py:258
  (24 other events, 283.5 us)

commit v2 on v0

v2 whole, which is shorter than its diff:
```python
import functools

import jax
import jax.numpy as jnp
from jax import lax
from jax.experimental import pallas as pl
from jax.experimental.pallas import tpu as pltpu
from jax.sharding import PartitionSpec as P

BLOCK = 128
ADAPTER_RANK = 16
STRIP = 64
VMEM_LIMIT = 12 * 1024 * 1024
F32 = jnp.float32
BF16 = jnp.bfloat16


def dequant_rows(piece, scales):
    count = piece.shape[0]
    block_of = lax.iota(jnp.int32, count) // BLOCK
    select = (block_of[:, None] == lax.iota(jnp.int32, scales.shape[0])[None, :]).astype(F32)
    row_scales = jnp.dot(select, scales, precision=lax.Precision.HIGHEST)
    expanded = jnp.repeat(row_scales, BLOCK, axis=1)
    return (piece.astype(F32) * expanded).astype(BF16)


def reduce_over_rows(left, right):
    return lax.dot_general(left, right, (((1,), (1,)), ((), ())), preferred_element_type=F32)


def contract_tokens(left, right):
    return lax.dot_general(left, right, (((0,), (0,)), ((), ())), preferred_element_type=F32)


def plain_path(tokens, token_adapter_index, frozen, scales, down, up, cotangent):
    rank_adapter = lax.iota(jnp.int32, down.shape[1]) // ADAPTER_RANK
    mask = (token_adapter_index[:, None] == rank_adapter[None, :]).astype(F32)
    shrink = (jnp.dot(tokens, down, preferred_element_type=F32) * mask).astype(BF16)
    spread = (2.0 * reduce_over_rows(cotangent, up) * mask).astype(BF16)
    weight = dequant_rows(lax.all_gather(frozen, "seq", axis=0, tiled=True), scales)
    values = jnp.dot(tokens, weight, preferred_element_type=F32)
    values = (values + 2.0 * jnp.dot(shrink, up, preferred_element_type=F32)).astype(BF16)
    act = reduce_over_rows(cotangent, weight) + reduce_over_rows(spread, down)
    grad_a = lax.psum_scatter(
        contract_tokens(tokens, spread), "seq", scatter_dimension=0, tiled=True
    )
    grad_b = lax.psum(2.0 * contract_tokens(shrink, cotangent), "seq")
    return values, act.astype(BF16), grad_a, grad_b


GAP = 60
VMEM = pl.BlockSpec(memory_space=pltpu.VMEM)
SMEM = pl.BlockSpec(memory_space=pltpu.SMEM)
ANY = pl.BlockSpec(memory_space=pl.ANY)
HBM = pl.BlockSpec(memory_space=pltpu.HBM)


def struct(shape, dtype):
    return jax.ShapeDtypeStruct(shape, dtype)


def kernel(body, name, us, out_shape, in_specs, out_specs, operands, scratch=(), alias=None):
    return pl.pallas_call(
        body,
        name=name,
        in_specs=in_specs,
        out_specs=out_specs,
        out_shape=out_shape,
        scratch_shapes=scratch,
        input_output_aliases=alias or {},
        compiler_params=pltpu.CompilerParams(vmem_limit_bytes=VMEM_LIMIT),
        cost_estimate=pl.CostEstimate(
            flops=int(us * 1.1e9), bytes_accessed=1, transcendentals=0
        ),
    )(*operands)


def after(value, *others):
    return lax.optimization_barrier((value,) + others)[0]


def place():
    s = lax.axis_index("seq")
    return s // 4, s // 2 % 2, s % 2, lax.axis_index("groups")


def strip_places(core, x):
    low = core * STRIP
    return low + x * (2 * STRIP), (1 - core) * (4 * STRIP), low + (1 - x) * (2 * STRIP)


def fetch(pairs, sems):
    copies = [pltpu.make_async_copy(a, b, sems.at[i]) for i, (a, b) in enumerate(pairs)]
    for copy in copies:
        copy.start()
    return copies


def dequant_body(w_far, scales_far, shared, rest, w, scales, sems):
    for copy in fetch(((scales_far, scales), (w_far, w)), sems):
        copy.wait()
    z, y, c, x = place()
    first = ((z * 2 + y) * 2 + c) * (w.shape[0] // STRIP)

    def scale_strips(out, at, count, source):
        for i in range(count // STRIP):
            start = source + i * STRIP
            block_row = (first * STRIP + start) // BLOCK
            rows = pl.ds(pl.multiple_of(start, STRIP), STRIP)
            for b in range(w.shape[1] // BLOCK):
                columns = pl.ds(b * BLOCK, BLOCK)
                value = w[rows, columns].astype(F32) * scales[b, block_row]
                out[pl.ds(at + i * STRIP, STRIP), columns] = value.astype(BF16)

    kept = rest.shape[0]
    mine, middle, other = strip_places(c, x)
    scale_strips(shared, 0, kept, mine)
    scale_strips(shared, kept, shared.shape[0] - kept, middle)
    scale_strips(rest, 0, kept, other)


def grads_body(rows, tok_far, idx, down_far, up_far, cot_far, _, *refs):
    shrink, spread, send, keep, tok, down, up, cot, acc, sems = refs
    c = place()[2]
    ranks, planes = up.shape[0], send.shape[0]
    depth = tok.shape[1] // planes
    half = ranks // 2
    pairs = [(up_far, up), (cot_far, cot)]
    for j in range(planes):
        part = pl.ds(j * depth, depth)
        pairs += [(tok_far.at[:, part], tok.at[:, part]), (down_far.at[part, :], down.at[part, :])]
    copies = fetch(pairs, sems)
    rank_adapter = lax.broadcasted_iota(jnp.int32, (ranks, 1), 0) // ADAPTER_RANK
    mask = (idx[...] == rank_adapter).astype(F32).T
    copies[0].wait()
    copies[1].wait()
    spread[...] = (2.0 * reduce_over_rows(cot[...], up[...]) * mask).astype(BF16)

    def store(j, y, core, at, value):
        @pl.when(c == core)
        def _():
            keep[j, y, pl.ds(at, value.shape[0]), :] = value

        @pl.when(c != core)
        def _():
            send[j, y, pl.ds(at, value.shape[0]), :] = value

    for j in range(planes):
        copies[2 + 2 * j].wait()
        copies[3 + 2 * j].wait()
        block = tok[:, j * depth : (j + 1) * depth]
        sum_j = jnp.dot(block, down[j * depth : (j + 1) * depth], preferred_element_type=F32)
        if j == 0:
            acc[...] = sum_j
        else:
            acc[...] += sum_j
        part = contract_tokens(block, spread[...])
        for y in range(2):
            for core in range(2):
                at = (y * 2 + core) * rows
                store(j, y, core, 0, part[at : at + rows])
    shrink[...] = (acc[...] * mask).astype(BF16)
    grad_b = contract_tokens(shrink[...], cot[...])
    for y in range(2):
        for j in range(planes):
            at = (y * planes + j) * ranks
            for core in range(2):
                piece = grad_b[core * half : (core + 1) * half, at : at + ranks]
                store(j, y, core, rows, piece)


def core_sum_body(keep, got, own, other):
    y = place()[1]
    for j in range(keep.shape[0]):
        own[j] = keep[j, y] + got[j, y]
        other[j] = (keep[j, 1 - y] + got[j, 1 - y]).astype(BF16)


def side_sum_body(rows, own, got, mine, s1, s2, s3):
    z = place()[0]
    planes, each = own.shape[:2]
    half = each - rows
    a_part = pl.ds(0, rows)
    for step, out in enumerate((mine, s1, s2, s3)):
        to = lax.rem(z + step, planes)
        piece = own[to, a_part, :] + got[to, a_part, :].astype(F32)
        out[pl.ds(0, rows), :] = piece.astype(out.dtype)
    for j in range(planes):
        piece = own[j, pl.ds(rows, half), :] + got[j, pl.ds(rows, half), :].astype(F32)
        piece = piece.astype(BF16)
        for out in (mine, s1, s2, s3):
            out[pl.ds(rows + j * half, half), :] = piece.astype(out.dtype)


def line_sum_body(mine, r1, r2, r3, grad_a, quarter):
    rows = grad_a.shape[0]
    total = (mine[...] + r2[...].astype(F32)) + (r1[...].astype(F32) + r3[...].astype(F32))
    grad_a[...] = total[:rows]
    quarter[...] = 2.0 * total[rows:]


def place_b_body(mine, side, core, core_side, out):
    _, y, c, _ = place()
    ranks = out.shape[0]
    half = ranks // 2
    planes = mine.shape[0] // half
    for ref, yy, cc in ((mine, y, c), (side, 1 - y, c), (core, y, 1 - c), (core_side, 1 - y, 1 - c)):
        row = pl.multiple_of(cc * half, half)
        for j in range(planes):
            column = pl.multiple_of((yy * planes + j) * ranks, ranks)
            out[pl.ds(row, half), pl.ds(column, ranks)] = ref[pl.ds(j * half, half), :]


def plane_body(k, first, rows, kept, counts, tok_far, cot, spread, down_far, *refs):
    pieces, refs = refs[: sum(counts)], refs[sum(counts) :]
    if first:
        shrink, up, act, acc, weight, block, tok, down, sem, sems = refs
    else:
        total, _, act, acc, weight, block, tok, down, sem, sems = refs
    z, y, c, x = place()
    depth = weight.shape[0]
    zz = lax.rem(z + 4 - k, 4)
    columns = pl.ds(pl.multiple_of(zz * depth, depth), depth)
    copies = fetch(((down_far.at[columns, :], down), (tok_far.at[:, columns], tok)), sems)
    middle = rows - 2 * kept

    def put(ref, at, count, to):
        weight[pl.ds(pl.multiple_of(to, STRIP), count), :] = ref[pl.ds(at, count), :]

    for h, cc in enumerate((c, 1 - c)):
        own = pieces[: counts[0]] if h == 0 else pieces[counts[0] :]
        where = []
        for ref in own:
            where += [(ref, at) for at in range(0, ref.shape[0], STRIP)]
        strips = iter(where)
        bases = [((y if i == 0 else 1 - y) * 2 + cc) * rows for i in range(2)]
        mine, inner, other = strip_places(cc, x)

        def next_strips(count, to):
            for i in range(count // STRIP):
                ref, at = next(strips, (None, 0))
                if ref is None:
                    here = pl.ds(pl.multiple_of(to + i * STRIP, STRIP), STRIP)
                    weight[here, :] = jnp.zeros((STRIP, weight.shape[1]), BF16)
                else:
                    put(ref, at, STRIP, to + i * STRIP)

        for base in bases:
            next_strips(kept, base + mine)
            next_strips(middle, base + inner)
        for base in bases:
            next_strips(kept, base + other)

    back = reduce_over_rows(cot[...], weight[...])
    copies[0].wait()
    back += reduce_over_rows(spread[...], down[...])
    block[...] = back.astype(BF16)
    copy = pltpu.make_async_copy(block, act.at[:, columns], sem)
    copy.start()
    copies[1].wait()
    forward = jnp.dot(tok[...], weight[...], preferred_element_type=F32)
    if first:
        forward += 2.0 * jnp.dot(shrink[...], up[...], preferred_element_type=F32)
    else:
        forward += total[...]
    acc[...] = forward
    copy.wait()


def last_body(k, rows, tok_far, cot, spread, down_far, own, got, total, _, act, values, *refs):
    tok, down, block, sems, sent = refs
    z, y, c, x = place()
    kept = own.shape[0]
    zz = lax.rem(z + 4 - k, 4)
    parts = []
    for cc in (c, 1 - c):
        start = ((zz * 2 + 1 - y) * 2 + cc) * rows + strip_places(cc, x)[2]
        parts.append(pl.ds(pl.multiple_of(start, BLOCK), kept))
    pairs = []
    for i, part in enumerate(parts):
        pairs += [(down_far.at[part, :], down.at[i]), (tok_far.at[:, part], tok.at[i])]
    copies = fetch(pairs, sems)
    outs = []
    for i, (part, weight) in enumerate(zip(parts, (own, got))):
        back = reduce_over_rows(cot[...], weight[...])
        copies[2 * i].wait()
        back += reduce_over_rows(spread[...], down[i])
        block[i] = back.astype(BF16)
        out = pltpu.make_async_copy(block.at[i], act.at[:, part], sent.at[i])
        out.start()
        outs.append(out)
    copies[1].wait()
    forward = total[...] + jnp.dot(tok[0], own[...], preferred_element_type=F32)
    copies[3].wait()
    forward += jnp.dot(tok[1], got[...], preferred_element_type=F32)
    values[...] = forward.astype(BF16)
    for out in outs:
        out.wait()


def cut_body(ref, out):
    out[...] = ref[pl.ds(0, out.shape[0]), :]


def pack_body(*refs):
    out, at = refs[-1], 0
    for ref in refs[:-1]:
        out[pl.ds(at, ref.shape[0]), :] = ref[...]
        at += ref.shape[0]


def swap(n, move):
    pairs = []
    for s in range(n):
        z, y, c = move(s // 4, s // 2 % 2, s % 2)
        pairs.append((s, (z % (n // 4) * 2 + y) * 2 + c))
    return pairs


def block_path(tokens, token_adapter_index, frozen, scales, down, up, cotangent):
    n, planes = 16, 4
    count, width = tokens.shape
    rows, columns = frozen.shape
    ranks = up.shape[0]
    depth = width // planes
    kept = 2 * STRIP
    shared_rows = rows - kept
    half = ranks // 2
    each = rows + half

    def over_z(name, v, by=1):
        with jax.named_scope(name):
            return lax.ppermute(v, "seq", swap(n, lambda z, y, c: (z + by, y, c)))

    def over_y(name, v):
        with jax.named_scope(name):
            return lax.ppermute(v, "seq", swap(n, lambda z, y, c: (z, 1 - y, c)))

    def over_core(name, v):
        with jax.named_scope(name):
            return lax.ppermute(v, "seq", swap(n, lambda z, y, c: (z, y, 1 - c)))

    def over_x(name, v):
        with jax.named_scope(name):
            return lax.ppermute(v, "groups", [(0, 1), (1, 0)])

    p0, rest = kernel(
        dequant_body,
        "scale_rows",
        5,
        [struct((shared_rows, columns), BF16), struct((kept, columns), BF16)],
        [HBM, HBM],
        [VMEM, VMEM],
        (frozen, scales.T),
        scratch=[
            pltpu.VMEM((rows, columns), BF16),
            pltpu.SMEM(scales.shape[::-1], F32),
            pltpu.SemaphoreType.DMA((2,)),
        ],
    )
    z1, y0 = over_z("z1", p0), over_y("y0", p0)

    piece = (planes, 2, each, ranks)
    shrink, spread, send, keep = kernel(
        functools.partial(grads_body, rows),
        "gradient_shares",
        6,
        [struct((count, ranks), BF16)] * 2 + [struct(piece, F32)] * 2,
        [HBM, VMEM, HBM, HBM, HBM, ANY],
        [VMEM] * 4,
        (tokens, token_adapter_index[None, :], down, up, cotangent, p0),
        scratch=[
            pltpu.VMEM(tokens.shape, BF16),
            pltpu.VMEM(down.shape, BF16),
            pltpu.VMEM(up.shape, BF16),
            pltpu.VMEM(cotangent.shape, BF16),
            pltpu.VMEM((count, ranks), F32),
            pltpu.SemaphoreType.DMA((2 + 2 * planes,)),
        ],
    )

    def plane(k, own, got, state):
        first = k == 0
        operands = [tokens, cotangent, spread, down] + own + got
        if first:
            operands += [shrink, up]
            specs = [HBM, VMEM, VMEM, HBM] + [VMEM] * (len(operands) - 4)
            alias = None
        else:
            operands += [state[1], state[0]]
            specs = [HBM, VMEM, VMEM, HBM] + [VMEM] * (len(operands) - 5) + [HBM]
            alias = {len(operands) - 1: 0}
        return kernel(
            functools.partial(plane_body, k, first, rows, kept, (len(own), len(got))),
            f"plane_{k}",
            GAP,
            [struct((count, width), BF16), struct((count, columns), F32)],
            specs,
            [HBM, VMEM],
            operands,
            scratch=[
                pltpu.VMEM((depth, columns), BF16),
                pltpu.VMEM((count, depth), BF16),
                pltpu.VMEM((count, depth), BF16),
                pltpu.VMEM((depth, ranks), BF16),
                pltpu.SemaphoreType.DMA,
                pltpu.SemaphoreType.DMA((2,)),
            ],
            alias=alias,
        )

    def pack(name, *parts):
        return kernel(
            pack_body,
            name,
            0,
            struct((sum(v.shape[0] for v in parts), columns), BF16),
            [VMEM] * len(parts),
            VMEM,
            parts,
        )

    def pack(name, *parts):
        return kernel(
            pack_body,
            name,
            0,
            struct((sum(v.shape[0] for v in parts), columns), BF16),
            [VMEM] * len(parts),
            VMEM,
            parts,
        )

    def last_rows(k, own, got, act, total):
        return kernel(
            functools.partial(last_body, k, rows),
            "last_rows",
            0,
            [struct((count, width), BF16), struct((count, columns), BF16)],
            [HBM, VMEM, VMEM, HBM, VMEM, VMEM, VMEM, HBM],
            [HBM, VMEM],
            [tokens, cotangent, spread, down, own, got, total, act],
            scratch=[
                pltpu.VMEM((2, count, kept), BF16),
                pltpu.VMEM((2, kept, ranks), BF16),
                pltpu.VMEM((2, count, kept), BF16),
                pltpu.SemaphoreType.DMA((4,)),
                pltpu.SemaphoreType.DMA((2,)),
            ],
            alias={7: 0},
        )

    e = {}
    last = []

    def event(*names):
        for name in names:
            if last and last[0] != name:
                e[name], e[last[0]] = lax.optimization_barrier((e[name], e[last[0]]))
            last[:] = [name]

    def cut(name, v, us=0.0):
        return kernel(
            cut_body, name, us, struct((kept, columns), BF16), [VMEM], VMEM, (v,)
        )

    def run_plane(k, own, got, state):
        own = [e[v] if isinstance(v, str) else v for v in own]
        state = plane(k, own, [e[v] for v in got], state)
        e["acc"] = state[1]
        event("acc")
        return state[0]

    e["share"] = over_core("core_share", send)
    e["z1"], e["y0"] = z1, y0
    event("z1")
    e["z2"], e["y1"] = over_z("z2", e["z1"]), over_y("y1", e["z1"])
    event("y0")
    e["x0"] = over_x("x0", e["y0"][:kept])
    e["cut"] = cut("cut_1", e["z1"], GAP)
    event("cut")
    e["x1a"] = over_x("x1a", e["cut"])
    event("share")
    e["own_y"], other_y = kernel(
        core_sum_body,
        "core_sum",
        0,
        [struct((planes, each, ranks), F32), struct((planes, each, ranks), BF16)],
        [VMEM] * 2,
        [VMEM] * 2,
        (keep, e["share"]),
    )
    event("own_y")
    e["side"] = over_y("side_share", other_y)
    event("z2")
    e["z3"], e["y2"] = over_z("z3", e["z2"]), over_y("y2", e["z2"])
    e["x2a"] = over_x("x2a", e["z2"][:kept])
    event("x1a")
    event("x0")
    e["c0"] = over_core("c0", pack("pack_0", p0, e["y0"], rest, e["x0"]))
    event("y1")
    e["x1b"] = over_x("x1b", e["y1"][:kept])
    event("side")
    line = struct((rows + planes * half, ranks), BF16)
    e["mine"], s1, s2, s3 = kernel(
        functools.partial(side_sum_body, rows),
        "side_sum",
        GAP,
        [struct(line.shape, F32), line, line, line],
        [VMEM] * 2,
        [VMEM] * 4,
        (e["own_y"], e["side"]),
    )
    event("mine")
    for i, v in enumerate((s1, s2, s3)):
        e[f"r{i + 1}"] = over_z(f"line_{i + 1}", v, i + 1)
    event("z3")
    e["y3"], e["x3a"] = over_y("y3", e["z3"]), over_x("x3a", e["z3"][:kept])
    event("x2a")
    event("x1b")
    e["c1"] = over_core("c1", pack("pack_1", e["z1"], e["y1"], e["x1a"], e["x1b"]))
    event("c0")
    act = run_plane(0, [p0, "y0", rest, "x0"], ["c0"], None)
    event("y2")
    e["x2b"] = over_x("x2b", e["y2"][:kept])
    event("x3a")
    event("c1")
    act = run_plane(1, ["z1", "y1", "x1a", "x1b"], ["c1"], (act, e["acc"]))
    event("y3")
    e["x3b"] = over_x("x3b", e["y3"][:kept])
    e["c3a"] = over_core("c3a", pack("pack_3", e["z3"], e["y3"], e["x3a"]))
    event("x2b")
    e["c2"] = over_core("c2", pack("pack_2", e["z2"], e["y2"], e["x2a"], e["x2b"]))
    event("r1")
    event("r2")
    event("r3")
    grad_a, e["quarter"] = kernel(
        line_sum_body,
        "line_sum",
        GAP,
        [struct((rows, ranks), F32), struct((planes * half, ranks), F32)],
        [VMEM] * 4,
        [VMEM] * 2,
        (e["mine"], e["r1"], e["r2"], e["r3"]),
    )
    event("quarter")
    e["side_quarter"] = over_y("side_up", e["quarter"])
    e["core_quarter"] = over_core("core_up", e["quarter"])
    event("c2")
    act = run_plane(2, ["z2", "y2", "x2a", "x2b"], ["c2"], (act, e["acc"]))
    event("c3a")
    act = run_plane(3, ["z3", "y3", "x3a"], ["c3a"], (act, e["acc"]))
    event("side_quarter")
    e["core_side"] = over_core("core_side_up", e["side_quarter"])
    event("core_quarter")
    event("core_side")
    grad_b = kernel(
        place_b_body,
        "place_up_gradient",
        0,
        struct((ranks, columns), F32),
        [VMEM] * 4,
        VMEM,
        (e["quarter"], e["side_quarter"], e["core_quarter"], e["core_side"]),
    )
    event("x3b")
    e["c3b"] = over_core("c3b", e["x3b"])
    event("c3b")
    act, values = last_rows(3, e["x3b"], e["c3b"], act, e["acc"])
    return values, act, grad_a, grad_b


def solution(mesh):
    sizes = (mesh.shape["groups"], mesh.shape["seq"])

    def on_device(*operands):
        rows, columns = operands[2].shape
        ranks = operands[5].shape[0]
        fits = rows == 5 * STRIP and columns == 8 * ranks
        path = block_path if sizes == (2, 16) and fits and ranks == BLOCK else plain_path
        return path(*operands)

    return jax.shard_map(
        on_device,
        mesh=mesh,
        in_specs=(
            P(("groups", "seq"), None),
            P(("groups", "seq")),
            P("seq", None),
            P(),
            P("groups", None),
            P("groups", None),
            P(("groups", "seq"), None),
        ),
        out_specs=(
            P(("groups", "seq"), None),
            P(("groups", "seq"), None),
            P(("groups", "seq"), None),
            P("groups", None),
        ),
        check_vma=False,
    )
```

time: 271 us -> 79.5 us (0.29)
  waiting for transfers between devices: 180 us -> 25.9 us
  matrix products: 50.2 us -> 0 us
  starting transfers between devices: 0.12 us -> 25.8 us
  Pallas kernels: 0 us -> 24.5 us
  local copies, waits for them, and re-layouts: 25.9 us -> 1.9 us
  between operations: 13.9 us -> 1.07 us
    all_gather x1 -> x0, waiting for transfers between devices: 76.2 us -> none  [on_device(): gathered = lax.all_gather(frozen_value_weight, 'seq', axis=0, tiled=True)]
    unnamed x4 -> x0, waiting for transfers between devices: 69.4 us -> none
    dot_general x9 -> x0, matrix products: 50.2 us -> none  [the longest x1 20 us: on_device(): forward_pass = jnp.dot(tokens, weight, preferred_element_type=jnp.float32)]
    psum x1 -> x0, waiting for transfers between devices: 34.6 us -> none  [on_device(): grad_b = lax.psum(2.0 * contract_tokens(down_projected, cotangent), 'seq')]
    ppermute x0 -> x27, waiting for transfers between devices: none -> 25.9 us  [the longest x6 12.7 us: over_z(): return lax.ppermute(v, 'seq', swap(n, lambda z, y, c: (z + by, y, c)))]
    ppermute x0 -> x27, starting transfers between devices: none -> 25.8 us  [the longest x6 9.22 us: over_z(): return lax.ppermute(v, 'seq', swap(n, lambda z, y, c: (z + by, y, c)))]
    pallas_call x0 -> x16, Pallas kernels: none -> 24.5 us  [kernel(): pl.pallas_call(body, name=name, in_specs=in_specs, out_specs=out_specs, o...]
    unnamed x14, local copies, waits for them, and re-layouts: 14.4 us -> 1.79 us
  transfers between devices with their start and end apart: 3 -> 27, of which waited for: 3 -> 9; matrix products, arithmetic and copies ran while one was open for 27% -> 0% of each run, Pallas kernels for 0% -> 26%
where the time goes in v2:
time: 79.5 us; the launch traced here: 79.3 us
  waiting for transfers between devices  25.9 us (33%)
  starting transfers between devices  25.8 us (32%)
  Pallas kernels  24.5 us (31%)
  local copies, waits for them, and re-layouts  1.9 us (2%)
  between operations  1.07 us (1%)
    pallas_call x16, Pallas kernels, kernel(): pl.pallas_call(body, name=name, in_specs=in_specs, out_specs=out_specs, o...  24.5 us
    ppermute x6, waiting for transfers between devices, over_z(): return lax.ppermute(v, 'seq', swap(n, lambda z, y, c: (z + by, y, c)))  12.7 us
    ppermute x6, starting transfers between devices, over_z(): return lax.ppermute(v, 'seq', swap(n, lambda z, y, c: (z + by, y, c)))  9.22 us
    ppermute x6, starting transfers between devices, over_y(): return lax.ppermute(v, 'seq', swap(n, lambda z, y, c: (z, 1 - y, c)))  8.6 us
    ppermute x7, waiting for transfers between devices, over_x(): return lax.ppermute(v, 'groups', [(0, 1), (1, 0)])  7.41 us
    ppermute x7, starting transfers between devices, over_x(): return lax.ppermute(v, 'groups', [(0, 1), (1, 0)])  7 us
    ppermute x6, waiting for transfers between devices, over_y(): return lax.ppermute(v, 'seq', swap(n, lambda z, y, c: (z, 1 - y, c)))  3.95 us
    ppermute x8, waiting for transfers between devices, over_core(): return lax.ppermute(v, 'seq', swap(n, lambda z, y, c: (z, y, 1 - c)))  1.89 us
  transfers between devices with their start and end apart: 27, of which 9 were waited for; matrix products, arithmetic and copies ran while one was open for 0% of the time, Pallas kernels for 26%

profile of v2, /device:TPU:0, one launch (start us, length us, event | category | flops | bytes accessed | tf_op | source)
XLA Modules:
  0.0 79.3 jit_solution(7384847579432805827)
XLA Ops:
  3.2 3.1 %collective-permute-start = (bf16[192,1024]{1,0:T(8,128)(2,1)S(1)}, bf16[192,1024]{1,0:T(8,128)(2,1)S(1)}, u32[]{:S(2)}, u32[]{:S(2)}) collective-permute-start(bf16[192,1024]{1,0:T(8,128)(2,1)S(1)} %get-tuple-element.87._.refs_0_), channel_id=1, source_target_pairs={{0,4},{1,5},{2,6},{3,7},{4,8},{5,9},{6,10},{7,11},{8,12},{9,13},{1... | collective-permute-start | bytes 1179656 | tf_op jit(solution)/shard_map/z1/ppermute | solution.py:333
  6.3 1.5 %collective-permute-start.3 = (bf16[192,1024]{1,0:T(8,128)(2,1)S(1)}, bf16[192,1024]{1,0:T(8,128)(2,1)S(1)}, u32[]{:S(2)}, u32[]{:S(2)}) collective-permute-start(bf16[192,1024]{1,0:T(8,128)(2,1)S(1)} %get-tuple-element.87._.refs_0_), channel_id=1, source_target_pairs={{0,2},{1,3},{2,0},{3,1},{4,6},{5,7},{6,4},{7,5},{8,10},{9,11},{10,... | collective-permute-start | bytes 1179656 | tf_op jit(solution)/shard_map/y0/ppermute | solution.py:337
  7.9 5.1 %gradient_shares.1 = (bf16[384,128]{1,0:T(8,128)(2,1)S(1)}, bf16[384,128]{1,0:T(8,128)(2,1)S(1)}, f32[4,2,384,128]{3,2,1,0:T(8,128)S(1)}, f32[4,2,384,128]{3,2,1,0:T(8,128)S(1)}) custom-call(bf16[384,5120]{1,0:T(8,128)(2,1)S(1)} %copy-done, s32[1,384]{1,0:T(1,128)S(1)} %broadcast_in_dim.3.idx, bf16[5120,128]{1,0:T(8,128)(2,1)S(1)} %copy-done.1, ...), custom_call_target="tpu_custom_call" | custom-call | flops 6600000000 | bytes 1 | tf_op jit(solution)/shard_map/gradient_shares/pallas_call | solution.py:63
  13.0 4.4 %collective-permute-done.ref.refs_0_ = bf16[192,1024]{1,0:T(8,128)(2,1)S(1)} collective-permute-done((bf16[192,1024]{1,0:T(8,128)(2,1)S(1)}, bf16[192,1024]{1,0:T(8,128)(2,1)S(1)}, u32[]{:S(2)}, u32[]{:S(2)}) %collective-permute-start) | collective-permute-done | bytes 393248 | tf_op jit(solution)/shard_map/z1/ppermute | solution.py:333
  18.5 1.6 %collective-permute-start.6 = (bf16[192,1024]{1,0:T(8,128)(2,1)S(1)}, bf16[192,1024]{1,0:T(8,128)(2,1)S(1)}, u32[]{:S(2)}, u32[]{:S(2)}) collective-permute-start(bf16[192,1024]{1,0:T(8,128)(2,1)S(1)} %collective-permute-done.ref.refs_0_), channel_id=1, source_target_pairs={{0,2},{1,3},{2,0},{3,1},{4,6},{5,7},{6,4},{7,5},{8,10},{9,11},{10,... | collective-permute-start | bytes 1179656 | tf_op jit(solution)/shard_map/y1/ppermute | solution.py:337
  20.8 1.5 %collective-permute-start.8 = (bf16[128,1024]{1,0:T(8,128)(2,1)S(1)}, bf16[128,1024]{1,0:T(8,128)(2,1)S(1)}, u32[]{:S(2)}, u32[]{:S(2)}) collective-permute-start(bf16[128,1024]{1,0:T(8,128)(2,1)S(1)} %cut_1.1), channel_id=1, source_target_pairs={{0,16},{16,0},{1,17},{17,1},{2,18},{18,2},{3,19},{19,3},{4,20},{20... | collective-permute-start | bytes 786440 | tf_op jit(solution)/shard_map/x1a/ppermute | solution.py:345
  22.9 6.6 %collective-permute-done.1.refs_0_ = bf16[192,1024]{1,0:T(8,128)(2,1)S(1)} collective-permute-done((bf16[192,1024]{1,0:T(8,128)(2,1)S(1)}, bf16[192,1024]{1,0:T(8,128)(2,1)S(1)}, u32[]{:S(2)}, u32[]{:S(2)}) %collective-permute-start.1) | collective-permute-done | bytes 393248 | tf_op jit(solution)/shard_map/z2/ppermute | solution.py:333
  29.6 1.5 %collective-permute-start.15 = (bf16[192,1024]{1,0:T(8,128)(2,1)S(1)}, bf16[192,1024]{1,0:T(8,128)(2,1)S(1)}, u32[]{:S(2)}, u32[]{:S(2)}) collective-permute-start(bf16[192,1024]{1,0:T(8,128)(2,1)S(1)} %collective-permute-done.1.refs_0_), channel_id=1, source_target_pairs={{0,2},{1,3},{2,0},{3,1},{4,6},{5,7},{6,4},{7,5},{8,10},{9,11},{10,... | collective-permute-start | bytes 1179656 | tf_op jit(solution)/shard_map/y2/ppermute | solution.py:337
  31.1 1.7 %collective-permute-done.7.refs_3_ = bf16[128,1024]{1,0:T(8,128)(2,1)S(1)} collective-permute-done((bf16[128,1024]{1,0:T(8,128)(2,1)S(1)}, bf16[128,1024]{1,0:T(8,128)(2,1)S(1)}, u32[]{:S(2)}, u32[]{:S(2)}) %collective-permute-start.7) | collective-permute-done | bytes 262176 | tf_op jit(solution)/shard_map/x0/ppermute | solution.py:345
  32.9 1.5 %collective-permute-start.12 = (bf16[128,1024]{1,0:T(8,128)(2,1)S(1)}, bf16[128,1024]{1,0:T(8,128)(2,1)S(1)}, u32[]{:S(2)}, u32[]{:S(2)}) collective-permute-start(bf16[128,1024]{1,0:T(8,128)(2,1)S(1)} %slice.20), channel_id=1, source_target_pairs={{0,16},{16,0},{1,17},{17,1},{2,18},{18,2},{3,19},{19,3},{4,20},{20... | collective-permute-start | bytes 786440 | tf_op jit(solution)/shard_map/x2a/ppermute | solution.py:345
  35.1 3.9 %collective-permute-done.5.got = bf16[4,384,128]{2,1,0:T(8,128)(2,1)S(1)} collective-permute-done((bf16[4,384,128]{2,1,0:T(8,128)(2,1)S(1)}, bf16[4,384,128]{2,1,0:T(8,128)(2,1)S(1)}, u32[]{:S(2)}, u32[]{:S(2)}) %collective-permute-start.5) | collective-permute-done | bytes 393248 | tf_op jit(solution)/shard_map/side_share/ppermute | solution.py:337
  39.1 1.6 %collective-permute-done.4.refs_0_ = bf16[192,1024]{1,0:T(8,128)(2,1)S(1)} collective-permute-done((bf16[192,1024]{1,0:T(8,128)(2,1)S(1)}, bf16[192,1024]{1,0:T(8,128)(2,1)S(1)}, u32[]{:S(2)}, u32[]{:S(2)}) %collective-permute-start.4) | collective-permute-done | bytes 393248 | tf_op jit(solution)/shard_map/z3/ppermute | solution.py:333
  41.8 1.9 %collective-permute-done.11.refs_3_ = bf16[128,1024]{1,0:T(8,128)(2,1)S(1)} collective-permute-done((bf16[128,1024]{1,0:T(8,128)(2,1)S(1)}, bf16[128,1024]{1,0:T(8,128)(2,1)S(1)}, u32[]{:S(2)}, u32[]{:S(2)}) %collective-permute-start.11) | collective-permute-done | bytes 262176 | tf_op jit(solution)/shard_map/x1b/ppermute | solution.py:345
  43.7 1.5 %collective-permute-start.14 = (bf16[128,1024]{1,0:T(8,128)(2,1)S(1)}, bf16[128,1024]{1,0:T(8,128)(2,1)S(1)}, u32[]{:S(2)}, u32[]{:S(2)}) collective-permute-start(bf16[128,1024]{1,0:T(8,128)(2,1)S(1)} %slice.21), channel_id=1, source_target_pairs={{0,16},{16,0},{1,17},{17,1},{2,18},{18,2},{3,19},{19,3},{4,20},{20... | collective-permute-start | bytes 786440 | tf_op jit(solution)/shard_map/x3a/ppermute | solution.py:345
  45.4 1.6 %collective-permute-start.18 = (bf16[576,128]{1,0:T(8,128)(2,1)S(1)}, bf16[576,128]{1,0:T(8,128)(2,1)S(1)}, u32[]{:S(2)}, u32[]{:S(2)}) collective-permute-start(bf16[576,128]{1,0:T(8,128)(2,1)S(1)} %get-tuple-element.129), channel_id=1, source_target_pairs={{0,4},{1,5},{2,6},{3,7},{4,8},{5,9},{6,10},{7,11},{8,12},{9,13},{1... | collective-permute-start | bytes 442376 | tf_op jit(solution)/shard_map/line_1/ppermute | solution.py:333
  47.0 3.8 %plane_0.1 = (bf16[384,5120]{1,0:T(8,128)(2,1)}, f32[384,1024]{1,0:T(8,128)S(1)}) custom-call(bf16[384,5120]{1,0:T(8,128)(2,1)S(1)} %copy-done, bf16[384,1024]{1,0:T(8,128)(2,1)S(1)} %copy-done.2, bf16[384,128]{1,0:T(8,128)(2,1)S(1)} %get-tuple-element.88.spread, bf16[5120,128]{1,0:T(8,128)(2,1)S(1)} %copy-done.1, ...), custom_call_target="tpu_custom_call" | custom-call | flops 65999998976 | bytes 1 | tf_op jit(solution)/shard_map/plane_0/pallas_call | solution.py:63
  50.8 2.6 %collective-permute-start.17 = (bf16[576,128]{1,0:T(8,128)(2,1)S(1)}, bf16[576,128]{1,0:T(8,128)(2,1)S(1)}, u32[]{:S(2)}, u32[]{:S(2)}) collective-permute-start(bf16[576,128]{1,0:T(8,128)(2,1)S(1)} %get-tuple-element.128), channel_id=1, source_target_pairs={{0,8},{1,9},{2,10},{3,11},{4,12},{5,13},{6,14},{7,15},{8,0},{9,1},... | collective-permute-start | bytes 442376 | tf_op jit(solution)/shard_map/line_2/ppermute | solution.py:333
  55.2 3.2 %plane_1.1 = (bf16[384,5120]{1,0:T(8,128)(2,1)}, f32[384,1024]{1,0:T(8,128)S(1)}) custom-call(bf16[384,5120]{1,0:T(8,128)(2,1)S(1)} %copy-done, bf16[384,1024]{1,0:T(8,128)(2,1)S(1)} %copy-done.2, bf16[384,128]{1,0:T(8,128)(2,1)S(1)} %get-tuple-element.88.spread, bf16[5120,128]{1,0:T(8,128)(2,1)S(1)} %copy-done.1, ...), custom_call_target="tpu_custom_call", output_to_operand_aliasing={{0}: (10, {})} | custom-call | flops 65999998976 | bytes 1 | tf_op jit(solution)/shard_map/plane_1/pallas_call | solution.py:63
  58.4 3.8 %collective-permute-done.19.refs_3_ = bf16[128,1024]{1,0:T(8,128)(2,1)S(1)} collective-permute-done((bf16[128,1024]{1,0:T(8,128)(2,1)S(1)}, bf16[128,1024]{1,0:T(8,128)(2,1)S(1)}, u32[]{:S(2)}, u32[]{:S(2)}) %collective-permute-start.19) | collective-permute-done | bytes 262176 | tf_op jit(solution)/shard_map/x2b/ppermute | solution.py:345
  63.1 2.3 %collective-permute-start.21 = (f32[256,128]{1,0:T(8,128)S(1)}, f32[256,128]{1,0:T(8,128)S(1)}, u32[]{:S(2)}, u32[]{:S(2)}) collective-permute-start(f32[256,128]{1,0:T(8,128)S(1)} %get-tuple-element.167.mine), channel_id=1, source_target_pairs={{0,2},{1,3},{2,0},{3,1},{4,6},{5,7},{6,4},{7,5},{8,10},{9,11},{10,... | collective-permute-start | bytes 393224 | tf_op jit(solution)/shard_map/side_up/ppermute | solution.py:337
  66.6 3.2 %plane_2.1 = (bf16[384,5120]{1,0:T(8,128)(2,1)}, f32[384,1024]{1,0:T(8,128)S(1)}) custom-call(bf16[384,5120]{1,0:T(8,128)(2,1)S(1)} %copy-done, bf16[384,1024]{1,0:T(8,128)(2,1)S(1)} %copy-done.2, bf16[384,128]{1,0:T(8,128)(2,1)S(1)} %get-tuple-element.88.spread, bf16[5120,128]{1,0:T(8,128)(2,1)S(1)} %copy-done.1, ...), custom_call_target="tpu_custom_call", output_to_operand_aliasing={{0}: (10, {})} | custom-call | flops 65999998976 | bytes 1 | tf_op jit(solution)/shard_map/plane_2/pallas_call | solution.py:63
  69.8 3.2 %plane_3.1 = (bf16[384,5120]{1,0:T(8,128)(2,1)}, f32[384,1024]{1,0:T(8,128)S(1)}) custom-call(bf16[384,5120]{1,0:T(8,128)(2,1)S(1)} %copy-done, bf16[384,1024]{1,0:T(8,128)(2,1)S(1)} %copy-done.2, bf16[384,128]{1,0:T(8,128)(2,1)S(1)} %get-tuple-element.88.spread, bf16[5120,128]{1,0:T(8,128)(2,1)S(1)} %copy-done.1, ...), custom_call_target="tpu_custom_call", output_to_operand_aliasing={{0}: (9, {})} | custom-call | flops 65999998976 | bytes 1 | tf_op jit(solution)/shard_map/plane_3/pallas_call | solution.py:63
  73.2 1.3 %collective-permute-done.24.core_side = f32[256,128]{1,0:T(8,128)S(1)} collective-permute-done((f32[256,128]{1,0:T(8,128)S(1)}, f32[256,128]{1,0:T(8,128)S(1)}, u32[]{:S(2)}, u32[]{:S(2)}) %collective-permute-start.24) | collective-permute-done | bytes 131104 | tf_op jit(solution)/shard_map/core_side_up/ppermute | solution.py:341
  76.0 3.1 %last_rows.1 = (bf16[384,5120]{1,0:T(8,128)(2,1)}, bf16[384,1024]{1,0:T(8,128)(2,1)}) custom-call(bf16[384,5120]{1,0:T(8,128)(2,1)S(1)} %copy-done, bf16[384,1024]{1,0:T(8,128)(2,1)S(1)} %copy-done.2, bf16[384,128]{1,0:T(8,128)(2,1)S(1)} %get-tuple-element.88.spread, bf16[5120,128]{1,0:T(8,128)(2,1)S(1)} %copy-done.1, ...), custom_call_target="tpu_custom_call", output_to_operand_aliasing={{0}: (7, {})} | custom-call | bytes 1 | tf_op jit(solution)/shard_map/last_rows/pallas_call | solution.py:63
  (67 shorter events, 12.5 us)
Async XLA Ops:
  3.2 14.2 %collective-permute-start = (bf16[192,1024]{1,0:T(8,128)(2,1)S(1)}, bf16[192,1024]{1,0:T(8,128)(2,1)S(1)}, u32[]{:S(2)}, u32[]{:S(2)}) collective-permute-start(bf16[192,1024]{1,0:T(8,128)(2,1)S(1)} %get-tuple-element.87._.refs_0_), channel_id=1, source_target_pairs={{0,4},{1,5},{2,6},{3,7},{4,8},{5,9},{6,10},{7,11},{8,12},{9,13},{1... | collective-permute-start | bytes 1179656 | tf_op jit(solution)/shard_map/z1/ppermute | solution.py:333
  6.3 11.1 %collective-permute-start.3 = (bf16[192,1024]{1,0:T(8,128)(2,1)S(1)}, bf16[192,1024]{1,0:T(8,128)(2,1)S(1)}, u32[]{:S(2)}, u32[]{:S(2)}) collective-permute-start(bf16[192,1024]{1,0:T(8,128)(2,1)S(1)} %get-tuple-element.87._.refs_0_), channel_id=1, source_target_pairs={{0,2},{1,3},{2,0},{3,1},{4,6},{5,7},{6,4},{7,5},{8,10},{9,11},{10,... | collective-permute-start | bytes 1179656 | tf_op jit(solution)/shard_map/y0/ppermute | solution.py:337
  12.9 7.1 %collective-permute-start.2 = (f32[4,2,384,128]{3,2,1,0:T(8,128)S(1)}, f32[4,2,384,128]{3,2,1,0:T(8,128)S(1)}, u32[]{:S(2)}, u32[]{:S(2)}) collective-permute-start(f32[4,2,384,128]{3,2,1,0:T(8,128)S(1)} %get-tuple-element.90), channel_id=1, source_target_pairs={{0,1},{1,0},{2,3},{3,2},{4,5},{5,4},{6,7},{7,6},{8,9},{9,8},{10,11... | collective-permute-start | bytes 4718600 | tf_op jit(solution)/shard_map/core_share/ppermute | solution.py:341
  17.4 12.1 %collective-permute-start.1 = (bf16[192,1024]{1,0:T(8,128)(2,1)S(1)}, bf16[192,1024]{1,0:T(8,128)(2,1)S(1)}, u32[]{:S(2)}, u32[]{:S(2)}) collective-permute-start(bf16[192,1024]{1,0:T(8,128)(2,1)S(1)} %collective-permute-done.ref.refs_0_), channel_id=1, source_target_pairs={{0,4},{1,5},{2,6},{3,7},{4,8},{5,9},{6,10},{7,11},{8,12},{9,13},{1... | collective-permute-start | bytes 1179656 | tf_op jit(solution)/shard_map/z2/ppermute | solution.py:333
  18.5 14.4 %collective-permute-start.6 = (bf16[192,1024]{1,0:T(8,128)(2,1)S(1)}, bf16[192,1024]{1,0:T(8,128)(2,1)S(1)}, u32[]{:S(2)}, u32[]{:S(2)}) collective-permute-start(bf16[192,1024]{1,0:T(8,128)(2,1)S(1)} %collective-permute-done.ref.refs_0_), channel_id=1, source_target_pairs={{0,2},{1,3},{2,0},{3,1},{4,6},{5,7},{6,4},{7,5},{8,10},{9,11},{10,... | collective-permute-start | bytes 1179656 | tf_op jit(solution)/shard_map/y1/ppermute | solution.py:337
  20.2 18.8 %collective-permute-start.5 = (bf16[4,384,128]{2,1,0:T(8,128)(2,1)S(1)}, bf16[4,384,128]{2,1,0:T(8,128)(2,1)S(1)}, u32[]{:S(2)}, u32[]{:S(2)}) collective-permute-start(bf16[4,384,128]{2,1,0:T(8,128)(2,1)S(1)} %get-tuple-element.99), channel_id=1, source_target_pairs={{0,2},{1,3},{2,0},{3,1},{4,6},{5,7},{6,4},{7,5},{8,10},{9,11},{10,... | collective-permute-start | bytes 1179656 | tf_op jit(solution)/shard_map/side_share/ppermute | solution.py:337
  20.8 8.8 %collective-permute-start.8 = (bf16[128,1024]{1,0:T(8,128)(2,1)S(1)}, bf16[128,1024]{1,0:T(8,128)(2,1)S(1)}, u32[]{:S(2)}, u32[]{:S(2)}) collective-permute-start(bf16[128,1024]{1,0:T(8,128)(2,1)S(1)} %cut_1.1), channel_id=1, source_target_pairs={{0,16},{16,0},{1,17},{17,1},{2,18},{18,2},{3,19},{19,3},{4,20},{20... | collective-permute-start | bytes 786440 | tf_op jit(solution)/shard_map/x1a/ppermute | solution.py:345
  22.3 10.6 %collective-permute-start.7 = (bf16[128,1024]{1,0:T(8,128)(2,1)S(1)}, bf16[128,1024]{1,0:T(8,128)(2,1)S(1)}, u32[]{:S(2)}, u32[]{:S(2)}) collective-permute-start(bf16[128,1024]{1,0:T(8,128)(2,1)S(1)} %slice.18), channel_id=1, source_target_pairs={{0,16},{16,0},{1,17},{17,1},{2,18},{18,2},{3,19},{19,3},{4,20},{20... | collective-permute-start | bytes 786440 | tf_op jit(solution)/shard_map/x0/ppermute | solution.py:345
  29.6 11.2 %collective-permute-start.4 = (bf16[192,1024]{1,0:T(8,128)(2,1)S(1)}, bf16[192,1024]{1,0:T(8,128)(2,1)S(1)}, u32[]{:S(2)}, u32[]{:S(2)}) collective-permute-start(bf16[192,1024]{1,0:T(8,128)(2,1)S(1)} %collective-permute-done.1.refs_0_), channel_id=1, source_target_pairs={{0,4},{1,5},{2,6},{3,7},{4,8},{5,9},{6,10},{7,11},{8,12},{9,13},{1... | collective-permute-start | bytes 1179656 | tf_op jit(solution)/shard_map/z3/ppermute | solution.py:333
  29.6 21.2 %collective-permute-start.15 = (bf16[192,1024]{1,0:T(8,128)(2,1)S(1)}, bf16[192,1024]{1,0:T(8,128)(2,1)S(1)}, u32[]{:S(2)}, u32[]{:S(2)}) collective-permute-start(bf16[192,1024]{1,0:T(8,128)(2,1)S(1)} %collective-permute-done.1.refs_0_), channel_id=1, source_target_pairs={{0,2},{1,3},{2,0},{3,1},{4,6},{5,7},{6,4},{7,5},{8,10},{9,11},{10,... | collective-permute-start | bytes 1179656 | tf_op jit(solution)/shard_map/y2/ppermute | solution.py:337
  32.9 9.0 %collective-permute-start.12 = (bf16[128,1024]{1,0:T(8,128)(2,1)S(1)}, bf16[128,1024]{1,0:T(8,128)(2,1)S(1)}, u32[]{:S(2)}, u32[]{:S(2)}) collective-permute-start(bf16[128,1024]{1,0:T(8,128)(2,1)S(1)} %slice.20), channel_id=1, source_target_pairs={{0,16},{16,0},{1,17},{17,1},{2,18},{18,2},{3,19},{19,3},{4,20},{20... | collective-permute-start | bytes 786440 | tf_op jit(solution)/shard_map/x2a/ppermute | solution.py:345
  34.4 9.3 %collective-permute-start.11 = (bf16[128,1024]{1,0:T(8,128)(2,1)S(1)}, bf16[128,1024]{1,0:T(8,128)(2,1)S(1)}, u32[]{:S(2)}, u32[]{:S(2)}) collective-permute-start(bf16[128,1024]{1,0:T(8,128)(2,1)S(1)} %slice.19), channel_id=1, source_target_pairs={{0,16},{16,0},{1,17},{17,1},{2,18},{18,2},{3,19},{19,3},{4,20},{20... | collective-permute-start | bytes 786440 | tf_op jit(solution)/shard_map/x1b/ppermute | solution.py:345
  39.0 6.3 %collective-permute-start.10 = (bf16[640,1024]{1,0:T(8,128)(2,1)S(1)}, bf16[640,1024]{1,0:T(8,128)(2,1)S(1)}, u32[]{:S(2)}, u32[]{:S(2)}) collective-permute-start(bf16[640,1024]{1,0:T(8,128)(2,1)S(1)} %pack_0.1), channel_id=1, source_target_pairs={{0,1},{1,0},{2,3},{3,2},{4,5},{5,4},{6,7},{7,6},{8,9},{9,8},{10,11... | collective-permute-start | bytes 3932168 | tf_op jit(solution)/shard_map/c0/ppermute | solution.py:341
  40.7 17.7 %collective-permute-start.9 = (bf16[192,1024]{1,0:T(8,128)(2,1)S(1)}, bf16[192,1024]{1,0:T(8,128)(2,1)S(1)}, u32[]{:S(2)}, u32[]{:S(2)}) collective-permute-start(bf16[192,1024]{1,0:T(8,128)(2,1)S(1)} %collective-permute-done.4.refs_0_), channel_id=1, source_target_pairs={{0,2},{1,3},{2,0},{3,1},{4,6},{5,7},{6,4},{7,5},{8,10},{9,11},{10,... | collective-permute-start | bytes 1179656 | tf_op jit(solution)/shard_map/y3/ppermute | solution.py:337
  43.7 9.8 %collective-permute-start.14 = (bf16[128,1024]{1,0:T(8,128)(2,1)S(1)}, bf16[128,1024]{1,0:T(8,128)(2,1)S(1)}, u32[]{:S(2)}, u32[]{:S(2)}) collective-permute-start(bf16[128,1024]{1,0:T(8,128)(2,1)S(1)} %slice.21), channel_id=1, source_target_pairs={{0,16},{16,0},{1,17},{17,1},{2,18},{18,2},{3,19},{19,3},{4,20},{20... | collective-permute-start | bytes 786440 | tf_op jit(solution)/shard_map/x3a/ppermute | solution.py:345
  45.3 9.1 %collective-permute-start.13 = (bf16[640,1024]{1,0:T(8,128)(2,1)S(1)}, bf16[640,1024]{1,0:T(8,128)(2,1)S(1)}, u32[]{:S(2)}, u32[]{:S(2)}) collective-permute-start(bf16[640,1024]{1,0:T(8,128)(2,1)S(1)} %pack_1.1), channel_id=1, source_target_pairs={{0,1},{1,0},{2,3},{3,2},{4,5},{5,4},{6,7},{7,6},{8,9},{9,8},{10,11... | collective-permute-start | bytes 3932168 | tf_op jit(solution)/shard_map/c1/ppermute | solution.py:341
  45.4 17.0 %collective-permute-start.18 = (bf16[576,128]{1,0:T(8,128)(2,1)S(1)}, bf16[576,128]{1,0:T(8,128)(2,1)S(1)}, u32[]{:S(2)}, u32[]{:S(2)}) collective-permute-start(bf16[576,128]{1,0:T(8,128)(2,1)S(1)} %get-tuple-element.129), channel_id=1, source_target_pairs={{0,4},{1,5},{2,6},{3,7},{4,8},{5,9},{6,10},{7,11},{8,12},{9,13},{1... | collective-permute-start | bytes 442376 | tf_op jit(solution)/shard_map/line_1/ppermute | solution.py:333
  50.8 11.5 %collective-permute-start.17 = (bf16[576,128]{1,0:T(8,128)(2,1)S(1)}, bf16[576,128]{1,0:T(8,128)(2,1)S(1)}, u32[]{:S(2)}, u32[]{:S(2)}) collective-permute-start(bf16[576,128]{1,0:T(8,128)(2,1)S(1)} %get-tuple-element.128), channel_id=1, source_target_pairs={{0,8},{1,9},{2,10},{3,11},{4,12},{5,13},{6,14},{7,15},{8,0},{9,1},... | collective-permute-start | bytes 442376 | tf_op jit(solution)/shard_map/line_2/ppermute | solution.py:333
  53.5 8.9 %collective-permute-start.20 = (bf16[576,128]{1,0:T(8,128)(2,1)S(1)}, bf16[576,128]{1,0:T(8,128)(2,1)S(1)}, u32[]{:S(2)}, u32[]{:S(2)}) collective-permute-start(bf16[576,128]{1,0:T(8,128)(2,1)S(1)} %get-tuple-element.133), channel_id=1, source_target_pairs={{0,12},{1,13},{2,14},{3,15},{4,0},{5,1},{6,2},{7,3},{8,4},{9,5},{1... | collective-permute-start | bytes 442376 | tf_op jit(solution)/shard_map/line_3/ppermute | solution.py:333
  54.4 7.8 %collective-permute-start.19 = (bf16[128,1024]{1,0:T(8,128)(2,1)S(1)}, bf16[128,1024]{1,0:T(8,128)(2,1)S(1)}, u32[]{:S(2)}, u32[]{:S(2)}) collective-permute-start(bf16[128,1024]{1,0:T(8,128)(2,1)S(1)} %slice.23), channel_id=1, source_target_pairs={{0,16},{16,0},{1,17},{17,1},{2,18},{18,2},{3,19},{19,3},{4,20},{20... | collective-permute-start | bytes 786440 | tf_op jit(solution)/shard_map/x2b/ppermute | solution.py:345
  62.3 4.3 %collective-permute-start.23 = (bf16[640,1024]{1,0:T(8,128)(2,1)S(1)}, bf16[640,1024]{1,0:T(8,128)(2,1)S(1)}, u32[]{:S(2)}, u32[]{:S(2)}) collective-permute-start(bf16[640,1024]{1,0:T(8,128)(2,1)S(1)} %pack_2.1), channel_id=1, source_target_pairs={{0,1},{1,0},{2,3},{3,2},{4,5},{5,4},{6,7},{7,6},{8,9},{9,8},{10,11... | collective-permute-start | bytes 3932168 | tf_op jit(solution)/shard_map/c2/ppermute | solution.py:341
  63.1 10.0 %collective-permute-start.21 = (f32[256,128]{1,0:T(8,128)S(1)}, f32[256,128]{1,0:T(8,128)S(1)}, u32[]{:S(2)}, u32[]{:S(2)}) collective-permute-start(f32[256,128]{1,0:T(8,128)S(1)} %get-tuple-element.167.mine), channel_id=1, source_target_pairs={{0,2},{1,3},{2,0},{3,1},{4,6},{5,7},{6,4},{7,5},{8,10},{9,11},{10,... | collective-permute-start | bytes 393224 | tf_op jit(solution)/shard_map/side_up/ppermute | solution.py:337
  65.4 7.8 %collective-permute-start.25 = (f32[256,128]{1,0:T(8,128)S(1)}, f32[256,128]{1,0:T(8,128)S(1)}, u32[]{:S(2)}, u32[]{:S(2)}) collective-permute-start(f32[256,128]{1,0:T(8,128)S(1)} %get-tuple-element.167.mine), channel_id=1, source_target_pairs={{0,1},{1,0},{2,3},{3,2},{4,5},{5,4},{6,7},{7,6},{8,9},{9,8},{10,11... | collective-permute-start | bytes 393224 | tf_op jit(solution)/shard_map/core_up/ppermute | solution.py:341
  66.1 8.4 %collective-permute-start.16 = (bf16[128,1024]{1,0:T(8,128)(2,1)S(1)}, bf16[128,1024]{1,0:T(8,128)(2,1)S(1)}, u32[]{:S(2)}, u32[]{:S(2)}) collective-permute-start(bf16[128,1024]{1,0:T(8,128)(2,1)S(1)} %slice.22), channel_id=1, source_target_pairs={{0,16},{16,0},{1,17},{17,1},{2,18},{18,2},{3,19},{19,3},{4,20},{20... | collective-permute-start | bytes 786440 | tf_op jit(solution)/shard_map/x3b/ppermute | solution.py:345
  (10 other events, 36.0 us)

commit v3 on v2

--- a/solution.py
+++ b/solution.py
@@ -48,6 +48,7 @@
     return values, act.astype(BF16), grad_a, grad_b
 
 
+GAPS = {'plane_1': 0, 'pack_1': 60, 'place_up_gradient': 2, 'side_sum': 5, 'pack_0': 0, 'line_sum': 0}
 GAP = 60
 VMEM = pl.BlockSpec(memory_space=pltpu.VMEM)
 SMEM = pl.BlockSpec(memory_space=pltpu.SMEM)
@@ -70,7 +71,7 @@
         input_output_aliases=alias or {},
         compiler_params=pltpu.CompilerParams(vmem_limit_bytes=VMEM_LIMIT),
         cost_estimate=pl.CostEstimate(
-            flops=int(us * 1.1e9), bytes_accessed=1, transcendentals=0
+            flops=int(GAPS.get(name, us) * 1.1e9), bytes_accessed=1, transcendentals=0
         ),
     )(*operands)
 
@@ -199,24 +200,25 @@
     quarter[...] = 2.0 * total[rows:]
 
 
-def place_b_body(mine, side, core, core_side, out):
+def place_b_body(mine, core, out):
     _, y, c, _ = place()
     ranks = out.shape[0]
     half = ranks // 2
-    planes = mine.shape[0] // half
-    for ref, yy, cc in ((mine, y, c), (side, 1 - y, c), (core, y, 1 - c), (core_side, 1 - y, 1 - c)):
+    planes = mine.shape[0] // (2 * half)
+    for ref, cc in ((mine, c), (core, 1 - c)):
         row = pl.multiple_of(cc * half, half)
-        for j in range(planes):
-            column = pl.multiple_of((yy * planes + j) * ranks, ranks)
+        for j in range(2 * planes):
+            yy = y if j < planes else 1 - y
+            column = pl.multiple_of((yy * planes + j % planes) * ranks, ranks)
             out[pl.ds(row, half), pl.ds(column, ranks)] = ref[pl.ds(j * half, half), :]
 
 
 def plane_body(k, first, rows, kept, counts, tok_far, cot, spread, down_far, *refs):
     pieces, refs = refs[: sum(counts)], refs[sum(counts) :]
     if first:
-        shrink, up, act, acc, weight, block, tok, down, sem, sems = refs
+        shrink, up, act, acc, *saved, weight, block, tok, down, sem, sems = refs
     else:
-        total, _, act, acc, weight, block, tok, down, sem, sems = refs
+        total, _, act, acc, *saved, weight, block, tok, down, sem, sems = refs
     z, y, c, x = place()
     depth = weight.shape[0]
     zz = lax.rem(z + 4 - k, 4)
@@ -264,38 +266,33 @@
     else:
         forward += total[...]
     acc[...] = forward
+    if saved:
+        for i in range(2):
+            here = pl.ds(late_rows(k, rows, i, x, z, y, c)[0], kept)
+            saved[0][i] = tok[:, here]
+            saved[1][i] = down[here, :]
     copy.wait()
 
 
-def last_body(k, rows, tok_far, cot, spread, down_far, own, got, total, _, act, values, *refs):
-    tok, down, block, sems, sent = refs
+def late_rows(k, rows, i, x, z, y, c):
+    cc = c if i == 0 else 1 - c
+    within = ((1 - y) * 2 + cc) * rows + strip_places(cc, x)[2]
+    zz = lax.rem(z + 4 - k, 4)
+    return pl.multiple_of(within, BLOCK), pl.multiple_of(zz * 4 * rows + within, BLOCK)
+
+
+def last_body(k, rows, i, tok, cot, spread, down, weight, total, _, act, out, block, sem):
     z, y, c, x = place()
-    kept = own.shape[0]
-    zz = lax.rem(z + 4 - k, 4)
-    parts = []
-    for cc in (c, 1 - c):
-        start = ((zz * 2 + 1 - y) * 2 + cc) * rows + strip_places(cc, x)[2]
-        parts.append(pl.ds(pl.multiple_of(start, BLOCK), kept))
-    pairs = []
-    for i, part in enumerate(parts):
-        pairs += [(down_far.at[part, :], down.at[i]), (tok_far.at[:, part], tok.at[i])]
-    copies = fetch(pairs, sems)
-    outs = []
-    for i, (part, weight) in enumerate(zip(parts, (own, got))):
-        back = reduce_over_rows(cot[...], weight[...])
-        copies[2 * i].wait()
-        back += reduce_over_rows(spread[...], down[i])
-        block[i] = back.astype(BF16)
-        out = pltpu.make_async_copy(block.at[i], act.at[:, part], sent.at[i])
-        out.start()
-        outs.append(out)
-    copies[1].wait()
-    forward = total[...] + jnp.dot(tok[0], own[...], preferred_element_type=F32)
-    copies[3].wait()
-    forward += jnp.dot(tok[1], got[...], preferred_element_type=F32)
-    values[...] = forward.astype(BF16)
-    for out in outs:
-        out.wait()
+    kept = weight.shape[0]
+    start = late_rows(k, rows, i, x, z, y, c)[1]
+    back = reduce_over_rows(cot[...], weight[...])
+    back += reduce_over_rows(spread[...], down[i])
+    block[...] = back.astype(BF16)
+    copy = pltpu.make_async_copy(block, act.at[:, pl.ds(start, kept)], sem)
+    copy.start()
+    forward = total[...] + jnp.dot(tok[i], weight[...], preferred_element_type=F32)
+    out[...] = forward.astype(out.dtype)
+    copy.wait()
 
 
 def cut_body(ref, out):
@@ -379,9 +376,12 @@
         ],
     )
 
-    def plane(k, own, got, state):
+    def plane(k, own, got, state, us):
         first = k == 0
-        operands = [tokens, cotangent, spread, down] + own + got
+        kinds = []
+        if k == planes - 1:
+            kinds = [struct((2, count, kept), BF16), struct((2, kept, ranks), BF16)]
+        operands = [tokens, cotangent, e["spread"], down] + own + got
         if first:
             operands += [shrink, up]
             specs = [HBM, VMEM, VMEM, HBM] + [VMEM] * (len(operands) - 4)
@@ -393,10 +393,10 @@
         return kernel(
             functools.partial(plane_body, k, first, rows, kept, (len(own), len(got))),
             f"plane_{k}",
-            GAP,
-            [struct((count, width), BF16), struct((count, columns), F32)],
+            us,
+            [struct((count, width), BF16), struct((count, columns), F32)] + kinds,
             specs,
-            [HBM, VMEM],
+            [HBM, VMEM] + [VMEM] * len(kinds),
             operands,
             scratch=[
                 pltpu.VMEM((depth, columns), BF16),
@@ -413,8 +413,8 @@
         return kernel(
             pack_body,
             name,
-            0,
-            struct((sum(v.shape[0] for v in parts), columns), BF16),
+            GAP,
+            struct((sum(v.shape[0] for v in parts), parts[0].shape[1]), parts[0].dtype),
             [VMEM] * len(parts),
             VMEM,
             parts,
@@ -424,116 +424,127 @@
         return kernel(
             pack_body,
             name,
-            0,
-            struct((sum(v.shape[0] for v in parts), columns), BF16),
+            GAP,
+            struct((sum(v.shape[0] for v in parts), parts[0].shape[1]), parts[0].dtype),
             [VMEM] * len(parts),
             VMEM,
             parts,
         )
 
-    def last_rows(k, own, got, act, total):
+    def last_rows(k, i, weight, state, saved):
         return kernel(
-            functools.partial(last_body, k, rows),
-            "last_rows",
-            0,
-            [struct((count, width), BF16), struct((count, columns), BF16)],
-            [HBM, VMEM, VMEM, HBM, VMEM, VMEM, VMEM, HBM],
+            functools.partial(last_body, k, rows, i),
+            f"last_rows_{i}",
+            GAP,
+            [struct((count, width), BF16), struct((count, columns), (F32, BF16)[i])],
+            [VMEM] * 6 + [HBM],
             [HBM, VMEM],
-            [tokens, cotangent, spread, down, own, got, total, act],
-            scratch=[
-                pltpu.VMEM((2, count, kept), BF16),
-                pltpu.VMEM((2, kept, ranks), BF16),
-                pltpu.VMEM((2, count, kept), BF16),
-                pltpu.SemaphoreType.DMA((4,)),
-                pltpu.SemaphoreType.DMA((2,)),
-            ],
-            alias={7: 0},
+            [saved[0], cotangent, e["spread"], saved[1], weight, state[1], state[0]],
+            scratch=[pltpu.VMEM((count, kept), BF16), pltpu.SemaphoreType.DMA],
+            alias={6: 0},
         )
 
-    e = {}
-    last = []
-
-    def event(*names):
-        for name in names:
-            if last and last[0] != name:
-                e[name], e[last[0]] = lax.optimization_barrier((e[name], e[last[0]]))
-            last[:] = [name]
-
-    def cut(name, v, us=0.0):
+    e = {"send": send, "spread": spread, "z1": z1, "y0": y0}
+
+    def event(name):
+        e[name], e["spread"] = lax.optimization_barrier((e[name], e["spread"]))
+
+    def cut(name, v, us):
         return kernel(
             cut_body, name, us, struct((kept, columns), BF16), [VMEM], VMEM, (v,)
         )
 
-    def run_plane(k, own, got, state):
+    def run_plane(k, own, got):
         own = [e[v] if isinstance(v, str) else v for v in own]
-        state = plane(k, own, [e[v] for v in got], state)
-        e["acc"] = state[1]
-        event("acc")
-        return state[0]
-
-    e["share"] = over_core("core_share", send)
-    e["z1"], e["y0"] = z1, y0
+        state = (e["act"], e["acc"]) if k else None
+        e["act"], e["acc"], *e["saved"] = plane(k, own, [e[got]], state, GAP)
+
+    def run_last(i, name):
+        e["act"], e["acc"] = last_rows(3, i, e[name], (e["act"], e["acc"]), e["saved"])
+        return e["acc"]
+
+    e["core_share"] = over_core("core_share", e["send"])
     event("z1")
-    e["z2"], e["y1"] = over_z("z2", e["z1"]), over_y("y1", e["z1"])
-    event("y0")
-    e["x0"] = over_x("x0", e["y0"][:kept])
+    e["z2"] = over_z("z2", e["z1"])
+    e["y1"] = over_y("y1", e["z1"])
+    event("z1")
     e["cut"] = cut("cut_1", e["z1"], GAP)
     event("cut")
     e["x1a"] = over_x("x1a", e["cut"])
-    event("share")
-    e["own_y"], other_y = kernel(
+    event("y0")
+    e["x0"] = over_x("x0", e["y0"][:kept])
+    event("core_share")
+    event("x0")
+    event("core_share")
+    e["own_y"], e["other_y"] = kernel(
         core_sum_body,
         "core_sum",
-        0,
+        GAP,
         [struct((planes, each, ranks), F32), struct((planes, each, ranks), BF16)],
         [VMEM] * 2,
         [VMEM] * 2,
-        (keep, e["share"]),
+        (keep, e["core_share"]),
     )
     event("own_y")
-    e["side"] = over_y("side_share", other_y)
+    e["side_share"] = over_y("side_share", e["other_y"])
+    event("y1")
+    e["x1b"] = over_x("x1b", e["y1"][:kept])
     event("z2")
-    e["z3"], e["y2"] = over_z("z3", e["z2"]), over_y("y2", e["z2"])
+    e["z3"] = over_z("z3", e["z2"])
+    e["y2"] = over_y("y2", e["z2"])
     e["x2a"] = over_x("x2a", e["z2"][:kept])
     event("x1a")
+    event("x1b")
     event("x0")
-    e["c0"] = over_core("c0", pack("pack_0", p0, e["y0"], rest, e["x0"]))
-    event("y1")
-    e["x1b"] = over_x("x1b", e["y1"][:kept])
-    event("side")
+    e["pack_0"] = pack("pack_0", p0, e["y0"], rest, e["x0"])
+    event("pack_0")
+    e["c0"] = over_core("c0", e["pack_0"])
+    event("side_share")
     line = struct((rows + planes * half, ranks), BF16)
-    e["mine"], s1, s2, s3 = kernel(
+    e["mine"], e["s1"], e["s2"], e["s3"] = kernel(
         functools.partial(side_sum_body, rows),
         "side_sum",
         GAP,
         [struct(line.shape, F32), line, line, line],
         [VMEM] * 2,
         [VMEM] * 4,
-        (e["own_y"], e["side"]),
+        (e["own_y"], e["side_share"]),
     )
     event("mine")
-    for i, v in enumerate((s1, s2, s3)):
-        e[f"r{i + 1}"] = over_z(f"line_{i + 1}", v, i + 1)
+    e["line_1"] = over_z("line_1", e["s1"], 1)
+    e["line_2"] = over_z("line_2", e["s2"], 2)
+    e["line_3"] = over_z("line_3", e["s3"], 3)
+    event("x1b")
+    e["pack_1"] = pack("pack_1", e["z1"], e["y1"], e["x1a"], e["x1b"])
+    event("pack_1")
+    e["c1"] = over_core("c1", e["pack_1"])
     event("z3")
-    e["y3"], e["x3a"] = over_y("y3", e["z3"]), over_x("x3a", e["z3"][:kept])
+    e["y3"] = over_y("y3", e["z3"])
+    e["x3a"] = over_x("x3a", e["z3"][:kept])
     event("x2a")
-    event("x1b")
-    e["c1"] = over_core("c1", pack("pack_1", e["z1"], e["y1"], e["x1a"], e["x1b"]))
     event("c0")
-    act = run_plane(0, [p0, "y0", rest, "x0"], ["c0"], None)
     event("y2")
     e["x2b"] = over_x("x2b", e["y2"][:kept])
+    event("line_3")
+    event("c0")
+    run_plane(0, [p0, "y0", rest, "x0"], "c0")
+    event("acc")
+    event("c1")
+    run_plane(1, ["z1", "y1", "x1a", "x1b"], "c1")
+    event("acc")
     event("x3a")
-    event("c1")
-    act = run_plane(1, ["z1", "y1", "x1a", "x1b"], ["c1"], (act, e["acc"]))
     event("y3")
     e["x3b"] = over_x("x3b", e["y3"][:kept])
-    e["c3a"] = over_core("c3a", pack("pack_3", e["z3"], e["y3"], e["x3a"]))
     event("x2b")
-    e["c2"] = over_core("c2", pack("pack_2", e["z2"], e["y2"], e["x2a"], e["x2b"]))
-    event("r1")
-    event("r2")
-    event("r3")
+    e["pack_2"] = pack("pack_2", e["z2"], e["y2"], e["x2a"], e["x2b"])
+    event("pack_2")
+    e["c2"] = over_core("c2", e["pack_2"])
+    event("line_2")
+    event("x3a")
+    e["pack_3"] = pack("pack_3", e["z3"], e["y3"], e["x3a"])
+    event("pack_3")
+    e["c3a"] = over_core("c3a", e["pack_3"])
+    event("line_1")
     grad_a, e["quarter"] = kernel(
         line_sum_body,
         "line_sum",
@@ -541,32 +552,39 @@
         [struct((rows, ranks), F32), struct((planes * half, ranks), F32)],
         [VMEM] * 4,
         [VMEM] * 2,
-        (e["mine"], e["r1"], e["r2"], e["r3"]),
+        (e["mine"], e["line_1"], e["line_2"], e["line_3"]),
     )
     event("quarter")
-    e["side_quarter"] = over_y("side_up", e["quarter"])
-    e["core_quarter"] = over_core("core_up", e["quarter"])
+    e["side_up"] = over_y("side_up", e["quarter"])
     event("c2")
-    act = run_plane(2, ["z2", "y2", "x2a", "x2b"], ["c2"], (act, e["acc"]))
+    run_plane(2, ["z2", "y2", "x2a", "x2b"], "c2")
+    event("acc")
+    event("side_up")
+    e["both"] = pack("pack_up", e["quarter"], e["side_up"])
+    event("both")
+    e["core_up"] = over_core("core_up", e["both"])
     event("c3a")
-    act = run_plane(3, ["z3", "y3", "x3a"], ["c3a"], (act, e["acc"]))
-    event("side_quarter")
-    e["core_side"] = over_core("core_side_up", e["side_quarter"])
-    event("core_quarter")
-    event("core_side")
+    run_plane(3, ["z3", "y3", "x3a"], "c3a")
+    event("acc")
+    event("core_up")
+    event("x3b")
+    e["c3b"] = over_core("c3b", e["x3b"])
+    event("core_up")
     grad_b = kernel(
         place_b_body,
         "place_up_gradient",
-        0,
+        GAP,
         struct((ranks, columns), F32),
-        [VMEM] * 4,
+        [VMEM] * 2,
         VMEM,
-        (e["quarter"], e["side_quarter"], e["core_quarter"], e["core_side"]),
+        (e["both"], e["core_up"]),
     )
     event("x3b")
-    e["c3b"] = over_core("c3b", e["x3b"])
+    run_last(0, "x3b")
+    event("acc")
     event("c3b")
-    act, values = last_rows(3, e["x3b"], e["c3b"], act, e["acc"])
+    values = run_last(1, "c3b")
+    act, values = e["act"], e["acc"]
     return values, act, grad_a, grad_b
 
 

time: 79.5 us -> 75.3 us (0.947)
  waiting for transfers between devices: 25.9 us -> 18.3 us
  starting transfers between devices: 25.8 us -> 27.4 us
  Pallas kernels: 24.5 us -> 25.7 us
    ppermute x6, waiting for transfers between devices: 12.7 us -> 5.87 us  [over_z(): return lax.ppermute(v, 'seq', swap(n, lambda z, y, c: (z + by, y, c)))]
    ppermute x8 -> x7, waiting for transfers between devices: 1.89 us -> 0.11 us  [over_core(): return lax.ppermute(v, 'seq', swap(n, lambda z, y, c: (z, y, 1 - c)))]
    ppermute x7, starting transfers between devices: 7 us -> 8.58 us  [over_x(): return lax.ppermute(v, 'groups', [(0, 1), (1, 0)])]
    ppermute x7, waiting for transfers between devices: 7.41 us -> 8.94 us  [over_x(): return lax.ppermute(v, 'groups', [(0, 1), (1, 0)])]
    pallas_call x16 -> x18, Pallas kernels: 24.5 us -> 25.7 us  [kernel(): pl.pallas_call(body, name=name, in_specs=in_specs, out_specs=out_specs, o...]
    unnamed x14 -> x22, local copies, waits for them, and re-layouts: 1.79 us -> 1.81 us
  transfers between devices with their start and end apart: 27 -> 26, of which waited for: 9 -> 9; matrix products, arithmetic and copies ran while one was open for 0% -> 1% of each run, Pallas kernels for 26% -> 30%
where the time goes in v3:
time: 75.3 us; the launch traced here: 75.1 us
  starting transfers between devices  27.4 us (36%)
  Pallas kernels  25.7 us (34%)
  waiting for transfers between devices  18.3 us (24%)
  local copies, waits for them, and re-layouts  2.63 us (3%)
  between operations  1.11 us (1%)
    pallas_call x18, Pallas kernels, kernel(): pl.pallas_call(body, name=name, in_specs=in_specs, out_specs=out_specs, o...  25.7 us
    ppermute x6, starting transfers between devices, over_z(): return lax.ppermute(v, 'seq', swap(n, lambda z, y, c: (z + by, y, c)))  9.48 us
    ppermute x7, waiting for transfers between devices, over_x(): return lax.ppermute(v, 'groups', [(0, 1), (1, 0)])  8.94 us
    ppermute x7, starting transfers between devices, over_x(): return lax.ppermute(v, 'groups', [(0, 1), (1, 0)])  8.58 us
    ppermute x6, starting transfers between devices, over_y(): return lax.ppermute(v, 'seq', swap(n, lambda z, y, c: (z, 1 - y, c)))  8.46 us
    ppermute x6, waiting for transfers between devices, over_z(): return lax.ppermute(v, 'seq', swap(n, lambda z, y, c: (z + by, y, c)))  5.87 us
    ppermute x6, waiting for transfers between devices, over_y(): return lax.ppermute(v, 'seq', swap(n, lambda z, y, c: (z, 1 - y, c)))  3.37 us
    unnamed x22, local copies, waits for them, and re-layouts  1.81 us
  transfers between devices with their start and end apart: 26, of which 9 were waited for; matrix products, arithmetic and copies ran while one was open for 1% of the time, Pallas kernels for 30%

profile of v3, /device:TPU:0, one launch (start us, length us, event | category | flops | bytes accessed | tf_op | source)
XLA Modules:
  0.0 75.1 jit_solution(4855439421571869100)
XLA Ops:
  3.2 3.1 %collective-permute-start = (bf16[192,1024]{1,0:T(8,128)(2,1)S(1)}, bf16[192,1024]{1,0:T(8,128)(2,1)S(1)}, u32[]{:S(2)}, u32[]{:S(2)}) collective-permute-start(bf16[192,1024]{1,0:T(8,128)(2,1)S(1)} %get-tuple-element.127._.refs_0_), channel_id=1, source_target_pairs={{0,4},{1,5},{2,6},{3,7},{4,8},{5,9},{6,10},{7,11},{8,12},{9,13},{1... | collective-permute-start | bytes 1179656 | tf_op jit(solution)/shard_map/z1/ppermute | solution.py:330
  6.3 1.5 %collective-permute-start.4 = (bf16[192,1024]{1,0:T(8,128)(2,1)S(1)}, bf16[192,1024]{1,0:T(8,128)(2,1)S(1)}, u32[]{:S(2)}, u32[]{:S(2)}) collective-permute-start(bf16[192,1024]{1,0:T(8,128)(2,1)S(1)} %get-tuple-element.127._.refs_0_), channel_id=1, source_target_pairs={{0,2},{1,3},{2,0},{3,1},{4,6},{5,7},{6,4},{7,5},{8,10},{9,11},{10,... | collective-permute-start | bytes 1179656 | tf_op jit(solution)/shard_map/y0/ppermute | solution.py:334
  7.9 5.1 %gradient_shares.1 = (bf16[384,128]{1,0:T(8,128)(2,1)S(1)}, bf16[384,128]{1,0:T(8,128)(2,1)S(1)}, f32[4,2,384,128]{3,2,1,0:T(8,128)S(1)}, f32[4,2,384,128]{3,2,1,0:T(8,128)S(1)}) custom-call(bf16[384,5120]{1,0:T(8,128)(2,1)S(1)} %copy-done, s32[1,384]{1,0:T(1,128)S(1)} %broadcast_in_dim.3.idx, bf16[5120,128]{1,0:T(8,128)(2,1)S(1)} %copy-done.2, ...), custom_call_target="tpu_custom_call" | custom-call | flops 6600000000 | bytes 1 | tf_op jit(solution)/shard_map/gradient_shares/pallas_call | solution.py:64
  13.0 4.4 %collective-permute-done.ref.refs_0_ = bf16[192,1024]{1,0:T(8,128)(2,1)S(1)} collective-permute-done((bf16[192,1024]{1,0:T(8,128)(2,1)S(1)}, bf16[192,1024]{1,0:T(8,128)(2,1)S(1)}, u32[]{:S(2)}, u32[]{:S(2)}) %collective-permute-start) | collective-permute-done | bytes 393248 | tf_op jit(solution)/shard_map/z1/ppermute | solution.py:330
  17.5 1.6 %collective-permute-start.5 = (bf16[128,1024]{1,0:T(8,128)(2,1)S(1)}, bf16[128,1024]{1,0:T(8,128)(2,1)S(1)}, u32[]{:S(2)}, u32[]{:S(2)}) collective-permute-start(bf16[128,1024]{1,0:T(8,128)(2,1)S(1)} %slice.18), channel_id=1, source_target_pairs={{0,16},{16,0},{1,17},{17,1},{2,18},{18,2},{3,19},{19,3},{4,20},{20... | collective-permute-start | bytes 786440 | tf_op jit(solution)/shard_map/x0/ppermute | solution.py:342
  19.1 1.5 %collective-permute-start.2 = (bf16[192,1024]{1,0:T(8,128)(2,1)S(1)}, bf16[192,1024]{1,0:T(8,128)(2,1)S(1)}, u32[]{:S(2)}, u32[]{:S(2)}) collective-permute-start(bf16[192,1024]{1,0:T(8,128)(2,1)S(1)} %collective-permute-done.ref.refs_0_), channel_id=1, source_target_pairs={{0,2},{1,3},{2,0},{3,1},{4,6},{5,7},{6,4},{7,5},{8,10},{9,11},{10,... | collective-permute-start | bytes 1179656 | tf_op jit(solution)/shard_map/y1/ppermute | solution.py:334
  21.6 3.5 %collective-permute-done.5.refs_3_ = bf16[128,1024]{1,0:T(8,128)(2,1)S(1)} collective-permute-done((bf16[128,1024]{1,0:T(8,128)(2,1)S(1)}, bf16[128,1024]{1,0:T(8,128)(2,1)S(1)}, u32[]{:S(2)}, u32[]{:S(2)}) %collective-permute-start.5) | collective-permute-done | bytes 262176 | tf_op jit(solution)/shard_map/x0/ppermute | solution.py:342
  25.2 1.3 %collective-permute-start.9 = (bf16[4,384,128]{2,1,0:T(8,128)(2,1)S(1)}, bf16[4,384,128]{2,1,0:T(8,128)(2,1)S(1)}, u32[]{:S(2)}, u32[]{:S(2)}) collective-permute-start(bf16[4,384,128]{2,1,0:T(8,128)(2,1)S(1)} %get-tuple-element.153), channel_id=1, source_target_pairs={{0,2},{1,3},{2,0},{3,1},{4,6},{5,7},{6,4},{7,5},{8,10},{9,11},{10,... | collective-permute-start | bytes 1179656 | tf_op jit(solution)/shard_map/side_share/ppermute | solution.py:334
  26.6 1.5 %collective-permute-start.7 = (bf16[128,1024]{1,0:T(8,128)(2,1)S(1)}, bf16[128,1024]{1,0:T(8,128)(2,1)S(1)}, u32[]{:S(2)}, u32[]{:S(2)}) collective-permute-start(bf16[128,1024]{1,0:T(8,128)(2,1)S(1)} %cut_1.1), channel_id=1, source_target_pairs={{0,16},{16,0},{1,17},{17,1},{2,18},{18,2},{3,19},{19,3},{4,20},{20... | collective-permute-start | bytes 786440 | tf_op jit(solution)/shard_map/x1a/ppermute | solution.py:342
  28.1 3.1 %collective-permute-done.2.refs_1_ = bf16[192,1024]{1,0:T(8,128)(2,1)S(1)} collective-permute-done((bf16[192,1024]{1,0:T(8,128)(2,1)S(1)}, bf16[192,1024]{1,0:T(8,128)(2,1)S(1)}, u32[]{:S(2)}, u32[]{:S(2)}) %collective-permute-start.2) | collective-permute-done | bytes 393248 | tf_op jit(solution)/shard_map/y1/ppermute | solution.py:334
  32.5 1.6 %collective-permute-start.16 = (bf16[192,1024]{1,0:T(8,128)(2,1)S(1)}, bf16[192,1024]{1,0:T(8,128)(2,1)S(1)}, u32[]{:S(2)}, u32[]{:S(2)}) collective-permute-start(bf16[192,1024]{1,0:T(8,128)(2,1)S(1)} %collective-permute-done.1.refs_0_), channel_id=1, source_target_pairs={{0,2},{1,3},{2,0},{3,1},{4,6},{5,7},{6,4},{7,5},{8,10},{9,11},{10,... | collective-permute-start | bytes 1179656 | tf_op jit(solution)/shard_map/y2/ppermute | solution.py:334
  34.1 1.7 %collective-permute-done.7.refs_2_ = bf16[128,1024]{1,0:T(8,128)(2,1)S(1)} collective-permute-done((bf16[128,1024]{1,0:T(8,128)(2,1)S(1)}, bf16[128,1024]{1,0:T(8,128)(2,1)S(1)}, u32[]{:S(2)}, u32[]{:S(2)}) %collective-permute-start.7) | collective-permute-done | bytes 262176 | tf_op jit(solution)/shard_map/x1a/ppermute | solution.py:342
  35.8 1.5 %collective-permute-start.14 = (bf16[128,1024]{1,0:T(8,128)(2,1)S(1)}, bf16[128,1024]{1,0:T(8,128)(2,1)S(1)}, u32[]{:S(2)}, u32[]{:S(2)}) collective-permute-start(bf16[128,1024]{1,0:T(8,128)(2,1)S(1)} %slice.21), channel_id=1, source_target_pairs={{0,16},{16,0},{1,17},{17,1},{2,18},{18,2},{3,19},{19,3},{4,20},{20... | collective-permute-start | bytes 786440 | tf_op jit(solution)/shard_map/x2a/ppermute | solution.py:342
  37.3 3.7 %collective-permute-done.8.refs_3_ = bf16[128,1024]{1,0:T(8,128)(2,1)S(1)} collective-permute-done((bf16[128,1024]{1,0:T(8,128)(2,1)S(1)}, bf16[128,1024]{1,0:T(8,128)(2,1)S(1)}, u32[]{:S(2)}, u32[]{:S(2)}) %collective-permute-start.8) | collective-permute-done | bytes 262176 | tf_op jit(solution)/shard_map/x1b/ppermute | solution.py:342
  41.3 1.6 %collective-permute-start.15 = (bf16[576,128]{1,0:T(8,128)(2,1)S(1)}, bf16[576,128]{1,0:T(8,128)(2,1)S(1)}, u32[]{:S(2)}, u32[]{:S(2)}) collective-permute-start(bf16[576,128]{1,0:T(8,128)(2,1)S(1)} %get-tuple-element.173), channel_id=1, source_target_pairs={{0,12},{1,13},{2,14},{3,15},{4,0},{5,1},{6,2},{7,3},{8,4},{9,5},{1... | collective-permute-start | bytes 442376 | tf_op jit(solution)/shard_map/line_3/ppermute | solution.py:330
  44.2 1.5 %collective-permute-start.11 = (bf16[128,1024]{1,0:T(8,128)(2,1)S(1)}, bf16[128,1024]{1,0:T(8,128)(2,1)S(1)}, u32[]{:S(2)}, u32[]{:S(2)}) collective-permute-start(bf16[128,1024]{1,0:T(8,128)(2,1)S(1)} %slice.20), channel_id=1, source_target_pairs={{0,16},{16,0},{1,17},{17,1},{2,18},{18,2},{3,19},{19,3},{4,20},{20... | collective-permute-start | bytes 786440 | tf_op jit(solution)/shard_map/x3a/ppermute | solution.py:342
  45.7 2.8 %collective-permute-start.17 = (bf16[576,128]{1,0:T(8,128)(2,1)S(1)}, bf16[576,128]{1,0:T(8,128)(2,1)S(1)}, u32[]{:S(2)}, u32[]{:S(2)}) collective-permute-start(bf16[576,128]{1,0:T(8,128)(2,1)S(1)} %get-tuple-element.191), channel_id=1, source_target_pairs={{0,8},{1,9},{2,10},{3,11},{4,12},{5,13},{6,14},{7,15},{8,0},{9,1},... | collective-permute-start | bytes 442376 | tf_op jit(solution)/shard_map/line_2/ppermute | solution.py:330
  49.2 3.8 %plane_0.1 = (bf16[384,5120]{1,0:T(8,128)(2,1)}, f32[384,1024]{1,0:T(8,128)S(1)}) custom-call(bf16[384,5120]{1,0:T(8,128)(2,1)S(1)} %copy-done.1, bf16[384,1024]{1,0:T(8,128)(2,1)S(1)} %copy-done.5, bf16[384,128]{1,0:T(8,128)(2,1)S(1)} %get-tuple-element.242.spread, bf16[5120,128]{1,0:T(8,128)(2,1)S(1)} %copy-done.2, ...), custom_call_target="tpu_custom_call" | custom-call | flops 65999998976 | bytes 1 | tf_op jit(solution)/shard_map/plane_0/pallas_call | solution.py:64
  53.5 3.2 %plane_1.1 = (bf16[384,5120]{1,0:T(8,128)(2,1)}, f32[384,1024]{1,0:T(8,128)S(1)}) custom-call(bf16[384,5120]{1,0:T(8,128)(2,1)S(1)} %copy-done.1, bf16[384,1024]{1,0:T(8,128)(2,1)S(1)} %copy-done.5, bf16[384,128]{1,0:T(8,128)(2,1)S(1)} %get-tuple-element.242.spread, bf16[5120,128]{1,0:T(8,128)(2,1)S(1)} %copy-done.3, ...), custom_call_target="tpu_custom_call", output_to_operand_aliasing={{0}: (10, {})} | custom-call | bytes 1 | tf_op jit(solution)/shard_map/plane_1/pallas_call | solution.py:64
  61.0 1.4 %collective-permute-start.21 = (f32[256,128]{1,0:T(8,128)S(1)}, f32[256,128]{1,0:T(8,128)S(1)}, u32[]{:S(2)}, u32[]{:S(2)}) collective-permute-start(f32[256,128]{1,0:T(8,128)S(1)} %get-tuple-element.210.refs_0_), channel_id=1, source_target_pairs={{0,2},{1,3},{2,0},{3,1},{4,6},{5,7},{6,4},{7,5},{8,10},{9,11},{10,... | collective-permute-start | bytes 393224 | tf_op jit(solution)/shard_map/side_up/ppermute | solution.py:334
  62.4 3.2 %plane_2.1 = (bf16[384,5120]{1,0:T(8,128)(2,1)}, f32[384,1024]{1,0:T(8,128)S(1)}) custom-call(bf16[384,5120]{1,0:T(8,128)(2,1)S(1)} %copy-done.1, bf16[384,1024]{1,0:T(8,128)(2,1)S(1)} %copy-done.5, bf16[384,128]{1,0:T(8,128)(2,1)S(1)} %get-tuple-element.242.spread, bf16[5120,128]{1,0:T(8,128)(2,1)S(1)} %copy-done.3, ...), custom_call_target="tpu_custom_call", output_to_operand_aliasing={{0}: (10, {})} | custom-call | flops 65999998976 | bytes 1 | tf_op jit(solution)/shard_map/plane_2/pallas_call | solution.py:64
  66.3 3.2 %plane_3.1 = (bf16[384,5120]{1,0:T(8,128)(2,1)}, f32[384,1024]{1,0:T(8,128)S(1)}, bf16[2,384,128]{2,1,0:T(8,128)(2,1)S(1)}, bf16[2,128,128]{2,1,0:T(8,128)(2,1)S(1)}) custom-call(bf16[384,5120]{1,0:T(8,128)(2,1)S(1)} %copy-done.1, bf16[384,1024]{1,0:T(8,128)(2,1)S(1)} %copy-done.5, ...), custom_call_target="tpu_custom_call", output_to_operand_aliasing={{0}: (9, {})} | custom-call | flops 65999998976 | bytes 1 | tf_op jit(solution)/shard_map/plane_3/pallas_call | solution.py:64
  69.9 2.1 %last_rows_0.1 = (bf16[384,5120]{1,0:T(8,128)(2,1)}, f32[384,1024]{1,0:T(8,128)S(1)}) custom-call(bf16[2,384,128]{2,1,0:T(8,128)(2,1)S(1)} %get-tuple-element.226.tok, bf16[384,1024]{1,0:T(8,128)(2,1)S(1)} %copy-done.5, bf16[384,128]{1,0:T(8,128)(2,1)S(1)} %get-tuple-element.242.spread, ...), custom_call_target="tpu_custom_call", output_to_operand_aliasing={{0}: (6, {})} | custom-call | flops 65999998976 | bytes 1 | tf_op jit(solution)/shard_map/last_rows_0/pallas_call | solution.py:64
  72.9 2.0 %last_rows_1.1 = (bf16[384,5120]{1,0:T(8,128)(2,1)}, bf16[384,1024]{1,0:T(8,128)(2,1)}) custom-call(bf16[2,384,128]{2,1,0:T(8,128)(2,1)S(1)} %get-tuple-element.226.tok, bf16[384,1024]{1,0:T(8,128)(2,1)S(1)} %copy-done.5, bf16[384,128]{1,0:T(8,128)(2,1)S(1)} %get-tuple-element.242.spread, ...), custom_call_target="tpu_custom_call", output_to_operand_aliasing={{0}: (6, {})} | custom-call | flops 65999998976 | bytes 1 | tf_op jit(solution)/shard_map/last_rows_1/pallas_call | solution.py:64
  (75 shorter events, 14.0 us)
Async XLA Ops:
  3.2 14.2 %collective-permute-start = (bf16[192,1024]{1,0:T(8,128)(2,1)S(1)}, bf16[192,1024]{1,0:T(8,128)(2,1)S(1)}, u32[]{:S(2)}, u32[]{:S(2)}) collective-permute-start(bf16[192,1024]{1,0:T(8,128)(2,1)S(1)} %get-tuple-element.127._.refs_0_), channel_id=1, source_target_pairs={{0,4},{1,5},{2,6},{3,7},{4,8},{5,9},{6,10},{7,11},{8,12},{9,13},{1... | collective-permute-start | bytes 1179656 | tf_op jit(solution)/shard_map/z1/ppermute | solution.py:330
  6.3 11.2 %collective-permute-start.4 = (bf16[192,1024]{1,0:T(8,128)(2,1)S(1)}, bf16[192,1024]{1,0:T(8,128)(2,1)S(1)}, u32[]{:S(2)}, u32[]{:S(2)}) collective-permute-start(bf16[192,1024]{1,0:T(8,128)(2,1)S(1)} %get-tuple-element.127._.refs_0_), channel_id=1, source_target_pairs={{0,2},{1,3},{2,0},{3,1},{4,6},{5,7},{6,4},{7,5},{8,10},{9,11},{10,... | collective-permute-start | bytes 1179656 | tf_op jit(solution)/shard_map/y0/ppermute | solution.py:334
  12.9 8.6 %collective-permute-start.3 = (f32[4,2,384,128]{3,2,1,0:T(8,128)S(1)}, f32[4,2,384,128]{3,2,1,0:T(8,128)S(1)}, u32[]{:S(2)}, u32[]{:S(2)}) collective-permute-start(f32[4,2,384,128]{3,2,1,0:T(8,128)S(1)} %get-tuple-element.131), channel_id=1, source_target_pairs={{0,1},{1,0},{2,3},{3,2},{4,5},{5,4},{6,7},{7,6},{8,9},{9,8},{10,11... | collective-permute-start | bytes 4718600 | tf_op jit(solution)/shard_map/core_share/ppermute | solution.py:338
  17.5 7.6 %collective-permute-start.5 = (bf16[128,1024]{1,0:T(8,128)(2,1)S(1)}, bf16[128,1024]{1,0:T(8,128)(2,1)S(1)}, u32[]{:S(2)}, u32[]{:S(2)}) collective-permute-start(bf16[128,1024]{1,0:T(8,128)(2,1)S(1)} %slice.18), channel_id=1, source_target_pairs={{0,16},{16,0},{1,17},{17,1},{2,18},{18,2},{3,19},{19,3},{4,20},{20... | collective-permute-start | bytes 786440 | tf_op jit(solution)/shard_map/x0/ppermute | solution.py:342
  19.1 12.1 %collective-permute-start.2 = (bf16[192,1024]{1,0:T(8,128)(2,1)S(1)}, bf16[192,1024]{1,0:T(8,128)(2,1)S(1)}, u32[]{:S(2)}, u32[]{:S(2)}) collective-permute-start(bf16[192,1024]{1,0:T(8,128)(2,1)S(1)} %collective-permute-done.ref.refs_0_), channel_id=1, source_target_pairs={{0,2},{1,3},{2,0},{3,1},{4,6},{5,7},{6,4},{7,5},{8,10},{9,11},{10,... | collective-permute-start | bytes 1179656 | tf_op jit(solution)/shard_map/y1/ppermute | solution.py:334
  20.6 11.3 %collective-permute-start.1 = (bf16[192,1024]{1,0:T(8,128)(2,1)S(1)}, bf16[192,1024]{1,0:T(8,128)(2,1)S(1)}, u32[]{:S(2)}, u32[]{:S(2)}) collective-permute-start(bf16[192,1024]{1,0:T(8,128)(2,1)S(1)} %collective-permute-done.ref.refs_0_), channel_id=1, source_target_pairs={{0,4},{1,5},{2,6},{3,7},{4,8},{5,9},{6,10},{7,11},{8,12},{9,13},{1... | collective-permute-start | bytes 1179656 | tf_op jit(solution)/shard_map/z2/ppermute | solution.py:330
  25.2 16.0 %collective-permute-start.9 = (bf16[4,384,128]{2,1,0:T(8,128)(2,1)S(1)}, bf16[4,384,128]{2,1,0:T(8,128)(2,1)S(1)}, u32[]{:S(2)}, u32[]{:S(2)}) collective-permute-start(bf16[4,384,128]{2,1,0:T(8,128)(2,1)S(1)} %get-tuple-element.153), channel_id=1, source_target_pairs={{0,2},{1,3},{2,0},{3,1},{4,6},{5,7},{6,4},{7,5},{8,10},{9,11},{10,... | collective-permute-start | bytes 1179656 | tf_op jit(solution)/shard_map/side_share/ppermute | solution.py:334
  26.6 9.2 %collective-permute-start.7 = (bf16[128,1024]{1,0:T(8,128)(2,1)S(1)}, bf16[128,1024]{1,0:T(8,128)(2,1)S(1)}, u32[]{:S(2)}, u32[]{:S(2)}) collective-permute-start(bf16[128,1024]{1,0:T(8,128)(2,1)S(1)} %cut_1.1), channel_id=1, source_target_pairs={{0,16},{16,0},{1,17},{17,1},{2,18},{18,2},{3,19},{19,3},{4,20},{20... | collective-permute-start | bytes 786440 | tf_op jit(solution)/shard_map/x1a/ppermute | solution.py:342
  31.1 9.9 %collective-permute-start.8 = (bf16[128,1024]{1,0:T(8,128)(2,1)S(1)}, bf16[128,1024]{1,0:T(8,128)(2,1)S(1)}, u32[]{:S(2)}, u32[]{:S(2)}) collective-permute-start(bf16[128,1024]{1,0:T(8,128)(2,1)S(1)} %slice.19), channel_id=1, source_target_pairs={{0,16},{16,0},{1,17},{17,1},{2,18},{18,2},{3,19},{19,3},{4,20},{20... | collective-permute-start | bytes 786440 | tf_op jit(solution)/shard_map/x1b/ppermute | solution.py:342
  31.9 11.2 %collective-permute-start.6 = (bf16[192,1024]{1,0:T(8,128)(2,1)S(1)}, bf16[192,1024]{1,0:T(8,128)(2,1)S(1)}, u32[]{:S(2)}, u32[]{:S(2)}) collective-permute-start(bf16[192,1024]{1,0:T(8,128)(2,1)S(1)} %collective-permute-done.1.refs_0_), channel_id=1, source_target_pairs={{0,4},{1,5},{2,6},{3,7},{4,8},{5,9},{6,10},{7,11},{8,12},{9,13},{1... | collective-permute-start | bytes 1179656 | tf_op jit(solution)/shard_map/z3/ppermute | solution.py:330
  32.5 13.2 %collective-permute-start.16 = (bf16[192,1024]{1,0:T(8,128)(2,1)S(1)}, bf16[192,1024]{1,0:T(8,128)(2,1)S(1)}, u32[]{:S(2)}, u32[]{:S(2)}) collective-permute-start(bf16[192,1024]{1,0:T(8,128)(2,1)S(1)} %collective-permute-done.1.refs_0_), channel_id=1, source_target_pairs={{0,2},{1,3},{2,0},{3,1},{4,6},{5,7},{6,4},{7,5},{8,10},{9,11},{10,... | collective-permute-start | bytes 1179656 | tf_op jit(solution)/shard_map/y2/ppermute | solution.py:334
  35.8 8.3 %collective-permute-start.14 = (bf16[128,1024]{1,0:T(8,128)(2,1)S(1)}, bf16[128,1024]{1,0:T(8,128)(2,1)S(1)}, u32[]{:S(2)}, u32[]{:S(2)}) collective-permute-start(bf16[128,1024]{1,0:T(8,128)(2,1)S(1)} %slice.21), channel_id=1, source_target_pairs={{0,16},{16,0},{1,17},{17,1},{2,18},{18,2},{3,19},{19,3},{4,20},{20... | collective-permute-start | bytes 786440 | tf_op jit(solution)/shard_map/x2a/ppermute | solution.py:342
  41.3 7.2 %collective-permute-start.15 = (bf16[576,128]{1,0:T(8,128)(2,1)S(1)}, bf16[576,128]{1,0:T(8,128)(2,1)S(1)}, u32[]{:S(2)}, u32[]{:S(2)}) collective-permute-start(bf16[576,128]{1,0:T(8,128)(2,1)S(1)} %get-tuple-element.173), channel_id=1, source_target_pairs={{0,12},{1,13},{2,14},{3,15},{4,0},{5,1},{6,2},{7,3},{8,4},{9,5},{1... | collective-permute-start | bytes 442376 | tf_op jit(solution)/shard_map/line_3/ppermute | solution.py:330
  43.1 13.7 %collective-permute-start.10 = (bf16[192,1024]{1,0:T(8,128)(2,1)S(1)}, bf16[192,1024]{1,0:T(8,128)(2,1)S(1)}, u32[]{:S(2)}, u32[]{:S(2)}) collective-permute-start(bf16[192,1024]{1,0:T(8,128)(2,1)S(1)} %collective-permute-done.6.refs_0_), channel_id=1, source_target_pairs={{0,2},{1,3},{2,0},{3,1},{4,6},{5,7},{6,4},{7,5},{8,10},{9,11},{10,... | collective-permute-start | bytes 1179656 | tf_op jit(solution)/shard_map/y3/ppermute | solution.py:334
  44.1 8.9 %collective-permute-start.12 = (bf16[640,1024]{1,0:T(8,128)(2,1)S(1)}, bf16[640,1024]{1,0:T(8,128)(2,1)S(1)}, u32[]{:S(2)}, u32[]{:S(2)}) collective-permute-start(bf16[640,1024]{1,0:T(8,128)(2,1)S(1)} %pack_1.1), channel_id=1, source_target_pairs={{0,1},{1,0},{2,3},{3,2},{4,5},{5,4},{6,7},{7,6},{8,9},{9,8},{10,11... | collective-permute-start | bytes 3932168 | tf_op jit(solution)/shard_map/c1/ppermute | solution.py:338
  44.2 12.5 %collective-permute-start.11 = (bf16[128,1024]{1,0:T(8,128)(2,1)S(1)}, bf16[128,1024]{1,0:T(8,128)(2,1)S(1)}, u32[]{:S(2)}, u32[]{:S(2)}) collective-permute-start(bf16[128,1024]{1,0:T(8,128)(2,1)S(1)} %slice.20), channel_id=1, source_target_pairs={{0,16},{16,0},{1,17},{17,1},{2,18},{18,2},{3,19},{19,3},{4,20},{20... | collective-permute-start | bytes 786440 | tf_op jit(solution)/shard_map/x3a/ppermute | solution.py:342
  45.7 13.1 %collective-permute-start.17 = (bf16[576,128]{1,0:T(8,128)(2,1)S(1)}, bf16[576,128]{1,0:T(8,128)(2,1)S(1)}, u32[]{:S(2)}, u32[]{:S(2)}) collective-permute-start(bf16[576,128]{1,0:T(8,128)(2,1)S(1)} %get-tuple-element.191), channel_id=1, source_target_pairs={{0,8},{1,9},{2,10},{3,11},{4,12},{5,13},{6,14},{7,15},{8,0},{9,1},... | collective-permute-start | bytes 442376 | tf_op jit(solution)/shard_map/line_2/ppermute | solution.py:330
  48.5 10.2 %collective-permute-start.18 = (bf16[128,1024]{1,0:T(8,128)(2,1)S(1)}, bf16[128,1024]{1,0:T(8,128)(2,1)S(1)}, u32[]{:S(2)}, u32[]{:S(2)}) collective-permute-start(bf16[128,1024]{1,0:T(8,128)(2,1)S(1)} %slice.22), channel_id=1, source_target_pairs={{0,16},{16,0},{1,17},{17,1},{2,18},{18,2},{3,19},{19,3},{4,20},{20... | collective-permute-start | bytes 786440 | tf_op jit(solution)/shard_map/x2b/ppermute | solution.py:342
  53.1 7.2 %collective-permute-start.20 = (bf16[576,128]{1,0:T(8,128)(2,1)S(1)}, bf16[576,128]{1,0:T(8,128)(2,1)S(1)}, u32[]{:S(2)}, u32[]{:S(2)}) collective-permute-start(bf16[576,128]{1,0:T(8,128)(2,1)S(1)} %get-tuple-element.203), channel_id=1, source_target_pairs={{0,4},{1,5},{2,6},{3,7},{4,8},{5,9},{6,10},{7,11},{8,12},{9,13},{1... | collective-permute-start | bytes 442376 | tf_op jit(solution)/shard_map/line_1/ppermute | solution.py:330
  57.5 12.1 %collective-permute-start.23 = (bf16[128,1024]{1,0:T(8,128)(2,1)}, bf16[128,1024]{1,0:T(8,128)(2,1)}, u32[]{:S(2)}, u32[]{:S(2)}) collective-permute-start(bf16[128,1024]{1,0:T(8,128)(2,1)} %slice.23), channel_id=1, source_target_pairs={{0,16},{16,0},{1,17},{17,1},{2,18},{18,2},{3,19},{19,3},{4,20},{20... | collective-permute-start | bytes 786440 | tf_op jit(solution)/shard_map/x3b/ppermute | solution.py:342
  58.8 3.6 %collective-permute-start.22 = (bf16[640,1024]{1,0:T(8,128)(2,1)S(1)}, bf16[640,1024]{1,0:T(8,128)(2,1)S(1)}, u32[]{:S(2)}, u32[]{:S(2)}) collective-permute-start(bf16[640,1024]{1,0:T(8,128)(2,1)S(1)} %pack_2.1), channel_id=1, source_target_pairs={{0,1},{1,0},{2,3},{3,2},{4,5},{5,4},{6,7},{7,6},{8,9},{9,8},{10,11... | collective-permute-start | bytes 3932168 | tf_op jit(solution)/shard_map/c2/ppermute | solution.py:338
  61.0 5.0 %collective-permute-start.21 = (f32[256,128]{1,0:T(8,128)S(1)}, f32[256,128]{1,0:T(8,128)S(1)}, u32[]{:S(2)}, u32[]{:S(2)}) collective-permute-start(f32[256,128]{1,0:T(8,128)S(1)} %get-tuple-element.210.refs_0_), channel_id=1, source_target_pairs={{0,2},{1,3},{2,0},{3,1},{4,6},{5,7},{6,4},{7,5},{8,10},{9,11},{10,... | collective-permute-start | bytes 393224 | tf_op jit(solution)/shard_map/side_up/ppermute | solution.py:334
  62.4 3.6 %collective-permute-start.19 = (bf16[512,1024]{1,0:T(8,128)(2,1)S(1)}, bf16[512,1024]{1,0:T(8,128)(2,1)S(1)}, u32[]{:S(2)}, u32[]{:S(2)}) collective-permute-start(bf16[512,1024]{1,0:T(8,128)(2,1)S(1)} %pack_3.1), channel_id=1, source_target_pairs={{0,1},{1,0},{2,3},{3,2},{4,5},{5,4},{6,7},{7,6},{8,9},{9,8},{10,11... | collective-permute-start | bytes 3145736 | tf_op jit(solution)/shard_map/c3a/ppermute | solution.py:338
  66.0 3.6 %collective-permute-start.24 = (f32[512,128]{1,0:T(8,128)S(1)}, f32[512,128]{1,0:T(8,128)S(1)}, u32[]{:S(2)}, u32[]{:S(2)}) collective-permute-start(f32[512,128]{1,0:T(8,128)S(1)} %pack_up.1.mine), channel_id=1, source_target_pairs={{0,1},{1,0},{2,3},{3,2},{4,5},{5,4},{6,7},{7,6},{8,9},{9,8},{10,11... | collective-permute-start | bytes 786440 | tf_op jit(solution)/shard_map/core_up/ppermute | solution.py:338
  (13 other events, 63.4 us)

commit v4 on v3

--- a/solution.py
+++ b/solution.py
@@ -11,6 +11,7 @@
 ADAPTER_RANK = 16
 STRIP = 64
 VMEM_LIMIT = 12 * 1024 * 1024
+STEP_US = 20
 F32 = jnp.float32
 BF16 = jnp.bfloat16
 
@@ -48,8 +49,7 @@
     return values, act.astype(BF16), grad_a, grad_b
 
 
-GAPS = {'plane_1': 0, 'pack_1': 60, 'place_up_gradient': 2, 'side_sum': 5, 'pack_0': 0, 'line_sum': 0}
-GAP = 60
+OTHER_US = dict(plane_1=0, place_up_gradient=2, side_sum=5, pack_0=0, line_sum=0, pack_2=2, pack_up=2, scale_rows=5, gradient_shares=6)
 VMEM = pl.BlockSpec(memory_space=pltpu.VMEM)
 SMEM = pl.BlockSpec(memory_space=pltpu.SMEM)
 ANY = pl.BlockSpec(memory_space=pl.ANY)
@@ -60,7 +60,7 @@
     return jax.ShapeDtypeStruct(shape, dtype)
 
 
-def kernel(body, name, us, out_shape, in_specs, out_specs, operands, scratch=(), alias=None):
+def kernel(body, name, out_shape, in_specs, out_specs, operands, scratch=(), alias=None):
     return pl.pallas_call(
         body,
         name=name,
@@ -71,13 +71,13 @@
         input_output_aliases=alias or {},
         compiler_params=pltpu.CompilerParams(vmem_limit_bytes=VMEM_LIMIT),
         cost_estimate=pl.CostEstimate(
-            flops=int(GAPS.get(name, us) * 1.1e9), bytes_accessed=1, transcendentals=0
+            flops=int(OTHER_US.get(name, STEP_US) * 1.1e9), bytes_accessed=1, transcendentals=0
         ),
     )(*operands)
 
 
-def after(value, *others):
-    return lax.optimization_barrier((value,) + others)[0]
+def hold(value, after):
+    return lax.optimization_barrier((value, after))
 
 
 def place():
@@ -325,26 +325,21 @@
     half = ranks // 2
     each = rows + half
 
-    def over_z(name, v, by=1):
-        with jax.named_scope(name):
-            return lax.ppermute(v, "seq", swap(n, lambda z, y, c: (z + by, y, c)))
-
-    def over_y(name, v):
-        with jax.named_scope(name):
-            return lax.ppermute(v, "seq", swap(n, lambda z, y, c: (z, 1 - y, c)))
-
-    def over_core(name, v):
-        with jax.named_scope(name):
-            return lax.ppermute(v, "seq", swap(n, lambda z, y, c: (z, y, 1 - c)))
-
-    def over_x(name, v):
-        with jax.named_scope(name):
-            return lax.ppermute(v, "groups", [(0, 1), (1, 0)])
+    def over_z(v, by=1):
+        return lax.ppermute(v, "seq", swap(n, lambda z, y, c: (z + by, y, c)))
+
+    def over_y(v):
+        return lax.ppermute(v, "seq", swap(n, lambda z, y, c: (z, 1 - y, c)))
+
+    def over_core(v):
+        return lax.ppermute(v, "seq", swap(n, lambda z, y, c: (z, y, 1 - c)))
+
+    def over_x(v):
+        return lax.ppermute(v, "groups", [(0, 1), (1, 0)])
 
     p0, rest = kernel(
         dequant_body,
         "scale_rows",
-        5,
         [struct((shared_rows, columns), BF16), struct((kept, columns), BF16)],
         [HBM, HBM],
         [VMEM, VMEM],
@@ -355,13 +350,12 @@
             pltpu.SemaphoreType.DMA((2,)),
         ],
     )
-    z1, y0 = over_z("z1", p0), over_y("y0", p0)
+    z1, y0 = over_z(p0), over_y(p0)
 
     piece = (planes, 2, each, ranks)
     shrink, spread, send, keep = kernel(
         functools.partial(grads_body, rows),
         "gradient_shares",
-        6,
         [struct((count, ranks), BF16)] * 2 + [struct(piece, F32)] * 2,
         [HBM, VMEM, HBM, HBM, HBM, ANY],
         [VMEM] * 4,
@@ -376,12 +370,12 @@
         ],
     )
 
-    def plane(k, own, got, state, us):
+    def plane(k, own, got, state, spread):
         first = k == 0
         kinds = []
         if k == planes - 1:
             kinds = [struct((2, count, kept), BF16), struct((2, kept, ranks), BF16)]
-        operands = [tokens, cotangent, e["spread"], down] + own + got
+        operands = [tokens, cotangent, spread, down] + own + got
         if first:
             operands += [shrink, up]
             specs = [HBM, VMEM, VMEM, HBM] + [VMEM] * (len(operands) - 4)
@@ -393,7 +387,6 @@
         return kernel(
             functools.partial(plane_body, k, first, rows, kept, (len(own), len(got))),
             f"plane_{k}",
-            us,
             [struct((count, width), BF16), struct((count, columns), F32)] + kinds,
             specs,
             [HBM, VMEM] + [VMEM] * len(kinds),
@@ -413,178 +406,148 @@
         return kernel(
             pack_body,
             name,
-            GAP,
             struct((sum(v.shape[0] for v in parts), parts[0].shape[1]), parts[0].dtype),
             [VMEM] * len(parts),
             VMEM,
             parts,
         )
 
-    def pack(name, *parts):
+    def last_rows(i, weight, state, saved, spread):
         return kernel(
-            pack_body,
-            name,
-            GAP,
-            struct((sum(v.shape[0] for v in parts), parts[0].shape[1]), parts[0].dtype),
-            [VMEM] * len(parts),
-            VMEM,
-            parts,
-        )
-
-    def last_rows(k, i, weight, state, saved):
-        return kernel(
-            functools.partial(last_body, k, rows, i),
+            functools.partial(last_body, planes - 1, rows, i),
             f"last_rows_{i}",
-            GAP,
             [struct((count, width), BF16), struct((count, columns), (F32, BF16)[i])],
             [VMEM] * 6 + [HBM],
             [HBM, VMEM],
-            [saved[0], cotangent, e["spread"], saved[1], weight, state[1], state[0]],
+            [saved[0], cotangent, spread, saved[1], weight, state[1], state[0]],
             scratch=[pltpu.VMEM((count, kept), BF16), pltpu.SemaphoreType.DMA],
             alias={6: 0},
         )
 
-    e = {"send": send, "spread": spread, "z1": z1, "y0": y0}
-
-    def event(name):
-        e[name], e["spread"] = lax.optimization_barrier((e[name], e["spread"]))
-
-    def cut(name, v, us):
+    def cut(name, v):
         return kernel(
-            cut_body, name, us, struct((kept, columns), BF16), [VMEM], VMEM, (v,)
+            cut_body, name, struct((kept, columns), BF16), [VMEM], VMEM, (v,)
         )
 
-    def run_plane(k, own, got):
-        own = [e[v] if isinstance(v, str) else v for v in own]
-        state = (e["act"], e["acc"]) if k else None
-        e["act"], e["acc"], *e["saved"] = plane(k, own, [e[got]], state, GAP)
-
-    def run_last(i, name):
-        e["act"], e["acc"] = last_rows(3, i, e[name], (e["act"], e["acc"]), e["saved"])
-        return e["acc"]
-
-    e["core_share"] = over_core("core_share", e["send"])
-    event("z1")
-    e["z2"] = over_z("z2", e["z1"])
-    e["y1"] = over_y("y1", e["z1"])
-    event("z1")
-    e["cut"] = cut("cut_1", e["z1"], GAP)
-    event("cut")
-    e["x1a"] = over_x("x1a", e["cut"])
-    event("y0")
-    e["x0"] = over_x("x0", e["y0"][:kept])
-    event("core_share")
-    event("x0")
-    event("core_share")
-    e["own_y"], e["other_y"] = kernel(
+    core_share = over_core(send)
+    z1, spread = hold(z1, spread)
+    z2 = over_z(z1)
+    y1 = over_y(z1)
+    z1, spread = hold(z1, spread)
+    cut_z1 = cut("cut_1", z1)
+    cut_z1, spread = hold(cut_z1, spread)
+    x1a = over_x(cut_z1)
+    y0, spread = hold(y0, spread)
+    x0 = over_x(y0[:kept])
+    core_share, spread = hold(core_share, spread)
+    own_y, other_y = kernel(
         core_sum_body,
         "core_sum",
-        GAP,
         [struct((planes, each, ranks), F32), struct((planes, each, ranks), BF16)],
         [VMEM] * 2,
         [VMEM] * 2,
-        (keep, e["core_share"]),
-    )
-    event("own_y")
-    e["side_share"] = over_y("side_share", e["other_y"])
-    event("y1")
-    e["x1b"] = over_x("x1b", e["y1"][:kept])
-    event("z2")
-    e["z3"] = over_z("z3", e["z2"])
-    e["y2"] = over_y("y2", e["z2"])
-    e["x2a"] = over_x("x2a", e["z2"][:kept])
-    event("x1a")
-    event("x1b")
-    event("x0")
-    e["pack_0"] = pack("pack_0", p0, e["y0"], rest, e["x0"])
-    event("pack_0")
-    e["c0"] = over_core("c0", e["pack_0"])
-    event("side_share")
+        (keep, core_share),
+    )
+    own_y, spread = hold(own_y, spread)
+    side_share = over_y(other_y)
+    x1a, spread = hold(x1a, spread)
+    y1, spread = hold(y1, spread)
+    x1b = over_x(y1[:kept])
+    z2, spread = hold(z2, spread)
+    z3 = over_z(z2)
+    y2 = over_y(z2)
+    x2a = over_x(z2[:kept])
+    x0, spread = hold(x0, spread)
+    side_share, spread = hold(side_share, spread)
+    x0, spread = hold(x0, spread)
+    pack_0 = pack("pack_0", p0, y0, rest, x0)
+    pack_0, spread = hold(pack_0, spread)
+    c0 = over_core(pack_0)
+    x1b, spread = hold(x1b, spread)
+    side_share, spread = hold(side_share, spread)
     line = struct((rows + planes * half, ranks), BF16)
-    e["mine"], e["s1"], e["s2"], e["s3"] = kernel(
+    mine, s1, s2, s3 = kernel(
         functools.partial(side_sum_body, rows),
         "side_sum",
-        GAP,
         [struct(line.shape, F32), line, line, line],
         [VMEM] * 2,
         [VMEM] * 4,
-        (e["own_y"], e["side_share"]),
-    )
-    event("mine")
-    e["line_1"] = over_z("line_1", e["s1"], 1)
-    e["line_2"] = over_z("line_2", e["s2"], 2)
-    e["line_3"] = over_z("line_3", e["s3"], 3)
-    event("x1b")
-    e["pack_1"] = pack("pack_1", e["z1"], e["y1"], e["x1a"], e["x1b"])
-    event("pack_1")
-    e["c1"] = over_core("c1", e["pack_1"])
-    event("z3")
-    e["y3"] = over_y("y3", e["z3"])
-    e["x3a"] = over_x("x3a", e["z3"][:kept])
-    event("x2a")
-    event("c0")
-    event("y2")
-    e["x2b"] = over_x("x2b", e["y2"][:kept])
-    event("line_3")
-    event("c0")
-    run_plane(0, [p0, "y0", rest, "x0"], "c0")
-    event("acc")
-    event("c1")
-    run_plane(1, ["z1", "y1", "x1a", "x1b"], "c1")
-    event("acc")
-    event("x3a")
-    event("y3")
-    e["x3b"] = over_x("x3b", e["y3"][:kept])
-    event("x2b")
-    e["pack_2"] = pack("pack_2", e["z2"], e["y2"], e["x2a"], e["x2b"])
-    event("pack_2")
-    e["c2"] = over_core("c2", e["pack_2"])
-    event("line_2")
-    event("x3a")
-    e["pack_3"] = pack("pack_3", e["z3"], e["y3"], e["x3a"])
-    event("pack_3")
-    e["c3a"] = over_core("c3a", e["pack_3"])
-    event("line_1")
-    grad_a, e["quarter"] = kernel(
+        (own_y, side_share),
+    )
+    mine, spread = hold(mine, spread)
+    line_1 = over_z(s1, 1)
+    line_2 = over_z(s2, 2)
+    line_3 = over_z(s3, 3)
+    x1b, spread = hold(x1b, spread)
+    pack_1 = pack("pack_1", z1, y1, x1a, x1b)
+    pack_1, spread = hold(pack_1, spread)
+    c1 = over_core(pack_1)
+    z3, spread = hold(z3, spread)
+    y3 = over_y(z3)
+    x3a = over_x(z3[:kept])
+    x2a, spread = hold(x2a, spread)
+    c0, spread = hold(c0, spread)
+    y2, spread = hold(y2, spread)
+    x2b = over_x(y2[:kept])
+    line_3, spread = hold(line_3, spread)
+    c0, spread = hold(c0, spread)
+    act, acc = plane(0, [p0, y0, rest, x0], [c0], None, spread)
+    acc, spread = hold(acc, spread)
+    c1, spread = hold(c1, spread)
+    act, acc = plane(1, [z1, y1, x1a, x1b], [c1], (act, acc), spread)
+    acc, spread = hold(acc, spread)
+    x3a, spread = hold(x3a, spread)
+    y3, spread = hold(y3, spread)
+    x3b = over_x(y3[:kept])
+    x2b, spread = hold(x2b, spread)
+    pack_2 = pack("pack_2", z2, y2, x2a, x2b)
+    pack_2, spread = hold(pack_2, spread)
+    c2 = over_core(pack_2)
+    x3a, spread = hold(x3a, spread)
+    pack_3 = pack("pack_3", z3, y3, x3a)
+    pack_3, spread = hold(pack_3, spread)
+    c3a = over_core(pack_3)
+    line_2, spread = hold(line_2, spread)
+    line_1, spread = hold(line_1, spread)
+    grad_a, quarter = kernel(
         line_sum_body,
         "line_sum",
-        GAP,
         [struct((rows, ranks), F32), struct((planes * half, ranks), F32)],
         [VMEM] * 4,
         [VMEM] * 2,
-        (e["mine"], e["line_1"], e["line_2"], e["line_3"]),
-    )
-    event("quarter")
-    e["side_up"] = over_y("side_up", e["quarter"])
-    event("c2")
-    run_plane(2, ["z2", "y2", "x2a", "x2b"], "c2")
-    event("acc")
-    event("side_up")
-    e["both"] = pack("pack_up", e["quarter"], e["side_up"])
-    event("both")
-    e["core_up"] = over_core("core_up", e["both"])
-    event("c3a")
-    run_plane(3, ["z3", "y3", "x3a"], "c3a")
-    event("acc")
-    event("core_up")
-    event("x3b")
-    e["c3b"] = over_core("c3b", e["x3b"])
-    event("core_up")
+        (mine, line_1, line_2, line_3),
+    )
+    quarter, spread = hold(quarter, spread)
+    side_up = over_y(quarter)
+    c2, spread = hold(c2, spread)
+    act, acc = plane(2, [z2, y2, x2a, x2b], [c2], (act, acc), spread)
+    acc, spread = hold(acc, spread)
+    side_up, spread = hold(side_up, spread)
+    x3b, spread = hold(x3b, spread)
+    c3b = over_core(x3b)
+    c3a, spread = hold(c3a, spread)
+    side_up, spread = hold(side_up, spread)
+    both = pack("pack_up", quarter, side_up)
+    both, spread = hold(both, spread)
+    core_up = over_core(both)
+    c3a, spread = hold(c3a, spread)
+    act, acc, *saved = plane(3, [z3, y3, x3a], [c3a], (act, acc), spread)
+    acc, spread = hold(acc, spread)
+    core_up, spread = hold(core_up, spread)
     grad_b = kernel(
         place_b_body,
         "place_up_gradient",
-        GAP,
         struct((ranks, columns), F32),
         [VMEM] * 2,
         VMEM,
-        (e["both"], e["core_up"]),
-    )
-    event("x3b")
-    run_last(0, "x3b")
-    event("acc")
-    event("c3b")
-    values = run_last(1, "c3b")
-    act, values = e["act"], e["acc"]
+        (both, core_up),
+    )
+    x3b, spread = hold(x3b, spread)
+    act, acc = last_rows(0, x3b, (act, acc), saved, spread)
+    acc, spread = hold(acc, spread)
+    c3b, spread = hold(c3b, spread)
+    act, acc = last_rows(1, c3b, (act, acc), saved, spread)
+    values = acc
     return values, act, grad_a, grad_b
 
 

time: 75.3 us -> 74.9 us (level)
  waiting for transfers between devices: 18.3 us -> 22.3 us
  starting transfers between devices: 27.4 us -> 24.7 us
  Pallas kernels: 25.7 us -> 24.8 us
    ppermute x6, starting transfers between devices: 8.46 us -> 6.15 us  [over_y(): return lax.ppermute(v, 'seq', swap(n, lambda z, y, c: (z, 1 - y, c)))]
    ppermute x6, waiting for transfers between devices: 5.87 us -> 7.59 us  [over_z(): return lax.ppermute(v, 'seq', swap(n, lambda z, y, c: (z + by, y, c)))]
    ppermute x6, waiting for transfers between devices: 3.37 us -> 4.94 us  [over_y(): return lax.ppermute(v, 'seq', swap(n, lambda z, y, c: (z, 1 - y, c)))]
    ppermute x6, starting transfers between devices: 9.48 us -> 7.99 us  [over_z(): return lax.ppermute(v, 'seq', swap(n, lambda z, y, c: (z + by, y, c)))]
    ppermute x7, starting transfers between devices: 8.58 us -> 9.77 us  [over_x(): return lax.ppermute(v, 'groups', [(0, 1), (1, 0)])]
    pallas_call x18, Pallas kernels: 25.7 us -> 24.8 us  [kernel(): pl.pallas_call(body, name=name, in_specs=in_specs, out_specs=out_specs, o...]
    ppermute x7, waiting for transfers between devices: 8.94 us -> 9.72 us  [over_x(): return lax.ppermute(v, 'groups', [(0, 1), (1, 0)])]
    unnamed x22 -> x14, local copies, waits for them, and re-layouts: 1.81 us -> 1.79 us
  transfers between devices with their start and end apart: 26 -> 26, of which waited for: 9 -> 10; matrix products, arithmetic and copies ran while one was open for 1% -> 0% of each run, Pallas kernels for 30% -> 29%
where the time goes in v4:
time: 74.9 us; the launch traced here: 74.7 us
  Pallas kernels  24.8 us (33%)
  starting transfers between devices  24.7 us (33%)
  waiting for transfers between devices  22.3 us (30%)
  local copies, waits for them, and re-layouts  1.9 us (3%)
  between operations  1.07 us (1%)
    pallas_call x18, Pallas kernels, kernel(): pl.pallas_call(body, name=name, in_specs=in_specs, out_specs=out_specs, o...  24.8 us
    ppermute x7, starting transfers between devices, over_x(): return lax.ppermute(v, 'groups', [(0, 1), (1, 0)])  9.77 us
    ppermute x7, waiting for transfers between devices, over_x(): return lax.ppermute(v, 'groups', [(0, 1), (1, 0)])  9.72 us
    ppermute x6, starting transfers between devices, over_z(): return lax.ppermute(v, 'seq', swap(n, lambda z, y, c: (z + by, y, c)))  7.99 us
    ppermute x6, waiting for transfers between devices, over_z(): return lax.ppermute(v, 'seq', swap(n, lambda z, y, c: (z + by, y, c)))  7.59 us
    ppermute x6, starting transfers between devices, over_y(): return lax.ppermute(v, 'seq', swap(n, lambda z, y, c: (z, 1 - y, c)))  6.15 us
    ppermute x6, waiting for transfers between devices, over_y(): return lax.ppermute(v, 'seq', swap(n, lambda z, y, c: (z, 1 - y, c)))  4.94 us
    unnamed x14, local copies, waits for them, and re-layouts  1.79 us
  transfers between devices with their start and end apart: 26, of which 10 were waited for; matrix products, arithmetic and copies ran while one was open for 0% of the time, Pallas kernels for 29%

profile of v4, /device:TPU:0, one launch (start us, length us, event | category | flops | bytes accessed | tf_op | source)
XLA Modules:
  0.0 74.7 jit_solution(7626876195279638261)
XLA Ops:
  3.2 3.1 %collective-permute-start = (bf16[192,1024]{1,0:T(8,128)(2,1)S(1)}, bf16[192,1024]{1,0:T(8,128)(2,1)S(1)}, u32[]{:S(2)}, u32[]{:S(2)}) collective-permute-start(bf16[192,1024]{1,0:T(8,128)(2,1)S(1)} %get-tuple-element.129._.refs_0_), channel_id=1, source_target_pairs={{0,4},{1,5},{2,6},{3,7},{4,8},{5,9},{6,10},{7,11},{8,12},{9,13},{1... | collective-permute-start | bytes 1179656 | tf_op jit(solution)/shard_map/ppermute | solution.py:329
  6.3 1.5 %collective-permute-start.5 = (bf16[192,1024]{1,0:T(8,128)(2,1)S(1)}, bf16[192,1024]{1,0:T(8,128)(2,1)S(1)}, u32[]{:S(2)}, u32[]{:S(2)}) collective-permute-start(bf16[192,1024]{1,0:T(8,128)(2,1)S(1)} %get-tuple-element.129._.refs_0_), channel_id=1, source_target_pairs={{0,2},{1,3},{2,0},{3,1},{4,6},{5,7},{6,4},{7,5},{8,10},{9,11},{10,... | collective-permute-start | bytes 1179656 | tf_op jit(solution)/shard_map/ppermute | solution.py:332
  7.9 5.1 %gradient_shares.1 = (bf16[384,128]{1,0:T(8,128)(2,1)S(1)}, bf16[384,128]{1,0:T(8,128)(2,1)S(1)}, f32[4,2,384,128]{3,2,1,0:T(8,128)S(1)}, f32[4,2,384,128]{3,2,1,0:T(8,128)S(1)}) custom-call(bf16[384,5120]{1,0:T(8,128)(2,1)S(1)} %copy-done, s32[1,384]{1,0:T(1,128)S(1)} %broadcast_in_dim.3.idx, bf16[5120,128]{1,0:T(8,128)(2,1)S(1)} %copy-done.1, ...), custom_call_target="tpu_custom_call" | custom-call | flops 6600000000 | bytes 1 | tf_op jit(solution)/shard_map/gradient_shares/pallas_call | solution.py:64
  13.0 4.4 %collective-permute-done.ref.refs_0_ = bf16[192,1024]{1,0:T(8,128)(2,1)S(1)} collective-permute-done((bf16[192,1024]{1,0:T(8,128)(2,1)S(1)}, bf16[192,1024]{1,0:T(8,128)(2,1)S(1)}, u32[]{:S(2)}, u32[]{:S(2)}) %collective-permute-start) | collective-permute-done | bytes 393248 | tf_op jit(solution)/shard_map/ppermute | solution.py:329
  17.4 1.5 %collective-permute-start.2 = (bf16[192,1024]{1,0:T(8,128)(2,1)S(1)}, bf16[192,1024]{1,0:T(8,128)(2,1)S(1)}, u32[]{:S(2)}, u32[]{:S(2)}) collective-permute-start(bf16[192,1024]{1,0:T(8,128)(2,1)S(1)} %collective-permute-done.ref.refs_0_), channel_id=1, source_target_pairs={{0,2},{1,3},{2,0},{3,1},{4,6},{5,7},{6,4},{7,5},{8,10},{9,11},{10,... | collective-permute-start | bytes 1179656 | tf_op jit(solution)/shard_map/ppermute | solution.py:332
  19.0 1.6 %collective-permute-start.3 = (bf16[128,1024]{1,0:T(8,128)(2,1)S(1)}, bf16[128,1024]{1,0:T(8,128)(2,1)S(1)}, u32[]{:S(2)}, u32[]{:S(2)}) collective-permute-start(bf16[128,1024]{1,0:T(8,128)(2,1)S(1)} %cut_1.1), channel_id=1, source_target_pairs={{0,16},{16,0},{1,17},{17,1},{2,18},{18,2},{3,19},{19,3},{4,20},{20... | collective-permute-start | bytes 786440 | tf_op jit(solution)/shard_map/ppermute | solution.py:338
  21.9 6.4 %collective-permute-done.3.refs_2_ = bf16[128,1024]{1,0:T(8,128)(2,1)S(1)} collective-permute-done((bf16[128,1024]{1,0:T(8,128)(2,1)S(1)}, bf16[128,1024]{1,0:T(8,128)(2,1)S(1)}, u32[]{:S(2)}, u32[]{:S(2)}) %collective-permute-start.3) | collective-permute-done | bytes 262176 | tf_op jit(solution)/shard_map/ppermute | solution.py:338
  29.5 1.6 %collective-permute-start.7 = (bf16[128,1024]{1,0:T(8,128)(2,1)S(1)}, bf16[128,1024]{1,0:T(8,128)(2,1)S(1)}, u32[]{:S(2)}, u32[]{:S(2)}) collective-permute-start(bf16[128,1024]{1,0:T(8,128)(2,1)S(1)} %slice.18), channel_id=1, source_target_pairs={{0,16},{16,0},{1,17},{17,1},{2,18},{18,2},{3,19},{19,3},{4,20},{20... | collective-permute-start | bytes 786440 | tf_op jit(solution)/shard_map/ppermute | solution.py:338
  31.2 1.5 %collective-permute-start.16 = (bf16[192,1024]{1,0:T(8,128)(2,1)S(1)}, bf16[192,1024]{1,0:T(8,128)(2,1)S(1)}, u32[]{:S(2)}, u32[]{:S(2)}) collective-permute-start(bf16[192,1024]{1,0:T(8,128)(2,1)S(1)} %collective-permute-done.1.refs_0_), channel_id=1, source_target_pairs={{0,2},{1,3},{2,0},{3,1},{4,6},{5,7},{6,4},{7,5},{8,10},{9,11},{10,... | collective-permute-start | bytes 1179656 | tf_op jit(solution)/shard_map/ppermute | solution.py:332
  32.7 1.2 %collective-permute-done.8.refs_3_ = bf16[128,1024]{1,0:T(8,128)(2,1)S(1)} collective-permute-done((bf16[128,1024]{1,0:T(8,128)(2,1)S(1)}, bf16[128,1024]{1,0:T(8,128)(2,1)S(1)}, u32[]{:S(2)}, u32[]{:S(2)}) %collective-permute-start.8) | collective-permute-done | bytes 262176 | tf_op jit(solution)/shard_map/ppermute | solution.py:338
  33.9 1.5 %collective-permute-start.14 = (bf16[128,1024]{1,0:T(8,128)(2,1)S(1)}, bf16[128,1024]{1,0:T(8,128)(2,1)S(1)}, u32[]{:S(2)}, u32[]{:S(2)}) collective-permute-start(bf16[128,1024]{1,0:T(8,128)(2,1)S(1)} %slice.21), channel_id=1, source_target_pairs={{0,16},{16,0},{1,17},{17,1},{2,18},{18,2},{3,19},{19,3},{4,20},{20... | collective-permute-start | bytes 786440 | tf_op jit(solution)/shard_map/ppermute | solution.py:338
  35.4 2.5 %collective-permute-done.9.got = bf16[4,384,128]{2,1,0:T(8,128)(2,1)S(1)} collective-permute-done((bf16[4,384,128]{2,1,0:T(8,128)(2,1)S(1)}, bf16[4,384,128]{2,1,0:T(8,128)(2,1)S(1)}, u32[]{:S(2)}, u32[]{:S(2)}) %collective-permute-start.9) | collective-permute-done | bytes 393248 | tf_op jit(solution)/shard_map/ppermute | solution.py:332
  38.0 1.5 %collective-permute-done.7.refs_3_ = bf16[128,1024]{1,0:T(8,128)(2,1)S(1)} collective-permute-done((bf16[128,1024]{1,0:T(8,128)(2,1)S(1)}, bf16[128,1024]{1,0:T(8,128)(2,1)S(1)}, u32[]{:S(2)}, u32[]{:S(2)}) %collective-permute-start.7) | collective-permute-done | bytes 262176 | tf_op jit(solution)/shard_map/ppermute | solution.py:338
  39.7 3.9 %collective-permute-start.15 = (bf16[576,128]{1,0:T(8,128)(2,1)S(1)}, bf16[576,128]{1,0:T(8,128)(2,1)S(1)}, u32[]{:S(2)}, u32[]{:S(2)}) collective-permute-start(bf16[576,128]{1,0:T(8,128)(2,1)S(1)} %get-tuple-element.175), channel_id=1, source_target_pairs={{0,12},{1,13},{2,14},{3,15},{4,0},{5,1},{6,2},{7,3},{8,4},{9,5},{1... | collective-permute-start | bytes 442376 | tf_op jit(solution)/shard_map/ppermute | solution.py:329
  44.3 1.6 %collective-permute-start.11 = (bf16[128,1024]{1,0:T(8,128)(2,1)S(1)}, bf16[128,1024]{1,0:T(8,128)(2,1)S(1)}, u32[]{:S(2)}, u32[]{:S(2)}) collective-permute-start(bf16[128,1024]{1,0:T(8,128)(2,1)S(1)} %slice.20), channel_id=1, source_target_pairs={{0,16},{16,0},{1,17},{17,1},{2,18},{18,2},{3,19},{19,3},{4,20},{20... | collective-permute-start | bytes 786440 | tf_op jit(solution)/shard_map/ppermute | solution.py:338
  47.8 1.6 %collective-permute-start.17 = (bf16[128,1024]{1,0:T(8,128)(2,1)S(1)}, bf16[128,1024]{1,0:T(8,128)(2,1)S(1)}, u32[]{:S(2)}, u32[]{:S(2)}) collective-permute-start(bf16[128,1024]{1,0:T(8,128)(2,1)S(1)} %slice.22), channel_id=1, source_target_pairs={{0,16},{16,0},{1,17},{17,1},{2,18},{18,2},{3,19},{19,3},{4,20},{20... | collective-permute-start | bytes 786440 | tf_op jit(solution)/shard_map/ppermute | solution.py:338
  49.3 3.8 %plane_0.1 = (bf16[384,5120]{1,0:T(8,128)(2,1)}, f32[384,1024]{1,0:T(8,128)S(1)}) custom-call(bf16[384,5120]{1,0:T(8,128)(2,1)S(1)} %copy-done, bf16[384,1024]{1,0:T(8,128)(2,1)S(1)} %copy-done.2, bf16[384,128]{1,0:T(8,128)(2,1)S(1)} %get-tuple-element.246.spread, bf16[5120,128]{1,0:T(8,128)(2,1)S(1)} %copy-done.1, ...), custom_call_target="tpu_custom_call" | custom-call | flops 22000001024 | bytes 1 | tf_op jit(solution)/shard_map/plane_0/pallas_call | solution.py:64
  53.4 3.2 %plane_1.1 = (bf16[384,5120]{1,0:T(8,128)(2,1)}, f32[384,1024]{1,0:T(8,128)S(1)}) custom-call(bf16[384,5120]{1,0:T(8,128)(2,1)S(1)} %copy-done, bf16[384,1024]{1,0:T(8,128)(2,1)S(1)} %copy-done.2, bf16[384,128]{1,0:T(8,128)(2,1)S(1)} %get-tuple-element.246.spread, bf16[5120,128]{1,0:T(8,128)(2,1)S(1)} %copy-done.1, ...), custom_call_target="tpu_custom_call", output_to_operand_aliasing={{0}: (10, {})} | custom-call | bytes 1 | tf_op jit(solution)/shard_map/plane_1/pallas_call | solution.py:64
  56.7 1.4 %collective-permute-start.19 = (bf16[128,1024]{1,0:T(8,128)(2,1)S(1)}, bf16[128,1024]{1,0:T(8,128)(2,1)S(1)}, u32[]{:S(2)}, u32[]{:S(2)}) collective-permute-start(bf16[128,1024]{1,0:T(8,128)(2,1)S(1)} %slice.23), channel_id=1, source_target_pairs={{0,16},{16,0},{1,17},{17,1},{2,18},{18,2},{3,19},{19,3},{4,20},{20... | collective-permute-start | bytes 786440 | tf_op jit(solution)/shard_map/ppermute | solution.py:338
  58.9 1.9 %collective-permute-done.20.r1 = bf16[576,128]{1,0:T(8,128)(2,1)S(1)} collective-permute-done((bf16[576,128]{1,0:T(8,128)(2,1)S(1)}, bf16[576,128]{1,0:T(8,128)(2,1)S(1)}, u32[]{:S(2)}, u32[]{:S(2)}) %collective-permute-start.20) | collective-permute-done | bytes 147488 | tf_op jit(solution)/shard_map/ppermute | solution.py:329
  62.1 3.2 %plane_2.1 = (bf16[384,5120]{1,0:T(8,128)(2,1)}, f32[384,1024]{1,0:T(8,128)S(1)}) custom-call(bf16[384,5120]{1,0:T(8,128)(2,1)S(1)} %copy-done, bf16[384,1024]{1,0:T(8,128)(2,1)S(1)} %copy-done.2, bf16[384,128]{1,0:T(8,128)(2,1)S(1)} %get-tuple-element.246.spread, bf16[5120,128]{1,0:T(8,128)(2,1)S(1)} %copy-done.1, ...), custom_call_target="tpu_custom_call", output_to_operand_aliasing={{0}: (10, {})} | custom-call | flops 22000001024 | bytes 1 | tf_op jit(solution)/shard_map/plane_2/pallas_call | solution.py:64
  65.3 1.2 %collective-permute-done.22.refs_1_ = f32[256,128]{1,0:T(8,128)S(1)} collective-permute-done((f32[256,128]{1,0:T(8,128)S(1)}, f32[256,128]{1,0:T(8,128)S(1)}, u32[]{:S(2)}, u32[]{:S(2)}) %collective-permute-start.22) | collective-permute-done | bytes 131104 | tf_op jit(solution)/shard_map/ppermute | solution.py:332
  66.7 3.3 %plane_3.1 = (bf16[384,5120]{1,0:T(8,128)(2,1)}, f32[384,1024]{1,0:T(8,128)S(1)}, bf16[2,384,128]{2,1,0:T(8,128)(2,1)S(1)}, bf16[2,128,128]{2,1,0:T(8,128)(2,1)S(1)}) custom-call(bf16[384,5120]{1,0:T(8,128)(2,1)S(1)} %copy-done, bf16[384,1024]{1,0:T(8,128)(2,1)S(1)} %copy-done.2, ...), custom_call_target="tpu_custom_call", output_to_operand_aliasing={{0}: (9, {})} | custom-call | flops 22000001024 | bytes 1 | tf_op jit(solution)/shard_map/plane_3/pallas_call | solution.py:64
  72.5 2.0 %last_rows_1.1 = (bf16[384,5120]{1,0:T(8,128)(2,1)}, bf16[384,1024]{1,0:T(8,128)(2,1)}) custom-call(bf16[2,384,128]{2,1,0:T(8,128)(2,1)S(1)} %get-tuple-element.233.tok, bf16[384,1024]{1,0:T(8,128)(2,1)S(1)} %copy-done.2, bf16[384,128]{1,0:T(8,128)(2,1)S(1)} %get-tuple-element.246.spread, ...), custom_call_target="tpu_custom_call", output_to_operand_aliasing={{0}: (6, {})} | custom-call | flops 22000001024 | bytes 1 | tf_op jit(solution)/shard_map/last_rows_1/pallas_call | solution.py:64
  (67 shorter events, 13.1 us)
Async XLA Ops:
  3.2 14.2 %collective-permute-start = (bf16[192,1024]{1,0:T(8,128)(2,1)S(1)}, bf16[192,1024]{1,0:T(8,128)(2,1)S(1)}, u32[]{:S(2)}, u32[]{:S(2)}) collective-permute-start(bf16[192,1024]{1,0:T(8,128)(2,1)S(1)} %get-tuple-element.129._.refs_0_), channel_id=1, source_target_pairs={{0,4},{1,5},{2,6},{3,7},{4,8},{5,9},{6,10},{7,11},{8,12},{9,13},{1... | collective-permute-start | bytes 1179656 | tf_op jit(solution)/shard_map/ppermute | solution.py:329
  6.3 12.7 %collective-permute-start.5 = (bf16[192,1024]{1,0:T(8,128)(2,1)S(1)}, bf16[192,1024]{1,0:T(8,128)(2,1)S(1)}, u32[]{:S(2)}, u32[]{:S(2)}) collective-permute-start(bf16[192,1024]{1,0:T(8,128)(2,1)S(1)} %get-tuple-element.129._.refs_0_), channel_id=1, source_target_pairs={{0,2},{1,3},{2,0},{3,1},{4,6},{5,7},{6,4},{7,5},{8,10},{9,11},{10,... | collective-permute-start | bytes 1179656 | tf_op jit(solution)/shard_map/ppermute | solution.py:332
  12.9 7.6 %collective-permute-start.4 = (f32[4,2,384,128]{3,2,1,0:T(8,128)S(1)}, f32[4,2,384,128]{3,2,1,0:T(8,128)S(1)}, u32[]{:S(2)}, u32[]{:S(2)}) collective-permute-start(f32[4,2,384,128]{3,2,1,0:T(8,128)S(1)} %get-tuple-element.136), channel_id=1, source_target_pairs={{0,1},{1,0},{2,3},{3,2},{4,5},{5,4},{6,7},{7,6},{8,9},{9,8},{10,11... | collective-permute-start | bytes 4718600 | tf_op jit(solution)/shard_map/ppermute | solution.py:335
  17.4 12.1 %collective-permute-start.2 = (bf16[192,1024]{1,0:T(8,128)(2,1)S(1)}, bf16[192,1024]{1,0:T(8,128)(2,1)S(1)}, u32[]{:S(2)}, u32[]{:S(2)}) collective-permute-start(bf16[192,1024]{1,0:T(8,128)(2,1)S(1)} %collective-permute-done.ref.refs_0_), channel_id=1, source_target_pairs={{0,2},{1,3},{2,0},{3,1},{4,6},{5,7},{6,4},{7,5},{8,10},{9,11},{10,... | collective-permute-start | bytes 1179656 | tf_op jit(solution)/shard_map/ppermute | solution.py:332
  19.0 12.1 %collective-permute-start.1 = (bf16[192,1024]{1,0:T(8,128)(2,1)S(1)}, bf16[192,1024]{1,0:T(8,128)(2,1)S(1)}, u32[]{:S(2)}, u32[]{:S(2)}) collective-permute-start(bf16[192,1024]{1,0:T(8,128)(2,1)S(1)} %collective-permute-done.ref.refs_0_), channel_id=1, source_target_pairs={{0,4},{1,5},{2,6},{3,7},{4,8},{5,9},{6,10},{7,11},{8,12},{9,13},{1... | collective-permute-start | bytes 1179656 | tf_op jit(solution)/shard_map/ppermute | solution.py:329
  19.0 9.3 %collective-permute-start.3 = (bf16[128,1024]{1,0:T(8,128)(2,1)S(1)}, bf16[128,1024]{1,0:T(8,128)(2,1)S(1)}, u32[]{:S(2)}, u32[]{:S(2)}) collective-permute-start(bf16[128,1024]{1,0:T(8,128)(2,1)S(1)} %cut_1.1), channel_id=1, source_target_pairs={{0,16},{16,0},{1,17},{17,1},{2,18},{18,2},{3,19},{19,3},{4,20},{20... | collective-permute-start | bytes 786440 | tf_op jit(solution)/shard_map/ppermute | solution.py:338
  20.7 17.2 %collective-permute-start.9 = (bf16[4,384,128]{2,1,0:T(8,128)(2,1)S(1)}, bf16[4,384,128]{2,1,0:T(8,128)(2,1)S(1)}, u32[]{:S(2)}, u32[]{:S(2)}) collective-permute-start(bf16[4,384,128]{2,1,0:T(8,128)(2,1)S(1)} %get-tuple-element.152), channel_id=1, source_target_pairs={{0,2},{1,3},{2,0},{3,1},{4,6},{5,7},{6,4},{7,5},{8,10},{9,11},{10,... | collective-permute-start | bytes 1179656 | tf_op jit(solution)/shard_map/ppermute | solution.py:332
  21.3 12.6 %collective-permute-start.8 = (bf16[128,1024]{1,0:T(8,128)(2,1)S(1)}, bf16[128,1024]{1,0:T(8,128)(2,1)S(1)}, u32[]{:S(2)}, u32[]{:S(2)}) collective-permute-start(bf16[128,1024]{1,0:T(8,128)(2,1)S(1)} %slice.19), channel_id=1, source_target_pairs={{0,16},{16,0},{1,17},{17,1},{2,18},{18,2},{3,19},{19,3},{4,20},{20... | collective-permute-start | bytes 786440 | tf_op jit(solution)/shard_map/ppermute | solution.py:338
  29.5 10.0 %collective-permute-start.7 = (bf16[128,1024]{1,0:T(8,128)(2,1)S(1)}, bf16[128,1024]{1,0:T(8,128)(2,1)S(1)}, u32[]{:S(2)}, u32[]{:S(2)}) collective-permute-start(bf16[128,1024]{1,0:T(8,128)(2,1)S(1)} %slice.18), channel_id=1, source_target_pairs={{0,16},{16,0},{1,17},{17,1},{2,18},{18,2},{3,19},{19,3},{4,20},{20... | collective-permute-start | bytes 786440 | tf_op jit(solution)/shard_map/ppermute | solution.py:338
  31.1 12.6 %collective-permute-start.6 = (bf16[192,1024]{1,0:T(8,128)(2,1)S(1)}, bf16[192,1024]{1,0:T(8,128)(2,1)S(1)}, u32[]{:S(2)}, u32[]{:S(2)}) collective-permute-start(bf16[192,1024]{1,0:T(8,128)(2,1)S(1)} %collective-permute-done.1.refs_0_), channel_id=1, source_target_pairs={{0,4},{1,5},{2,6},{3,7},{4,8},{5,9},{6,10},{7,11},{8,12},{9,13},{1... | collective-permute-start | bytes 1179656 | tf_op jit(solution)/shard_map/ppermute | solution.py:329
  31.2 14.6 %collective-permute-start.16 = (bf16[192,1024]{1,0:T(8,128)(2,1)S(1)}, bf16[192,1024]{1,0:T(8,128)(2,1)S(1)}, u32[]{:S(2)}, u32[]{:S(2)}) collective-permute-start(bf16[192,1024]{1,0:T(8,128)(2,1)S(1)} %collective-permute-done.1.refs_0_), channel_id=1, source_target_pairs={{0,2},{1,3},{2,0},{3,1},{4,6},{5,7},{6,4},{7,5},{8,10},{9,11},{10,... | collective-permute-start | bytes 1179656 | tf_op jit(solution)/shard_map/ppermute | solution.py:332
  33.9 10.4 %collective-permute-start.14 = (bf16[128,1024]{1,0:T(8,128)(2,1)S(1)}, bf16[128,1024]{1,0:T(8,128)(2,1)S(1)}, u32[]{:S(2)}, u32[]{:S(2)}) collective-permute-start(bf16[128,1024]{1,0:T(8,128)(2,1)S(1)} %slice.21), channel_id=1, source_target_pairs={{0,16},{16,0},{1,17},{17,1},{2,18},{18,2},{3,19},{19,3},{4,20},{20... | collective-permute-start | bytes 786440 | tf_op jit(solution)/shard_map/ppermute | solution.py:338
  39.6 4.7 %collective-permute-start.13 = (bf16[640,1024]{1,0:T(8,128)(2,1)S(1)}, bf16[640,1024]{1,0:T(8,128)(2,1)S(1)}, u32[]{:S(2)}, u32[]{:S(2)}) collective-permute-start(bf16[640,1024]{1,0:T(8,128)(2,1)S(1)} %pack_0.1), channel_id=1, source_target_pairs={{0,1},{1,0},{2,3},{3,2},{4,5},{5,4},{6,7},{7,6},{8,9},{9,8},{10,11... | collective-permute-start | bytes 3932168 | tf_op jit(solution)/shard_map/ppermute | solution.py:335
  39.7 8.0 %collective-permute-start.15 = (bf16[576,128]{1,0:T(8,128)(2,1)S(1)}, bf16[576,128]{1,0:T(8,128)(2,1)S(1)}, u32[]{:S(2)}, u32[]{:S(2)}) collective-permute-start(bf16[576,128]{1,0:T(8,128)(2,1)S(1)} %get-tuple-element.175), channel_id=1, source_target_pairs={{0,12},{1,13},{2,14},{3,15},{4,0},{5,1},{6,2},{7,3},{8,4},{9,5},{1... | collective-permute-start | bytes 442376 | tf_op jit(solution)/shard_map/ppermute | solution.py:329
  43.7 13.0 %collective-permute-start.10 = (bf16[192,1024]{1,0:T(8,128)(2,1)S(1)}, bf16[192,1024]{1,0:T(8,128)(2,1)S(1)}, u32[]{:S(2)}, u32[]{:S(2)}) collective-permute-start(bf16[192,1024]{1,0:T(8,128)(2,1)S(1)} %collective-permute-done.6.refs_0_), channel_id=1, source_target_pairs={{0,2},{1,3},{2,0},{3,1},{4,6},{5,7},{6,4},{7,5},{8,10},{9,11},{10,... | collective-permute-start | bytes 1179656 | tf_op jit(solution)/shard_map/ppermute | solution.py:332
  44.3 8.9 %collective-permute-start.12 = (bf16[640,1024]{1,0:T(8,128)(2,1)S(1)}, bf16[640,1024]{1,0:T(8,128)(2,1)S(1)}, u32[]{:S(2)}, u32[]{:S(2)}) collective-permute-start(bf16[640,1024]{1,0:T(8,128)(2,1)S(1)} %pack_1.1), channel_id=1, source_target_pairs={{0,1},{1,0},{2,3},{3,2},{4,5},{5,4},{6,7},{7,6},{8,9},{9,8},{10,11... | collective-permute-start | bytes 3932168 | tf_op jit(solution)/shard_map/ppermute | solution.py:335
  44.3 12.4 %collective-permute-start.11 = (bf16[128,1024]{1,0:T(8,128)(2,1)S(1)}, bf16[128,1024]{1,0:T(8,128)(2,1)S(1)}, u32[]{:S(2)}, u32[]{:S(2)}) collective-permute-start(bf16[128,1024]{1,0:T(8,128)(2,1)S(1)} %slice.20), channel_id=1, source_target_pairs={{0,16},{16,0},{1,17},{17,1},{2,18},{18,2},{3,19},{19,3},{4,20},{20... | collective-permute-start | bytes 786440 | tf_op jit(solution)/shard_map/ppermute | solution.py:338
  45.8 13.1 %collective-permute-start.21 = (bf16[576,128]{1,0:T(8,128)(2,1)S(1)}, bf16[576,128]{1,0:T(8,128)(2,1)S(1)}, u32[]{:S(2)}, u32[]{:S(2)}) collective-permute-start(bf16[576,128]{1,0:T(8,128)(2,1)S(1)} %get-tuple-element.204), channel_id=1, source_target_pairs={{0,8},{1,9},{2,10},{3,11},{4,12},{5,13},{6,14},{7,15},{8,0},{9,1},... | collective-permute-start | bytes 442376 | tf_op jit(solution)/shard_map/ppermute | solution.py:329
  47.8 10.9 %collective-permute-start.17 = (bf16[128,1024]{1,0:T(8,128)(2,1)S(1)}, bf16[128,1024]{1,0:T(8,128)(2,1)S(1)}, u32[]{:S(2)}, u32[]{:S(2)}) collective-permute-start(bf16[128,1024]{1,0:T(8,128)(2,1)S(1)} %slice.22), channel_id=1, source_target_pairs={{0,16},{16,0},{1,17},{17,1},{2,18},{18,2},{3,19},{19,3},{4,20},{20... | collective-permute-start | bytes 786440 | tf_op jit(solution)/shard_map/ppermute | solution.py:338
  53.1 7.7 %collective-permute-start.20 = (bf16[576,128]{1,0:T(8,128)(2,1)S(1)}, bf16[576,128]{1,0:T(8,128)(2,1)S(1)}, u32[]{:S(2)}, u32[]{:S(2)}) collective-permute-start(bf16[576,128]{1,0:T(8,128)(2,1)S(1)} %get-tuple-element.203), channel_id=1, source_target_pairs={{0,4},{1,5},{2,6},{3,7},{4,8},{5,9},{6,10},{7,11},{8,12},{9,13},{1... | collective-permute-start | bytes 442376 | tf_op jit(solution)/shard_map/ppermute | solution.py:329
  56.7 9.8 %collective-permute-start.19 = (bf16[128,1024]{1,0:T(8,128)(2,1)S(1)}, bf16[128,1024]{1,0:T(8,128)(2,1)S(1)}, u32[]{:S(2)}, u32[]{:S(2)}) collective-permute-start(bf16[128,1024]{1,0:T(8,128)(2,1)S(1)} %slice.23), channel_id=1, source_target_pairs={{0,16},{16,0},{1,17},{17,1},{2,18},{18,2},{3,19},{19,3},{4,20},{20... | collective-permute-start | bytes 786440 | tf_op jit(solution)/shard_map/ppermute | solution.py:338
  61.6 5.0 %collective-permute-start.22 = (f32[256,128]{1,0:T(8,128)S(1)}, f32[256,128]{1,0:T(8,128)S(1)}, u32[]{:S(2)}, u32[]{:S(2)}) collective-permute-start(f32[256,128]{1,0:T(8,128)S(1)} %get-tuple-element.212.refs_0_), channel_id=1, source_target_pairs={{0,2},{1,3},{2,0},{3,1},{4,6},{5,7},{6,4},{7,5},{8,10},{9,11},{10,... | collective-permute-start | bytes 393224 | tf_op jit(solution)/shard_map/ppermute | solution.py:332
  62.1 4.5 %collective-permute-start.18 = (bf16[512,1024]{1,0:T(8,128)(2,1)S(1)}, bf16[512,1024]{1,0:T(8,128)(2,1)S(1)}, u32[]{:S(2)}, u32[]{:S(2)}) collective-permute-start(bf16[512,1024]{1,0:T(8,128)(2,1)S(1)} %pack_3.1), channel_id=1, source_target_pairs={{0,1},{1,0},{2,3},{3,2},{4,5},{5,4},{6,7},{7,6},{8,9},{9,8},{10,11... | collective-permute-start | bytes 3145736 | tf_op jit(solution)/shard_map/ppermute | solution.py:335
  66.6 3.9 %collective-permute-start.25 = (f32[512,128]{1,0:T(8,128)S(1)}, f32[512,128]{1,0:T(8,128)S(1)}, u32[]{:S(2)}, u32[]{:S(2)}) collective-permute-start(f32[512,128]{1,0:T(8,128)S(1)} %pack_up.1.mine), channel_id=1, source_target_pairs={{0,1},{1,0},{2,3},{3,2},{4,5},{5,4},{6,7},{7,6},{8,9},{9,8},{10,11... | collective-permute-start | bytes 786440 | tf_op jit(solution)/shard_map/ppermute | solution.py:335
  (9 other events, 34.8 us)

commit v5 on v4

--- a/solution.py
+++ b/solution.py
@@ -49,7 +49,7 @@
     return values, act.astype(BF16), grad_a, grad_b
 
 
-OTHER_US = dict(plane_1=0, place_up_gradient=2, side_sum=5, pack_0=0, line_sum=0, pack_2=2, pack_up=2, scale_rows=5, gradient_shares=6)
+OTHER_US = dict(plane_1=0, side_sum=5, pack_0=0, line_sum=0, pack_2=2, pack_up=2, scale_rows=5, gradient_shares=6)
 VMEM = pl.BlockSpec(memory_space=pltpu.VMEM)
 SMEM = pl.BlockSpec(memory_space=pltpu.SMEM)
 ANY = pl.BlockSpec(memory_space=pl.ANY)
@@ -200,7 +200,7 @@
     quarter[...] = 2.0 * total[rows:]
 
 
-def place_b_body(mine, core, out):
+def place_b(mine, core, out):
     _, y, c, _ = place()
     ranks = out.shape[0]
     half = ranks // 2
@@ -281,18 +281,38 @@
     return pl.multiple_of(within, BLOCK), pl.multiple_of(zz * 4 * rows + within, BLOCK)
 
 
-def last_body(k, rows, i, tok, cot, spread, down, weight, total, _, act, out, block, sem):
+def last_body(k, rows, i, tok, cot, spread, down, weight, total, *refs):
+    if i == 0:
+        _, act, out, block, sems = refs
+    else:
+        both, core_up, _, act, out, grad_b, block, values, placed, sems = refs
     z, y, c, x = place()
     kept = weight.shape[0]
     start = late_rows(k, rows, i, x, z, y, c)[1]
+    copies = []
+
+    def send(source, target):
+        copies.append(pltpu.make_async_copy(source, target, sems.at[len(copies)]))
+        copies[-1].start()
+
+    if i == 1:
+        place_b(both, core_up, placed)
+        send(placed, grad_b)
     back = reduce_over_rows(cot[...], weight[...])
     back += reduce_over_rows(spread[...], down[i])
     block[...] = back.astype(BF16)
-    copy = pltpu.make_async_copy(block, act.at[:, pl.ds(start, kept)], sem)
-    copy.start()
-    forward = total[...] + jnp.dot(tok[i], weight[...], preferred_element_type=F32)
-    out[...] = forward.astype(out.dtype)
-    copy.wait()
+    send(block, act.at[:, pl.ds(start, kept)])
+    if i == 0:
+        out[...] = total[...] + jnp.dot(tok[i], weight[...], preferred_element_type=F32)
+    else:
+        step = weight.shape[1] // 2
+        for at in range(0, weight.shape[1], step):
+            here = pl.ds(at, step)
+            forward = jnp.dot(tok[i], weight[:, here], preferred_element_type=F32)
+            values[:, here] = (total[:, here] + forward).astype(BF16)
+            send(values.at[:, here], out.at[:, here])
+    for copy in copies:
+        copy.wait()
 
 
 def cut_body(ref, out):
@@ -412,16 +432,24 @@
             parts,
         )
 
-    def last_rows(i, weight, state, saved, spread):
+    def last_rows(i, weight, state, saved, spread, *gradient):
+        kinds = [struct((count, width), BF16)]
+        scratch = [pltpu.VMEM((count, kept), BF16)]
+        if i == 0:
+            kinds += [struct((count, columns), F32)]
+        else:
+            kinds += [struct((count, columns), BF16), struct((ranks, columns), F32)]
+            scratch += [pltpu.VMEM((count, columns), BF16), pltpu.VMEM((ranks, columns), F32)]
+        operands = [saved[0], cotangent, spread, saved[1], weight, state[1], *gradient, state[0]]
         return kernel(
             functools.partial(last_body, planes - 1, rows, i),
             f"last_rows_{i}",
-            [struct((count, width), BF16), struct((count, columns), (F32, BF16)[i])],
-            [VMEM] * 6 + [HBM],
-            [HBM, VMEM],
-            [saved[0], cotangent, spread, saved[1], weight, state[1], state[0]],
-            scratch=[pltpu.VMEM((count, kept), BF16), pltpu.SemaphoreType.DMA],
-            alias={6: 0},
+            kinds,
+            [VMEM] * (len(operands) - 1) + [HBM],
+            [HBM, VMEM] if i == 0 else [HBM] * 3,
+            operands,
+            scratch=scratch + [pltpu.SemaphoreType.DMA((1 if i == 0 else 4,))],
+            alias={len(operands) - 1: 0},
         )
 
     def cut(name, v):
@@ -522,32 +550,20 @@
     c2, spread = hold(c2, spread)
     act, acc = plane(2, [z2, y2, x2a, x2b], [c2], (act, acc), spread)
     acc, spread = hold(acc, spread)
-    side_up, spread = hold(side_up, spread)
-    x3b, spread = hold(x3b, spread)
-    c3b = over_core(x3b)
     c3a, spread = hold(c3a, spread)
+    act, acc, *saved = plane(3, [z3, y3, x3a], [c3a], (act, acc), spread)
+    acc, spread = hold(acc, spread)
     side_up, spread = hold(side_up, spread)
     both = pack("pack_up", quarter, side_up)
     both, spread = hold(both, spread)
     core_up = over_core(both)
-    c3a, spread = hold(c3a, spread)
-    act, acc, *saved = plane(3, [z3, y3, x3a], [c3a], (act, acc), spread)
+    x3b, spread = hold(x3b, spread)
+    c3b = over_core(x3b)
+    act, acc = last_rows(0, x3b, (act, acc), saved, spread)
     acc, spread = hold(acc, spread)
     core_up, spread = hold(core_up, spread)
-    grad_b = kernel(
-        place_b_body,
-        "place_up_gradient",
-        struct((ranks, columns), F32),
-        [VMEM] * 2,
-        VMEM,
-        (both, core_up),
-    )
-    x3b, spread = hold(x3b, spread)
-    act, acc = last_rows(0, x3b, (act, acc), saved, spread)
-    acc, spread = hold(acc, spread)
     c3b, spread = hold(c3b, spread)
-    act, acc = last_rows(1, c3b, (act, acc), saved, spread)
-    values = acc
+    act, values, grad_b = last_rows(1, c3b, (act, acc), saved, spread, both, core_up)
     return values, act, grad_a, grad_b
 
 

time: 74.9 us -> 72.6 us (0.969)
  Pallas kernels: 24.8 us -> 23.5 us
  waiting for transfers between devices: 22.3 us -> 21.2 us
    pallas_call x18 -> x17, Pallas kernels: 24.8 us -> 23.5 us  [kernel(): pl.pallas_call(body, name=name, in_specs=in_specs, out_specs=out_specs, o...]
    ppermute x6, waiting for transfers between devices: 4.94 us -> 3.7 us  [over_y(): return lax.ppermute(v, 'seq', swap(n, lambda z, y, c: (z, 1 - y, c)))]
where the time goes in v5:
time: 72.6 us; the launch traced here: 72.4 us
  starting transfers between devices  24.7 us (34%)
  Pallas kernels  23.5 us (32%)
  waiting for transfers between devices  21.2 us (29%)
  local copies, waits for them, and re-layouts  1.9 us (3%)
  between operations  1.09 us (2%)
    pallas_call x17, Pallas kernels, kernel(): pl.pallas_call(body, name=name, in_specs=in_specs, out_specs=out_specs, o...  23.5 us
    ppermute x7, starting transfers between devices, over_x(): return lax.ppermute(v, 'groups', [(0, 1), (1, 0)])  9.77 us
    ppermute x7, waiting for transfers between devices, over_x(): return lax.ppermute(v, 'groups', [(0, 1), (1, 0)])  9.72 us
    ppermute x6, starting transfers between devices, over_z(): return lax.ppermute(v, 'seq', swap(n, lambda z, y, c: (z + by, y, c)))  7.99 us
    ppermute x6, waiting for transfers between devices, over_z(): return lax.ppermute(v, 'seq', swap(n, lambda z, y, c: (z + by, y, c)))  7.59 us
    ppermute x6, starting transfers between devices, over_y(): return lax.ppermute(v, 'seq', swap(n, lambda z, y, c: (z, 1 - y, c)))  6.15 us
    ppermute x6, waiting for transfers between devices, over_y(): return lax.ppermute(v, 'seq', swap(n, lambda z, y, c: (z, 1 - y, c)))  3.7 us
    unnamed x14, local copies, waits for them, and re-layouts  1.79 us
  transfers between devices with their start and end apart: 26, of which 10 were waited for; matrix products, arithmetic and copies ran while one was open for 0% of the time, Pallas kernels for 29%

profile of v5, /device:TPU:0, one launch (start us, length us, event | category | flops | bytes accessed | tf_op | source)
XLA Modules:
  0.0 72.4 jit_solution(12936049617217982793)
XLA Ops:
  3.2 3.1 %collective-permute-start = (bf16[192,1024]{1,0:T(8,128)(2,1)S(1)}, bf16[192,1024]{1,0:T(8,128)(2,1)S(1)}, u32[]{:S(2)}, u32[]{:S(2)}) collective-permute-start(bf16[192,1024]{1,0:T(8,128)(2,1)S(1)} %get-tuple-element.124._.refs_0_), channel_id=1, source_target_pairs={{0,4},{1,5},{2,6},{3,7},{4,8},{5,9},{6,10},{7,11},{8,12},{9,13},{1... | collective-permute-start | bytes 1179656 | tf_op jit(solution)/shard_map/ppermute | solution.py:349
  6.3 1.5 %collective-permute-start.5 = (bf16[192,1024]{1,0:T(8,128)(2,1)S(1)}, bf16[192,1024]{1,0:T(8,128)(2,1)S(1)}, u32[]{:S(2)}, u32[]{:S(2)}) collective-permute-start(bf16[192,1024]{1,0:T(8,128)(2,1)S(1)} %get-tuple-element.124._.refs_0_), channel_id=1, source_target_pairs={{0,2},{1,3},{2,0},{3,1},{4,6},{5,7},{6,4},{7,5},{8,10},{9,11},{10,... | collective-permute-start | bytes 1179656 | tf_op jit(solution)/shard_map/ppermute | solution.py:352
  7.9 5.1 %gradient_shares.1 = (bf16[384,128]{1,0:T(8,128)(2,1)S(1)}, bf16[384,128]{1,0:T(8,128)(2,1)S(1)}, f32[4,2,384,128]{3,2,1,0:T(8,128)S(1)}, f32[4,2,384,128]{3,2,1,0:T(8,128)S(1)}) custom-call(bf16[384,5120]{1,0:T(8,128)(2,1)S(1)} %copy-done, s32[1,384]{1,0:T(1,128)S(1)} %broadcast_in_dim.3.idx, bf16[5120,128]{1,0:T(8,128)(2,1)S(1)} %copy-done.1, ...), custom_call_target="tpu_custom_call" | custom-call | flops 6600000000 | bytes 1 | tf_op jit(solution)/shard_map/gradient_shares/pallas_call | solution.py:64
  13.0 4.4 %collective-permute-done.ref.refs_0_ = bf16[192,1024]{1,0:T(8,128)(2,1)S(1)} collective-permute-done((bf16[192,1024]{1,0:T(8,128)(2,1)S(1)}, bf16[192,1024]{1,0:T(8,128)(2,1)S(1)}, u32[]{:S(2)}, u32[]{:S(2)}) %collective-permute-start) | collective-permute-done | bytes 393248 | tf_op jit(solution)/shard_map/ppermute | solution.py:349
  17.4 1.5 %collective-permute-start.2 = (bf16[192,1024]{1,0:T(8,128)(2,1)S(1)}, bf16[192,1024]{1,0:T(8,128)(2,1)S(1)}, u32[]{:S(2)}, u32[]{:S(2)}) collective-permute-start(bf16[192,1024]{1,0:T(8,128)(2,1)S(1)} %collective-permute-done.ref.refs_0_), channel_id=1, source_target_pairs={{0,2},{1,3},{2,0},{3,1},{4,6},{5,7},{6,4},{7,5},{8,10},{9,11},{10,... | collective-permute-start | bytes 1179656 | tf_op jit(solution)/shard_map/ppermute | solution.py:352
  19.0 1.6 %collective-permute-start.3 = (bf16[128,1024]{1,0:T(8,128)(2,1)S(1)}, bf16[128,1024]{1,0:T(8,128)(2,1)S(1)}, u32[]{:S(2)}, u32[]{:S(2)}) collective-permute-start(bf16[128,1024]{1,0:T(8,128)(2,1)S(1)} %cut_1.1), channel_id=1, source_target_pairs={{0,16},{16,0},{1,17},{17,1},{2,18},{18,2},{3,19},{19,3},{4,20},{20... | collective-permute-start | bytes 786440 | tf_op jit(solution)/shard_map/ppermute | solution.py:358
  21.9 6.4 %collective-permute-done.3.refs_2_ = bf16[128,1024]{1,0:T(8,128)(2,1)S(1)} collective-permute-done((bf16[128,1024]{1,0:T(8,128)(2,1)S(1)}, bf16[128,1024]{1,0:T(8,128)(2,1)S(1)}, u32[]{:S(2)}, u32[]{:S(2)}) %collective-permute-start.3) | collective-permute-done | bytes 262176 | tf_op jit(solution)/shard_map/ppermute | solution.py:358
  29.5 1.6 %collective-permute-start.7 = (bf16[128,1024]{1,0:T(8,128)(2,1)S(1)}, bf16[128,1024]{1,0:T(8,128)(2,1)S(1)}, u32[]{:S(2)}, u32[]{:S(2)}) collective-permute-start(bf16[128,1024]{1,0:T(8,128)(2,1)S(1)} %slice.18), channel_id=1, source_target_pairs={{0,16},{16,0},{1,17},{17,1},{2,18},{18,2},{3,19},{19,3},{4,20},{20... | collective-permute-start | bytes 786440 | tf_op jit(solution)/shard_map/ppermute | solution.py:358
  31.2 1.5 %collective-permute-start.16 = (bf16[192,1024]{1,0:T(8,128)(2,1)S(1)}, bf16[192,1024]{1,0:T(8,128)(2,1)S(1)}, u32[]{:S(2)}, u32[]{:S(2)}) collective-permute-start(bf16[192,1024]{1,0:T(8,128)(2,1)S(1)} %collective-permute-done.1.refs_0_), channel_id=1, source_target_pairs={{0,2},{1,3},{2,0},{3,1},{4,6},{5,7},{6,4},{7,5},{8,10},{9,11},{10,... | collective-permute-start | bytes 1179656 | tf_op jit(solution)/shard_map/ppermute | solution.py:352
  32.7 1.2 %collective-permute-done.8.refs_3_ = bf16[128,1024]{1,0:T(8,128)(2,1)S(1)} collective-permute-done((bf16[128,1024]{1,0:T(8,128)(2,1)S(1)}, bf16[128,1024]{1,0:T(8,128)(2,1)S(1)}, u32[]{:S(2)}, u32[]{:S(2)}) %collective-permute-start.8) | collective-permute-done | bytes 262176 | tf_op jit(solution)/shard_map/ppermute | solution.py:358
  33.9 1.5 %collective-permute-start.14 = (bf16[128,1024]{1,0:T(8,128)(2,1)S(1)}, bf16[128,1024]{1,0:T(8,128)(2,1)S(1)}, u32[]{:S(2)}, u32[]{:S(2)}) collective-permute-start(bf16[128,1024]{1,0:T(8,128)(2,1)S(1)} %slice.21), channel_id=1, source_target_pairs={{0,16},{16,0},{1,17},{17,1},{2,18},{18,2},{3,19},{19,3},{4,20},{20... | collective-permute-start | bytes 786440 | tf_op jit(solution)/shard_map/ppermute | solution.py:358
  35.4 2.5 %collective-permute-done.9.got = bf16[4,384,128]{2,1,0:T(8,128)(2,1)S(1)} collective-permute-done((bf16[4,384,128]{2,1,0:T(8,128)(2,1)S(1)}, bf16[4,384,128]{2,1,0:T(8,128)(2,1)S(1)}, u32[]{:S(2)}, u32[]{:S(2)}) %collective-permute-start.9) | collective-permute-done | bytes 393248 | tf_op jit(solution)/shard_map/ppermute | solution.py:352
  38.0 1.5 %collective-permute-done.7.refs_3_ = bf16[128,1024]{1,0:T(8,128)(2,1)S(1)} collective-permute-done((bf16[128,1024]{1,0:T(8,128)(2,1)S(1)}, bf16[128,1024]{1,0:T(8,128)(2,1)S(1)}, u32[]{:S(2)}, u32[]{:S(2)}) %collective-permute-start.7) | collective-permute-done | bytes 262176 | tf_op jit(solution)/shard_map/ppermute | solution.py:358
  39.7 3.9 %collective-permute-start.15 = (bf16[576,128]{1,0:T(8,128)(2,1)S(1)}, bf16[576,128]{1,0:T(8,128)(2,1)S(1)}, u32[]{:S(2)}, u32[]{:S(2)}) collective-permute-start(bf16[576,128]{1,0:T(8,128)(2,1)S(1)} %get-tuple-element.170), channel_id=1, source_target_pairs={{0,12},{1,13},{2,14},{3,15},{4,0},{5,1},{6,2},{7,3},{8,4},{9,5},{1... | collective-permute-start | bytes 442376 | tf_op jit(solution)/shard_map/ppermute | solution.py:349
  44.3 1.6 %collective-permute-start.11 = (bf16[128,1024]{1,0:T(8,128)(2,1)S(1)}, bf16[128,1024]{1,0:T(8,128)(2,1)S(1)}, u32[]{:S(2)}, u32[]{:S(2)}) collective-permute-start(bf16[128,1024]{1,0:T(8,128)(2,1)S(1)} %slice.20), channel_id=1, source_target_pairs={{0,16},{16,0},{1,17},{17,1},{2,18},{18,2},{3,19},{19,3},{4,20},{20... | collective-permute-start | bytes 786440 | tf_op jit(solution)/shard_map/ppermute | solution.py:358
  46.5 1.2 %collective-permute-done.15.r3 = bf16[576,128]{1,0:T(8,128)(2,1)S(1)} collective-permute-done((bf16[576,128]{1,0:T(8,128)(2,1)S(1)}, bf16[576,128]{1,0:T(8,128)(2,1)S(1)}, u32[]{:S(2)}, u32[]{:S(2)}) %collective-permute-start.15) | collective-permute-done | bytes 147488 | tf_op jit(solution)/shard_map/ppermute | solution.py:349
  47.8 1.6 %collective-permute-start.17 = (bf16[128,1024]{1,0:T(8,128)(2,1)S(1)}, bf16[128,1024]{1,0:T(8,128)(2,1)S(1)}, u32[]{:S(2)}, u32[]{:S(2)}) collective-permute-start(bf16[128,1024]{1,0:T(8,128)(2,1)S(1)} %slice.22), channel_id=1, source_target_pairs={{0,16},{16,0},{1,17},{17,1},{2,18},{18,2},{3,19},{19,3},{4,20},{20... | collective-permute-start | bytes 786440 | tf_op jit(solution)/shard_map/ppermute | solution.py:358
  49.3 3.8 %plane_0.1 = (bf16[384,5120]{1,0:T(8,128)(2,1)}, f32[384,1024]{1,0:T(8,128)S(1)}) custom-call(bf16[384,5120]{1,0:T(8,128)(2,1)S(1)} %copy-done, bf16[384,1024]{1,0:T(8,128)(2,1)S(1)} %copy-done.2, bf16[384,128]{1,0:T(8,128)(2,1)S(1)} %get-tuple-element.235.spread, bf16[5120,128]{1,0:T(8,128)(2,1)S(1)} %copy-done.1, ...), custom_call_target="tpu_custom_call" | custom-call | flops 22000001024 | bytes 1 | tf_op jit(solution)/shard_map/plane_0/pallas_call | solution.py:64
  53.4 3.2 %plane_1.1 = (bf16[384,5120]{1,0:T(8,128)(2,1)}, f32[384,1024]{1,0:T(8,128)S(1)}) custom-call(bf16[384,5120]{1,0:T(8,128)(2,1)S(1)} %copy-done, bf16[384,1024]{1,0:T(8,128)(2,1)S(1)} %copy-done.2, bf16[384,128]{1,0:T(8,128)(2,1)S(1)} %get-tuple-element.235.spread, bf16[5120,128]{1,0:T(8,128)(2,1)S(1)} %copy-done.1, ...), custom_call_target="tpu_custom_call", output_to_operand_aliasing={{0}: (10, {})} | custom-call | bytes 1 | tf_op jit(solution)/shard_map/plane_1/pallas_call | solution.py:64
  56.7 1.4 %collective-permute-start.22 = (bf16[128,1024]{1,0:T(8,128)(2,1)S(1)}, bf16[128,1024]{1,0:T(8,128)(2,1)S(1)}, u32[]{:S(2)}, u32[]{:S(2)}) collective-permute-start(bf16[128,1024]{1,0:T(8,128)(2,1)S(1)} %slice.23), channel_id=1, source_target_pairs={{0,16},{16,0},{1,17},{17,1},{2,18},{18,2},{3,19},{19,3},{4,20},{20... | collective-permute-start | bytes 786440 | tf_op jit(solution)/shard_map/ppermute | solution.py:358
  58.9 1.9 %collective-permute-done.20.r1 = bf16[576,128]{1,0:T(8,128)(2,1)S(1)} collective-permute-done((bf16[576,128]{1,0:T(8,128)(2,1)S(1)}, bf16[576,128]{1,0:T(8,128)(2,1)S(1)}, u32[]{:S(2)}, u32[]{:S(2)}) %collective-permute-start.20) | collective-permute-done | bytes 147488 | tf_op jit(solution)/shard_map/ppermute | solution.py:349
  62.1 3.2 %plane_2.1 = (bf16[384,5120]{1,0:T(8,128)(2,1)}, f32[384,1024]{1,0:T(8,128)S(1)}) custom-call(bf16[384,5120]{1,0:T(8,128)(2,1)S(1)} %copy-done, bf16[384,1024]{1,0:T(8,128)(2,1)S(1)} %copy-done.2, bf16[384,128]{1,0:T(8,128)(2,1)S(1)} %get-tuple-element.235.spread, bf16[5120,128]{1,0:T(8,128)(2,1)S(1)} %copy-done.1, ...), custom_call_target="tpu_custom_call", output_to_operand_aliasing={{0}: (10, {})} | custom-call | flops 22000001024 | bytes 1 | tf_op jit(solution)/shard_map/plane_2/pallas_call | solution.py:64
  65.3 3.3 %plane_3.1 = (bf16[384,5120]{1,0:T(8,128)(2,1)}, f32[384,1024]{1,0:T(8,128)S(1)}, bf16[2,384,128]{2,1,0:T(8,128)(2,1)S(1)}, bf16[2,128,128]{2,1,0:T(8,128)(2,1)S(1)}) custom-call(bf16[384,5120]{1,0:T(8,128)(2,1)S(1)} %copy-done, bf16[384,1024]{1,0:T(8,128)(2,1)S(1)} %copy-done.2, ...), custom_call_target="tpu_custom_call", output_to_operand_aliasing={{0}: (9, {})} | custom-call | flops 22000001024 | bytes 1 | tf_op jit(solution)/shard_map/plane_3/pallas_call | solution.py:64
  70.6 1.6 %last_rows_1.1 = (bf16[384,5120]{1,0:T(8,128)(2,1)}, bf16[384,1024]{1,0:T(8,128)(2,1)}, f32[128,1024]{1,0:T(8,128)}) custom-call(bf16[2,384,128]{2,1,0:T(8,128)(2,1)S(1)} %get-tuple-element.219.tok, bf16[384,1024]{1,0:T(8,128)(2,1)S(1)} %copy-done.2, bf16[384,128]{1,0:T(8,128)(2,1)S(1)} %get-tuple-element.235.spread, ...), custom_call_target="tpu_custom_call", output_to_operand_aliasing={{0}: (8, {})} | custom-call | flops 22000001024 | bytes 1 | tf_op jit(solution)/shard_map/last_rows_1/pallas_call | solution.py:64
  (66 shorter events, 11.2 us)
Async XLA Ops:
  3.2 14.2 %collective-permute-start = (bf16[192,1024]{1,0:T(8,128)(2,1)S(1)}, bf16[192,1024]{1,0:T(8,128)(2,1)S(1)}, u32[]{:S(2)}, u32[]{:S(2)}) collective-permute-start(bf16[192,1024]{1,0:T(8,128)(2,1)S(1)} %get-tuple-element.124._.refs_0_), channel_id=1, source_target_pairs={{0,4},{1,5},{2,6},{3,7},{4,8},{5,9},{6,10},{7,11},{8,12},{9,13},{1... | collective-permute-start | bytes 1179656 | tf_op jit(solution)/shard_map/ppermute | solution.py:349
  6.3 12.7 %collective-permute-start.5 = (bf16[192,1024]{1,0:T(8,128)(2,1)S(1)}, bf16[192,1024]{1,0:T(8,128)(2,1)S(1)}, u32[]{:S(2)}, u32[]{:S(2)}) collective-permute-start(bf16[192,1024]{1,0:T(8,128)(2,1)S(1)} %get-tuple-element.124._.refs_0_), channel_id=1, source_target_pairs={{0,2},{1,3},{2,0},{3,1},{4,6},{5,7},{6,4},{7,5},{8,10},{9,11},{10,... | collective-permute-start | bytes 1179656 | tf_op jit(solution)/shard_map/ppermute | solution.py:352
  12.9 7.6 %collective-permute-start.4 = (f32[4,2,384,128]{3,2,1,0:T(8,128)S(1)}, f32[4,2,384,128]{3,2,1,0:T(8,128)S(1)}, u32[]{:S(2)}, u32[]{:S(2)}) collective-permute-start(f32[4,2,384,128]{3,2,1,0:T(8,128)S(1)} %get-tuple-element.131), channel_id=1, source_target_pairs={{0,1},{1,0},{2,3},{3,2},{4,5},{5,4},{6,7},{7,6},{8,9},{9,8},{10,11... | collective-permute-start | bytes 4718600 | tf_op jit(solution)/shard_map/ppermute | solution.py:355
  17.4 12.1 %collective-permute-start.2 = (bf16[192,1024]{1,0:T(8,128)(2,1)S(1)}, bf16[192,1024]{1,0:T(8,128)(2,1)S(1)}, u32[]{:S(2)}, u32[]{:S(2)}) collective-permute-start(bf16[192,1024]{1,0:T(8,128)(2,1)S(1)} %collective-permute-done.ref.refs_0_), channel_id=1, source_target_pairs={{0,2},{1,3},{2,0},{3,1},{4,6},{5,7},{6,4},{7,5},{8,10},{9,11},{10,... | collective-permute-start | bytes 1179656 | tf_op jit(solution)/shard_map/ppermute | solution.py:352
  19.0 12.1 %collective-permute-start.1 = (bf16[192,1024]{1,0:T(8,128)(2,1)S(1)}, bf16[192,1024]{1,0:T(8,128)(2,1)S(1)}, u32[]{:S(2)}, u32[]{:S(2)}) collective-permute-start(bf16[192,1024]{1,0:T(8,128)(2,1)S(1)} %collective-permute-done.ref.refs_0_), channel_id=1, source_target_pairs={{0,4},{1,5},{2,6},{3,7},{4,8},{5,9},{6,10},{7,11},{8,12},{9,13},{1... | collective-permute-start | bytes 1179656 | tf_op jit(solution)/shard_map/ppermute | solution.py:349
  19.0 9.3 %collective-permute-start.3 = (bf16[128,1024]{1,0:T(8,128)(2,1)S(1)}, bf16[128,1024]{1,0:T(8,128)(2,1)S(1)}, u32[]{:S(2)}, u32[]{:S(2)}) collective-permute-start(bf16[128,1024]{1,0:T(8,128)(2,1)S(1)} %cut_1.1), channel_id=1, source_target_pairs={{0,16},{16,0},{1,17},{17,1},{2,18},{18,2},{3,19},{19,3},{4,20},{20... | collective-permute-start | bytes 786440 | tf_op jit(solution)/shard_map/ppermute | solution.py:358
  20.7 17.2 %collective-permute-start.9 = (bf16[4,384,128]{2,1,0:T(8,128)(2,1)S(1)}, bf16[4,384,128]{2,1,0:T(8,128)(2,1)S(1)}, u32[]{:S(2)}, u32[]{:S(2)}) collective-permute-start(bf16[4,384,128]{2,1,0:T(8,128)(2,1)S(1)} %get-tuple-element.147), channel_id=1, source_target_pairs={{0,2},{1,3},{2,0},{3,1},{4,6},{5,7},{6,4},{7,5},{8,10},{9,11},{10,... | collective-permute-start | bytes 1179656 | tf_op jit(solution)/shard_map/ppermute | solution.py:352
  21.3 12.6 %collective-permute-start.8 = (bf16[128,1024]{1,0:T(8,128)(2,1)S(1)}, bf16[128,1024]{1,0:T(8,128)(2,1)S(1)}, u32[]{:S(2)}, u32[]{:S(2)}) collective-permute-start(bf16[128,1024]{1,0:T(8,128)(2,1)S(1)} %slice.19), channel_id=1, source_target_pairs={{0,16},{16,0},{1,17},{17,1},{2,18},{18,2},{3,19},{19,3},{4,20},{20... | collective-permute-start | bytes 786440 | tf_op jit(solution)/shard_map/ppermute | solution.py:358
  29.5 10.0 %collective-permute-start.7 = (bf16[128,1024]{1,0:T(8,128)(2,1)S(1)}, bf16[128,1024]{1,0:T(8,128)(2,1)S(1)}, u32[]{:S(2)}, u32[]{:S(2)}) collective-permute-start(bf16[128,1024]{1,0:T(8,128)(2,1)S(1)} %slice.18), channel_id=1, source_target_pairs={{0,16},{16,0},{1,17},{17,1},{2,18},{18,2},{3,19},{19,3},{4,20},{20... | collective-permute-start | bytes 786440 | tf_op jit(solution)/shard_map/ppermute | solution.py:358
  31.1 12.6 %collective-permute-start.6 = (bf16[192,1024]{1,0:T(8,128)(2,1)S(1)}, bf16[192,1024]{1,0:T(8,128)(2,1)S(1)}, u32[]{:S(2)}, u32[]{:S(2)}) collective-permute-start(bf16[192,1024]{1,0:T(8,128)(2,1)S(1)} %collective-permute-done.1.refs_0_), channel_id=1, source_target_pairs={{0,4},{1,5},{2,6},{3,7},{4,8},{5,9},{6,10},{7,11},{8,12},{9,13},{1... | collective-permute-start | bytes 1179656 | tf_op jit(solution)/shard_map/ppermute | solution.py:349
  31.2 14.6 %collective-permute-start.16 = (bf16[192,1024]{1,0:T(8,128)(2,1)S(1)}, bf16[192,1024]{1,0:T(8,128)(2,1)S(1)}, u32[]{:S(2)}, u32[]{:S(2)}) collective-permute-start(bf16[192,1024]{1,0:T(8,128)(2,1)S(1)} %collective-permute-done.1.refs_0_), channel_id=1, source_target_pairs={{0,2},{1,3},{2,0},{3,1},{4,6},{5,7},{6,4},{7,5},{8,10},{9,11},{10,... | collective-permute-start | bytes 1179656 | tf_op jit(solution)/shard_map/ppermute | solution.py:352
  33.9 10.4 %collective-permute-start.14 = (bf16[128,1024]{1,0:T(8,128)(2,1)S(1)}, bf16[128,1024]{1,0:T(8,128)(2,1)S(1)}, u32[]{:S(2)}, u32[]{:S(2)}) collective-permute-start(bf16[128,1024]{1,0:T(8,128)(2,1)S(1)} %slice.21), channel_id=1, source_target_pairs={{0,16},{16,0},{1,17},{17,1},{2,18},{18,2},{3,19},{19,3},{4,20},{20... | collective-permute-start | bytes 786440 | tf_op jit(solution)/shard_map/ppermute | solution.py:358
  39.6 4.7 %collective-permute-start.13 = (bf16[640,1024]{1,0:T(8,128)(2,1)S(1)}, bf16[640,1024]{1,0:T(8,128)(2,1)S(1)}, u32[]{:S(2)}, u32[]{:S(2)}) collective-permute-start(bf16[640,1024]{1,0:T(8,128)(2,1)S(1)} %pack_0.1), channel_id=1, source_target_pairs={{0,1},{1,0},{2,3},{3,2},{4,5},{5,4},{6,7},{7,6},{8,9},{9,8},{10,11... | collective-permute-start | bytes 3932168 | tf_op jit(solution)/shard_map/ppermute | solution.py:355
  39.7 8.0 %collective-permute-start.15 = (bf16[576,128]{1,0:T(8,128)(2,1)S(1)}, bf16[576,128]{1,0:T(8,128)(2,1)S(1)}, u32[]{:S(2)}, u32[]{:S(2)}) collective-permute-start(bf16[576,128]{1,0:T(8,128)(2,1)S(1)} %get-tuple-element.170), channel_id=1, source_target_pairs={{0,12},{1,13},{2,14},{3,15},{4,0},{5,1},{6,2},{7,3},{8,4},{9,5},{1... | collective-permute-start | bytes 442376 | tf_op jit(solution)/shard_map/ppermute | solution.py:349
  43.7 13.0 %collective-permute-start.10 = (bf16[192,1024]{1,0:T(8,128)(2,1)S(1)}, bf16[192,1024]{1,0:T(8,128)(2,1)S(1)}, u32[]{:S(2)}, u32[]{:S(2)}) collective-permute-start(bf16[192,1024]{1,0:T(8,128)(2,1)S(1)} %collective-permute-done.6.refs_0_), channel_id=1, source_target_pairs={{0,2},{1,3},{2,0},{3,1},{4,6},{5,7},{6,4},{7,5},{8,10},{9,11},{10,... | collective-permute-start | bytes 1179656 | tf_op jit(solution)/shard_map/ppermute | solution.py:352
  44.3 8.9 %collective-permute-start.12 = (bf16[640,1024]{1,0:T(8,128)(2,1)S(1)}, bf16[640,1024]{1,0:T(8,128)(2,1)S(1)}, u32[]{:S(2)}, u32[]{:S(2)}) collective-permute-start(bf16[640,1024]{1,0:T(8,128)(2,1)S(1)} %pack_1.1), channel_id=1, source_target_pairs={{0,1},{1,0},{2,3},{3,2},{4,5},{5,4},{6,7},{7,6},{8,9},{9,8},{10,11... | collective-permute-start | bytes 3932168 | tf_op jit(solution)/shard_map/ppermute | solution.py:355
  44.3 12.4 %collective-permute-start.11 = (bf16[128,1024]{1,0:T(8,128)(2,1)S(1)}, bf16[128,1024]{1,0:T(8,128)(2,1)S(1)}, u32[]{:S(2)}, u32[]{:S(2)}) collective-permute-start(bf16[128,1024]{1,0:T(8,128)(2,1)S(1)} %slice.20), channel_id=1, source_target_pairs={{0,16},{16,0},{1,17},{17,1},{2,18},{18,2},{3,19},{19,3},{4,20},{20... | collective-permute-start | bytes 786440 | tf_op jit(solution)/shard_map/ppermute | solution.py:358
  45.8 13.1 %collective-permute-start.21 = (bf16[576,128]{1,0:T(8,128)(2,1)S(1)}, bf16[576,128]{1,0:T(8,128)(2,1)S(1)}, u32[]{:S(2)}, u32[]{:S(2)}) collective-permute-start(bf16[576,128]{1,0:T(8,128)(2,1)S(1)} %get-tuple-element.200), channel_id=1, source_target_pairs={{0,8},{1,9},{2,10},{3,11},{4,12},{5,13},{6,14},{7,15},{8,0},{9,1},... | collective-permute-start | bytes 442376 | tf_op jit(solution)/shard_map/ppermute | solution.py:349
  47.8 10.9 %collective-permute-start.17 = (bf16[128,1024]{1,0:T(8,128)(2,1)S(1)}, bf16[128,1024]{1,0:T(8,128)(2,1)S(1)}, u32[]{:S(2)}, u32[]{:S(2)}) collective-permute-start(bf16[128,1024]{1,0:T(8,128)(2,1)S(1)} %slice.22), channel_id=1, source_target_pairs={{0,16},{16,0},{1,17},{17,1},{2,18},{18,2},{3,19},{19,3},{4,20},{20... | collective-permute-start | bytes 786440 | tf_op jit(solution)/shard_map/ppermute | solution.py:358
  53.1 7.7 %collective-permute-start.20 = (bf16[576,128]{1,0:T(8,128)(2,1)S(1)}, bf16[576,128]{1,0:T(8,128)(2,1)S(1)}, u32[]{:S(2)}, u32[]{:S(2)}) collective-permute-start(bf16[576,128]{1,0:T(8,128)(2,1)S(1)} %get-tuple-element.199), channel_id=1, source_target_pairs={{0,4},{1,5},{2,6},{3,7},{4,8},{5,9},{6,10},{7,11},{8,12},{9,13},{1... | collective-permute-start | bytes 442376 | tf_op jit(solution)/shard_map/ppermute | solution.py:349
  56.7 12.0 %collective-permute-start.22 = (bf16[128,1024]{1,0:T(8,128)(2,1)S(1)}, bf16[128,1024]{1,0:T(8,128)(2,1)S(1)}, u32[]{:S(2)}, u32[]{:S(2)}) collective-permute-start(bf16[128,1024]{1,0:T(8,128)(2,1)S(1)} %slice.23), channel_id=1, source_target_pairs={{0,16},{16,0},{1,17},{17,1},{2,18},{18,2},{3,19},{19,3},{4,20},{20... | collective-permute-start | bytes 786440 | tf_op jit(solution)/shard_map/ppermute | solution.py:358
  58.8 3.3 %collective-permute-start.19 = (bf16[640,1024]{1,0:T(8,128)(2,1)S(1)}, bf16[640,1024]{1,0:T(8,128)(2,1)S(1)}, u32[]{:S(2)}, u32[]{:S(2)}) collective-permute-start(bf16[640,1024]{1,0:T(8,128)(2,1)S(1)} %pack_2.1), channel_id=1, source_target_pairs={{0,1},{1,0},{2,3},{3,2},{4,5},{5,4},{6,7},{7,6},{8,9},{9,8},{10,11... | collective-permute-start | bytes 3932168 | tf_op jit(solution)/shard_map/ppermute | solution.py:355
  61.6 3.7 %collective-permute-start.18 = (bf16[512,1024]{1,0:T(8,128)(2,1)S(1)}, bf16[512,1024]{1,0:T(8,128)(2,1)S(1)}, u32[]{:S(2)}, u32[]{:S(2)}) collective-permute-start(bf16[512,1024]{1,0:T(8,128)(2,1)S(1)} %pack_3.1), channel_id=1, source_target_pairs={{0,1},{1,0},{2,3},{3,2},{4,5},{5,4},{6,7},{7,6},{8,9},{9,8},{10,11... | collective-permute-start | bytes 3145736 | tf_op jit(solution)/shard_map/ppermute | solution.py:355
  61.6 7.0 %collective-permute-start.23 = (f32[256,128]{1,0:T(8,128)S(1)}, f32[256,128]{1,0:T(8,128)S(1)}, u32[]{:S(2)}, u32[]{:S(2)}) collective-permute-start(f32[256,128]{1,0:T(8,128)S(1)} %get-tuple-element.220.refs_0_), channel_id=1, source_target_pairs={{0,2},{1,3},{2,0},{3,1},{4,6},{5,7},{6,4},{7,5},{8,10},{9,11},{10,... | collective-permute-start | bytes 393224 | tf_op jit(solution)/shard_map/ppermute | solution.py:352
  (9 other events, 32.4 us)

commit v6 on v5

--- a/solution.py
+++ b/solution.py
@@ -517,7 +517,7 @@
     c0, spread = hold(c0, spread)
     y2, spread = hold(y2, spread)
     x2b = over_x(y2[:kept])
-    line_3, spread = hold(line_3, spread)
+    line_2, spread = hold(line_2, spread)
     c0, spread = hold(c0, spread)
     act, acc = plane(0, [p0, y0, rest, x0], [c0], None, spread)
     acc, spread = hold(acc, spread)
@@ -535,7 +535,7 @@
     pack_3 = pack("pack_3", z3, y3, x3a)
     pack_3, spread = hold(pack_3, spread)
     c3a = over_core(pack_3)
-    line_2, spread = hold(line_2, spread)
+    line_3, spread = hold(line_3, spread)
     line_1, spread = hold(line_1, spread)
     grad_a, quarter = kernel(
         line_sum_body,

time: 72.6 us -> 77.5 us (1.067)
  starting transfers between devices: 24.7 us -> 28.2 us
  waiting for transfers between devices: 21.2 us -> 22.7 us
    ppermute x6, starting transfers between devices: 7.99 us -> 12.3 us  [over_z(): return lax.ppermute(v, 'seq', swap(n, lambda z, y, c: (z + by, y, c)))]
    ppermute x6, waiting for transfers between devices: 7.59 us -> 9.34 us  [over_z(): return lax.ppermute(v, 'seq', swap(n, lambda z, y, c: (z + by, y, c)))]
    ppermute x7, starting transfers between devices: 9.77 us -> 8.88 us  [over_x(): return lax.ppermute(v, 'groups', [(0, 1), (1, 0)])]
  transfers between devices with their start and end apart: 26 -> 26, of which waited for: 10 -> 11; matrix products, arithmetic and copies ran while one was open for 0% -> 0% of each run, Pallas kernels for 29% -> 27%
where the time goes in v6:
time: 77.5 us; the launch traced here: 77.3 us
  starting transfers between devices  28.2 us (36%)
  Pallas kernels  23.4 us (30%)
  waiting for transfers between devices  22.7 us (29%)
  local copies, waits for them, and re-layouts  1.9 us (2%)
  between operations  1.08 us (1%)
    pallas_call x17, Pallas kernels, kernel(): pl.pallas_call(body, name=name, in_specs=in_specs, out_specs=out_specs, o...  23.4 us
    ppermute x6, starting transfers between devices, over_z(): return lax.ppermute(v, 'seq', swap(n, lambda z, y, c: (z + by, y, c)))  12.3 us
    ppermute x6, waiting for transfers between devices, over_z(): return lax.ppermute(v, 'seq', swap(n, lambda z, y, c: (z + by, y, c)))  9.34 us
    ppermute x7, waiting for transfers between devices, over_x(): return lax.ppermute(v, 'groups', [(0, 1), (1, 0)])  9.29 us
    ppermute x7, starting transfers between devices, over_x(): return lax.ppermute(v, 'groups', [(0, 1), (1, 0)])  8.88 us
    ppermute x6, starting transfers between devices, over_y(): return lax.ppermute(v, 'seq', swap(n, lambda z, y, c: (z, 1 - y, c)))  6.16 us
    ppermute x6, waiting for transfers between devices, over_y(): return lax.ppermute(v, 'seq', swap(n, lambda z, y, c: (z, 1 - y, c)))  3.91 us
    unnamed x14, local copies, waits for them, and re-layouts  1.79 us
  transfers between devices with their start and end apart: 26, of which 11 were waited for; matrix products, arithmetic and copies ran while one was open for 0% of the time, Pallas kernels for 27%

profile of v6, /device:TPU:0, one launch (start us, length us, event | category | flops | bytes accessed | tf_op | source)
XLA Modules:
  0.0 77.3 jit_solution(4501276889989712533)
XLA Ops:
  3.2 3.1 %collective-permute-start = (bf16[192,1024]{1,0:T(8,128)(2,1)S(1)}, bf16[192,1024]{1,0:T(8,128)(2,1)S(1)}, u32[]{:S(2)}, u32[]{:S(2)}) collective-permute-start(bf16[192,1024]{1,0:T(8,128)(2,1)S(1)} %get-tuple-element.124._.refs_0_), channel_id=1, source_target_pairs={{0,4},{1,5},{2,6},{3,7},{4,8},{5,9},{6,10},{7,11},{8,12},{9,13},{1... | collective-permute-start | bytes 1179656 | tf_op jit(solution)/shard_map/ppermute | solution.py:349
  6.3 1.5 %collective-permute-start.5 = (bf16[192,1024]{1,0:T(8,128)(2,1)S(1)}, bf16[192,1024]{1,0:T(8,128)(2,1)S(1)}, u32[]{:S(2)}, u32[]{:S(2)}) collective-permute-start(bf16[192,1024]{1,0:T(8,128)(2,1)S(1)} %get-tuple-element.124._.refs_0_), channel_id=1, source_target_pairs={{0,2},{1,3},{2,0},{3,1},{4,6},{5,7},{6,4},{7,5},{8,10},{9,11},{10,... | collective-permute-start | bytes 1179656 | tf_op jit(solution)/shard_map/ppermute | solution.py:352
  7.9 5.1 %gradient_shares.1 = (bf16[384,128]{1,0:T(8,128)(2,1)S(1)}, bf16[384,128]{1,0:T(8,128)(2,1)S(1)}, f32[4,2,384,128]{3,2,1,0:T(8,128)S(1)}, f32[4,2,384,128]{3,2,1,0:T(8,128)S(1)}) custom-call(bf16[384,5120]{1,0:T(8,128)(2,1)S(1)} %copy-done, s32[1,384]{1,0:T(1,128)S(1)} %broadcast_in_dim.3.idx, bf16[5120,128]{1,0:T(8,128)(2,1)S(1)} %copy-done.1, ...), custom_call_target="tpu_custom_call" | custom-call | flops 6600000000 | bytes 1 | tf_op jit(solution)/shard_map/gradient_shares/pallas_call | solution.py:64
  13.0 4.4 %collective-permute-done.ref.refs_0_ = bf16[192,1024]{1,0:T(8,128)(2,1)S(1)} collective-permute-done((bf16[192,1024]{1,0:T(8,128)(2,1)S(1)}, bf16[192,1024]{1,0:T(8,128)(2,1)S(1)}, u32[]{:S(2)}, u32[]{:S(2)}) %collective-permute-start) | collective-permute-done | bytes 393248 | tf_op jit(solution)/shard_map/ppermute | solution.py:349
  17.4 1.5 %collective-permute-start.2 = (bf16[192,1024]{1,0:T(8,128)(2,1)S(1)}, bf16[192,1024]{1,0:T(8,128)(2,1)S(1)}, u32[]{:S(2)}, u32[]{:S(2)}) collective-permute-start(bf16[192,1024]{1,0:T(8,128)(2,1)S(1)} %collective-permute-done.ref.refs_0_), channel_id=1, source_target_pairs={{0,2},{1,3},{2,0},{3,1},{4,6},{5,7},{6,4},{7,5},{8,10},{9,11},{10,... | collective-permute-start | bytes 1179656 | tf_op jit(solution)/shard_map/ppermute | solution.py:352
  19.0 1.6 %collective-permute-start.3 = (bf16[128,1024]{1,0:T(8,128)(2,1)S(1)}, bf16[128,1024]{1,0:T(8,128)(2,1)S(1)}, u32[]{:S(2)}, u32[]{:S(2)}) collective-permute-start(bf16[128,1024]{1,0:T(8,128)(2,1)S(1)} %cut_1.1), channel_id=1, source_target_pairs={{0,16},{16,0},{1,17},{17,1},{2,18},{18,2},{3,19},{19,3},{4,20},{20... | collective-permute-start | bytes 786440 | tf_op jit(solution)/shard_map/ppermute | solution.py:358
  21.9 6.4 %collective-permute-done.3.refs_2_ = bf16[128,1024]{1,0:T(8,128)(2,1)S(1)} collective-permute-done((bf16[128,1024]{1,0:T(8,128)(2,1)S(1)}, bf16[128,1024]{1,0:T(8,128)(2,1)S(1)}, u32[]{:S(2)}, u32[]{:S(2)}) %collective-permute-start.3) | collective-permute-done | bytes 262176 | tf_op jit(solution)/shard_map/ppermute | solution.py:358
  29.5 1.6 %collective-permute-start.7 = (bf16[128,1024]{1,0:T(8,128)(2,1)S(1)}, bf16[128,1024]{1,0:T(8,128)(2,1)S(1)}, u32[]{:S(2)}, u32[]{:S(2)}) collective-permute-start(bf16[128,1024]{1,0:T(8,128)(2,1)S(1)} %slice.18), channel_id=1, source_target_pairs={{0,16},{16,0},{1,17},{17,1},{2,18},{18,2},{3,19},{19,3},{4,20},{20... | collective-permute-start | bytes 786440 | tf_op jit(solution)/shard_map/ppermute | solution.py:358
  31.2 1.5 %collective-permute-start.16 = (bf16[192,1024]{1,0:T(8,128)(2,1)S(1)}, bf16[192,1024]{1,0:T(8,128)(2,1)S(1)}, u32[]{:S(2)}, u32[]{:S(2)}) collective-permute-start(bf16[192,1024]{1,0:T(8,128)(2,1)S(1)} %collective-permute-done.1.refs_0_), channel_id=1, source_target_pairs={{0,2},{1,3},{2,0},{3,1},{4,6},{5,7},{6,4},{7,5},{8,10},{9,11},{10,... | collective-permute-start | bytes 1179656 | tf_op jit(solution)/shard_map/ppermute | solution.py:352
  33.9 1.5 %collective-permute-start.14 = (bf16[128,1024]{1,0:T(8,128)(2,1)S(1)}, bf16[128,1024]{1,0:T(8,128)(2,1)S(1)}, u32[]{:S(2)}, u32[]{:S(2)}) collective-permute-start(bf16[128,1024]{1,0:T(8,128)(2,1)S(1)} %slice.21), channel_id=1, source_target_pairs={{0,16},{16,0},{1,17},{17,1},{2,18},{18,2},{3,19},{19,3},{4,20},{20... | collective-permute-start | bytes 786440 | tf_op jit(solution)/shard_map/ppermute | solution.py:358
  35.4 2.5 %collective-permute-done.9.got = bf16[4,384,128]{2,1,0:T(8,128)(2,1)S(1)} collective-permute-done((bf16[4,384,128]{2,1,0:T(8,128)(2,1)S(1)}, bf16[4,384,128]{2,1,0:T(8,128)(2,1)S(1)}, u32[]{:S(2)}, u32[]{:S(2)}) %collective-permute-start.9) | collective-permute-done | bytes 393248 | tf_op jit(solution)/shard_map/ppermute | solution.py:352
  38.0 1.5 %collective-permute-done.7.refs_3_ = bf16[128,1024]{1,0:T(8,128)(2,1)S(1)} collective-permute-done((bf16[128,1024]{1,0:T(8,128)(2,1)S(1)}, bf16[128,1024]{1,0:T(8,128)(2,1)S(1)}, u32[]{:S(2)}, u32[]{:S(2)}) %collective-permute-start.7) | collective-permute-done | bytes 262176 | tf_op jit(solution)/shard_map/ppermute | solution.py:358
  39.7 2.4 %collective-permute-start.15 = (bf16[576,128]{1,0:T(8,128)(2,1)S(1)}, bf16[576,128]{1,0:T(8,128)(2,1)S(1)}, u32[]{:S(2)}, u32[]{:S(2)}) collective-permute-start(bf16[576,128]{1,0:T(8,128)(2,1)S(1)} %get-tuple-element.170), channel_id=1, source_target_pairs={{0,8},{1,9},{2,10},{3,11},{4,12},{5,13},{6,14},{7,15},{8,0},{9,1},... | collective-permute-start | bytes 442376 | tf_op jit(solution)/shard_map/ppermute | solution.py:349
  42.9 1.5 %collective-permute-start.11 = (bf16[128,1024]{1,0:T(8,128)(2,1)S(1)}, bf16[128,1024]{1,0:T(8,128)(2,1)S(1)}, u32[]{:S(2)}, u32[]{:S(2)}) collective-permute-start(bf16[128,1024]{1,0:T(8,128)(2,1)S(1)} %slice.20), channel_id=1, source_target_pairs={{0,16},{16,0},{1,17},{17,1},{2,18},{18,2},{3,19},{19,3},{4,20},{20... | collective-permute-start | bytes 786440 | tf_op jit(solution)/shard_map/ppermute | solution.py:358
  44.6 3.5 %collective-permute-start.21 = (bf16[576,128]{1,0:T(8,128)(2,1)S(1)}, bf16[576,128]{1,0:T(8,128)(2,1)S(1)}, u32[]{:S(2)}, u32[]{:S(2)}) collective-permute-start(bf16[576,128]{1,0:T(8,128)(2,1)S(1)} %get-tuple-element.200), channel_id=1, source_target_pairs={{0,12},{1,13},{2,14},{3,15},{4,0},{5,1},{6,2},{7,3},{8,4},{9,5},{1... | collective-permute-start | bytes 442376 | tf_op jit(solution)/shard_map/ppermute | solution.py:349
  48.1 2.4 %collective-permute-done.15.r2 = bf16[576,128]{1,0:T(8,128)(2,1)S(1)} collective-permute-done((bf16[576,128]{1,0:T(8,128)(2,1)S(1)}, bf16[576,128]{1,0:T(8,128)(2,1)S(1)}, u32[]{:S(2)}, u32[]{:S(2)}) %collective-permute-start.15) | collective-permute-done | bytes 147488 | tf_op jit(solution)/shard_map/ppermute | solution.py:349
  50.5 1.6 %collective-permute-start.17 = (bf16[128,1024]{1,0:T(8,128)(2,1)S(1)}, bf16[128,1024]{1,0:T(8,128)(2,1)S(1)}, u32[]{:S(2)}, u32[]{:S(2)}) collective-permute-start(bf16[128,1024]{1,0:T(8,128)(2,1)S(1)} %slice.22), channel_id=1, source_target_pairs={{0,16},{16,0},{1,17},{17,1},{2,18},{18,2},{3,19},{19,3},{4,20},{20... | collective-permute-start | bytes 786440 | tf_op jit(solution)/shard_map/ppermute | solution.py:358
  52.1 3.8 %plane_0.1 = (bf16[384,5120]{1,0:T(8,128)(2,1)}, f32[384,1024]{1,0:T(8,128)S(1)}) custom-call(bf16[384,5120]{1,0:T(8,128)(2,1)S(1)} %copy-done, bf16[384,1024]{1,0:T(8,128)(2,1)S(1)} %copy-done.2, bf16[384,128]{1,0:T(8,128)(2,1)S(1)} %get-tuple-element.235.spread, bf16[5120,128]{1,0:T(8,128)(2,1)S(1)} %copy-done.1, ...), custom_call_target="tpu_custom_call" | custom-call | flops 22000001024 | bytes 1 | tf_op jit(solution)/shard_map/plane_0/pallas_call | solution.py:64
  55.9 3.3 %collective-permute-start.20 = (bf16[576,128]{1,0:T(8,128)(2,1)S(1)}, bf16[576,128]{1,0:T(8,128)(2,1)S(1)}, u32[]{:S(2)}, u32[]{:S(2)}) collective-permute-start(bf16[576,128]{1,0:T(8,128)(2,1)S(1)} %get-tuple-element.199), channel_id=1, source_target_pairs={{0,4},{1,5},{2,6},{3,7},{4,8},{5,9},{6,10},{7,11},{8,12},{9,13},{1... | collective-permute-start | bytes 442376 | tf_op jit(solution)/shard_map/ppermute | solution.py:349
  59.2 3.2 %plane_1.1 = (bf16[384,5120]{1,0:T(8,128)(2,1)}, f32[384,1024]{1,0:T(8,128)S(1)}) custom-call(bf16[384,5120]{1,0:T(8,128)(2,1)S(1)} %copy-done, bf16[384,1024]{1,0:T(8,128)(2,1)S(1)} %copy-done.2, bf16[384,128]{1,0:T(8,128)(2,1)S(1)} %get-tuple-element.235.spread, bf16[5120,128]{1,0:T(8,128)(2,1)S(1)} %copy-done.1, ...), custom_call_target="tpu_custom_call", output_to_operand_aliasing={{0}: (10, {})} | custom-call | bytes 1 | tf_op jit(solution)/shard_map/plane_1/pallas_call | solution.py:64
  63.4 2.5 %collective-permute-done.20.r1 = bf16[576,128]{1,0:T(8,128)(2,1)S(1)} collective-permute-done((bf16[576,128]{1,0:T(8,128)(2,1)S(1)}, bf16[576,128]{1,0:T(8,128)(2,1)S(1)}, u32[]{:S(2)}, u32[]{:S(2)}) %collective-permute-start.20) | collective-permute-done | bytes 147488 | tf_op jit(solution)/shard_map/ppermute | solution.py:349
  67.0 3.2 %plane_2.1 = (bf16[384,5120]{1,0:T(8,128)(2,1)}, f32[384,1024]{1,0:T(8,128)S(1)}) custom-call(bf16[384,5120]{1,0:T(8,128)(2,1)S(1)} %copy-done, bf16[384,1024]{1,0:T(8,128)(2,1)S(1)} %copy-done.2, bf16[384,128]{1,0:T(8,128)(2,1)S(1)} %get-tuple-element.235.spread, bf16[5120,128]{1,0:T(8,128)(2,1)S(1)} %copy-done.1, ...), custom_call_target="tpu_custom_call", output_to_operand_aliasing={{0}: (10, {})} | custom-call | flops 22000001024 | bytes 1 | tf_op jit(solution)/shard_map/plane_2/pallas_call | solution.py:64
  70.3 3.3 %plane_3.1 = (bf16[384,5120]{1,0:T(8,128)(2,1)}, f32[384,1024]{1,0:T(8,128)S(1)}, bf16[2,384,128]{2,1,0:T(8,128)(2,1)S(1)}, bf16[2,128,128]{2,1,0:T(8,128)(2,1)S(1)}) custom-call(bf16[384,5120]{1,0:T(8,128)(2,1)S(1)} %copy-done, bf16[384,1024]{1,0:T(8,128)(2,1)S(1)} %copy-done.2, ...), custom_call_target="tpu_custom_call", output_to_operand_aliasing={{0}: (9, {})} | custom-call | flops 22000001024 | bytes 1 | tf_op jit(solution)/shard_map/plane_3/pallas_call | solution.py:64
  75.6 1.6 %last_rows_1.1 = (bf16[384,5120]{1,0:T(8,128)(2,1)}, bf16[384,1024]{1,0:T(8,128)(2,1)}, f32[128,1024]{1,0:T(8,128)}) custom-call(bf16[2,384,128]{2,1,0:T(8,128)(2,1)S(1)} %get-tuple-element.219.tok, bf16[384,1024]{1,0:T(8,128)(2,1)S(1)} %copy-done.2, bf16[384,128]{1,0:T(8,128)(2,1)S(1)} %get-tuple-element.235.spread, ...), custom_call_target="tpu_custom_call", output_to_operand_aliasing={{0}: (8, {})} | custom-call | flops 22000001024 | bytes 1 | tf_op jit(solution)/shard_map/last_rows_1/pallas_call | solution.py:64
  (66 shorter events, 11.9 us)
Async XLA Ops:
  3.2 14.2 %collective-permute-start = (bf16[192,1024]{1,0:T(8,128)(2,1)S(1)}, bf16[192,1024]{1,0:T(8,128)(2,1)S(1)}, u32[]{:S(2)}, u32[]{:S(2)}) collective-permute-start(bf16[192,1024]{1,0:T(8,128)(2,1)S(1)} %get-tuple-element.124._.refs_0_), channel_id=1, source_target_pairs={{0,4},{1,5},{2,6},{3,7},{4,8},{5,9},{6,10},{7,11},{8,12},{9,13},{1... | collective-permute-start | bytes 1179656 | tf_op jit(solution)/shard_map/ppermute | solution.py:349
  6.3 12.7 %collective-permute-start.5 = (bf16[192,1024]{1,0:T(8,128)(2,1)S(1)}, bf16[192,1024]{1,0:T(8,128)(2,1)S(1)}, u32[]{:S(2)}, u32[]{:S(2)}) collective-permute-start(bf16[192,1024]{1,0:T(8,128)(2,1)S(1)} %get-tuple-element.124._.refs_0_), channel_id=1, source_target_pairs={{0,2},{1,3},{2,0},{3,1},{4,6},{5,7},{6,4},{7,5},{8,10},{9,11},{10,... | collective-permute-start | bytes 1179656 | tf_op jit(solution)/shard_map/ppermute | solution.py:352
  12.9 7.6 %collective-permute-start.4 = (f32[4,2,384,128]{3,2,1,0:T(8,128)S(1)}, f32[4,2,384,128]{3,2,1,0:T(8,128)S(1)}, u32[]{:S(2)}, u32[]{:S(2)}) collective-permute-start(f32[4,2,384,128]{3,2,1,0:T(8,128)S(1)} %get-tuple-element.131), channel_id=1, source_target_pairs={{0,1},{1,0},{2,3},{3,2},{4,5},{5,4},{6,7},{7,6},{8,9},{9,8},{10,11... | collective-permute-start | bytes 4718600 | tf_op jit(solution)/shard_map/ppermute | solution.py:355
  17.4 12.1 %collective-permute-start.2 = (bf16[192,1024]{1,0:T(8,128)(2,1)S(1)}, bf16[192,1024]{1,0:T(8,128)(2,1)S(1)}, u32[]{:S(2)}, u32[]{:S(2)}) collective-permute-start(bf16[192,1024]{1,0:T(8,128)(2,1)S(1)} %collective-permute-done.ref.refs_0_), channel_id=1, source_target_pairs={{0,2},{1,3},{2,0},{3,1},{4,6},{5,7},{6,4},{7,5},{8,10},{9,11},{10,... | collective-permute-start | bytes 1179656 | tf_op jit(solution)/shard_map/ppermute | solution.py:352
  19.0 12.1 %collective-permute-start.1 = (bf16[192,1024]{1,0:T(8,128)(2,1)S(1)}, bf16[192,1024]{1,0:T(8,128)(2,1)S(1)}, u32[]{:S(2)}, u32[]{:S(2)}) collective-permute-start(bf16[192,1024]{1,0:T(8,128)(2,1)S(1)} %collective-permute-done.ref.refs_0_), channel_id=1, source_target_pairs={{0,4},{1,5},{2,6},{3,7},{4,8},{5,9},{6,10},{7,11},{8,12},{9,13},{1... | collective-permute-start | bytes 1179656 | tf_op jit(solution)/shard_map/ppermute | solution.py:349
  19.0 9.3 %collective-permute-start.3 = (bf16[128,1024]{1,0:T(8,128)(2,1)S(1)}, bf16[128,1024]{1,0:T(8,128)(2,1)S(1)}, u32[]{:S(2)}, u32[]{:S(2)}) collective-permute-start(bf16[128,1024]{1,0:T(8,128)(2,1)S(1)} %cut_1.1), channel_id=1, source_target_pairs={{0,16},{16,0},{1,17},{17,1},{2,18},{18,2},{3,19},{19,3},{4,20},{20... | collective-permute-start | bytes 786440 | tf_op jit(solution)/shard_map/ppermute | solution.py:358
  20.7 17.2 %collective-permute-start.9 = (bf16[4,384,128]{2,1,0:T(8,128)(2,1)S(1)}, bf16[4,384,128]{2,1,0:T(8,128)(2,1)S(1)}, u32[]{:S(2)}, u32[]{:S(2)}) collective-permute-start(bf16[4,384,128]{2,1,0:T(8,128)(2,1)S(1)} %get-tuple-element.147), channel_id=1, source_target_pairs={{0,2},{1,3},{2,0},{3,1},{4,6},{5,7},{6,4},{7,5},{8,10},{9,11},{10,... | collective-permute-start | bytes 1179656 | tf_op jit(solution)/shard_map/ppermute | solution.py:352
  21.3 12.6 %collective-permute-start.8 = (bf16[128,1024]{1,0:T(8,128)(2,1)S(1)}, bf16[128,1024]{1,0:T(8,128)(2,1)S(1)}, u32[]{:S(2)}, u32[]{:S(2)}) collective-permute-start(bf16[128,1024]{1,0:T(8,128)(2,1)S(1)} %slice.19), channel_id=1, source_target_pairs={{0,16},{16,0},{1,17},{17,1},{2,18},{18,2},{3,19},{19,3},{4,20},{20... | collective-permute-start | bytes 786440 | tf_op jit(solution)/shard_map/ppermute | solution.py:358
  29.5 10.0 %collective-permute-start.7 = (bf16[128,1024]{1,0:T(8,128)(2,1)S(1)}, bf16[128,1024]{1,0:T(8,128)(2,1)S(1)}, u32[]{:S(2)}, u32[]{:S(2)}) collective-permute-start(bf16[128,1024]{1,0:T(8,128)(2,1)S(1)} %slice.18), channel_id=1, source_target_pairs={{0,16},{16,0},{1,17},{17,1},{2,18},{18,2},{3,19},{19,3},{4,20},{20... | collective-permute-start | bytes 786440 | tf_op jit(solution)/shard_map/ppermute | solution.py:358
  31.1 11.1 %collective-permute-start.6 = (bf16[192,1024]{1,0:T(8,128)(2,1)S(1)}, bf16[192,1024]{1,0:T(8,128)(2,1)S(1)}, u32[]{:S(2)}, u32[]{:S(2)}) collective-permute-start(bf16[192,1024]{1,0:T(8,128)(2,1)S(1)} %collective-permute-done.1.refs_0_), channel_id=1, source_target_pairs={{0,4},{1,5},{2,6},{3,7},{4,8},{5,9},{6,10},{7,11},{8,12},{9,13},{1... | collective-permute-start | bytes 1179656 | tf_op jit(solution)/shard_map/ppermute | solution.py:349
  31.2 13.4 %collective-permute-start.16 = (bf16[192,1024]{1,0:T(8,128)(2,1)S(1)}, bf16[192,1024]{1,0:T(8,128)(2,1)S(1)}, u32[]{:S(2)}, u32[]{:S(2)}) collective-permute-start(bf16[192,1024]{1,0:T(8,128)(2,1)S(1)} %collective-permute-done.1.refs_0_), channel_id=1, source_target_pairs={{0,2},{1,3},{2,0},{3,1},{4,6},{5,7},{6,4},{7,5},{8,10},{9,11},{10,... | collective-permute-start | bytes 1179656 | tf_op jit(solution)/shard_map/ppermute | solution.py:352
  33.9 9.0 %collective-permute-start.14 = (bf16[128,1024]{1,0:T(8,128)(2,1)S(1)}, bf16[128,1024]{1,0:T(8,128)(2,1)S(1)}, u32[]{:S(2)}, u32[]{:S(2)}) collective-permute-start(bf16[128,1024]{1,0:T(8,128)(2,1)S(1)} %slice.21), channel_id=1, source_target_pairs={{0,16},{16,0},{1,17},{17,1},{2,18},{18,2},{3,19},{19,3},{4,20},{20... | collective-permute-start | bytes 786440 | tf_op jit(solution)/shard_map/ppermute | solution.py:358
  39.6 3.3 %collective-permute-start.13 = (bf16[640,1024]{1,0:T(8,128)(2,1)S(1)}, bf16[640,1024]{1,0:T(8,128)(2,1)S(1)}, u32[]{:S(2)}, u32[]{:S(2)}) collective-permute-start(bf16[640,1024]{1,0:T(8,128)(2,1)S(1)} %pack_0.1), channel_id=1, source_target_pairs={{0,1},{1,0},{2,3},{3,2},{4,5},{5,4},{6,7},{7,6},{8,9},{9,8},{10,11... | collective-permute-start | bytes 3932168 | tf_op jit(solution)/shard_map/ppermute | solution.py:355
  39.7 10.8 %collective-permute-start.15 = (bf16[576,128]{1,0:T(8,128)(2,1)S(1)}, bf16[576,128]{1,0:T(8,128)(2,1)S(1)}, u32[]{:S(2)}, u32[]{:S(2)}) collective-permute-start(bf16[576,128]{1,0:T(8,128)(2,1)S(1)} %get-tuple-element.170), channel_id=1, source_target_pairs={{0,8},{1,9},{2,10},{3,11},{4,12},{5,13},{6,14},{7,15},{8,0},{9,1},... | collective-permute-start | bytes 442376 | tf_op jit(solution)/shard_map/ppermute | solution.py:349
  42.2 20.3 %collective-permute-start.10 = (bf16[192,1024]{1,0:T(8,128)(2,1)S(1)}, bf16[192,1024]{1,0:T(8,128)(2,1)S(1)}, u32[]{:S(2)}, u32[]{:S(2)}) collective-permute-start(bf16[192,1024]{1,0:T(8,128)(2,1)S(1)} %collective-permute-done.6.refs_0_), channel_id=1, source_target_pairs={{0,2},{1,3},{2,0},{3,1},{4,6},{5,7},{6,4},{7,5},{8,10},{9,11},{10,... | collective-permute-start | bytes 1179656 | tf_op jit(solution)/shard_map/ppermute | solution.py:352
  42.9 13.0 %collective-permute-start.12 = (bf16[640,1024]{1,0:T(8,128)(2,1)S(1)}, bf16[640,1024]{1,0:T(8,128)(2,1)S(1)}, u32[]{:S(2)}, u32[]{:S(2)}) collective-permute-start(bf16[640,1024]{1,0:T(8,128)(2,1)S(1)} %pack_1.1), channel_id=1, source_target_pairs={{0,1},{1,0},{2,3},{3,2},{4,5},{5,4},{6,7},{7,6},{8,9},{9,8},{10,11... | collective-permute-start | bytes 3932168 | tf_op jit(solution)/shard_map/ppermute | solution.py:355
  42.9 19.5 %collective-permute-start.11 = (bf16[128,1024]{1,0:T(8,128)(2,1)S(1)}, bf16[128,1024]{1,0:T(8,128)(2,1)S(1)}, u32[]{:S(2)}, u32[]{:S(2)}) collective-permute-start(bf16[128,1024]{1,0:T(8,128)(2,1)S(1)} %slice.20), channel_id=1, source_target_pairs={{0,16},{16,0},{1,17},{17,1},{2,18},{18,2},{3,19},{19,3},{4,20},{20... | collective-permute-start | bytes 786440 | tf_op jit(solution)/shard_map/ppermute | solution.py:358
  44.6 18.8 %collective-permute-start.21 = (bf16[576,128]{1,0:T(8,128)(2,1)S(1)}, bf16[576,128]{1,0:T(8,128)(2,1)S(1)}, u32[]{:S(2)}, u32[]{:S(2)}) collective-permute-start(bf16[576,128]{1,0:T(8,128)(2,1)S(1)} %get-tuple-element.200), channel_id=1, source_target_pairs={{0,12},{1,13},{2,14},{3,15},{4,0},{5,1},{6,2},{7,3},{8,4},{9,5},{1... | collective-permute-start | bytes 442376 | tf_op jit(solution)/shard_map/ppermute | solution.py:349
  50.5 12.6 %collective-permute-start.17 = (bf16[128,1024]{1,0:T(8,128)(2,1)S(1)}, bf16[128,1024]{1,0:T(8,128)(2,1)S(1)}, u32[]{:S(2)}, u32[]{:S(2)}) collective-permute-start(bf16[128,1024]{1,0:T(8,128)(2,1)S(1)} %slice.22), channel_id=1, source_target_pairs={{0,16},{16,0},{1,17},{17,1},{2,18},{18,2},{3,19},{19,3},{4,20},{20... | collective-permute-start | bytes 786440 | tf_op jit(solution)/shard_map/ppermute | solution.py:358
  55.9 9.9 %collective-permute-start.20 = (bf16[576,128]{1,0:T(8,128)(2,1)S(1)}, bf16[576,128]{1,0:T(8,128)(2,1)S(1)}, u32[]{:S(2)}, u32[]{:S(2)}) collective-permute-start(bf16[576,128]{1,0:T(8,128)(2,1)S(1)} %get-tuple-element.199), channel_id=1, source_target_pairs={{0,4},{1,5},{2,6},{3,7},{4,8},{5,9},{6,10},{7,11},{8,12},{9,13},{1... | collective-permute-start | bytes 442376 | tf_op jit(solution)/shard_map/ppermute | solution.py:349
  62.5 11.1 %collective-permute-start.22 = (bf16[128,1024]{1,0:T(8,128)(2,1)S(1)}, bf16[128,1024]{1,0:T(8,128)(2,1)S(1)}, u32[]{:S(2)}, u32[]{:S(2)}) collective-permute-start(bf16[128,1024]{1,0:T(8,128)(2,1)S(1)} %slice.23), channel_id=1, source_target_pairs={{0,16},{16,0},{1,17},{17,1},{2,18},{18,2},{3,19},{19,3},{4,20},{20... | collective-permute-start | bytes 786440 | tf_op jit(solution)/shard_map/ppermute | solution.py:358
  63.2 3.8 %collective-permute-start.19 = (bf16[640,1024]{1,0:T(8,128)(2,1)S(1)}, bf16[640,1024]{1,0:T(8,128)(2,1)S(1)}, u32[]{:S(2)}, u32[]{:S(2)}) collective-permute-start(bf16[640,1024]{1,0:T(8,128)(2,1)S(1)} %pack_2.1), channel_id=1, source_target_pairs={{0,1},{1,0},{2,3},{3,2},{4,5},{5,4},{6,7},{7,6},{8,9},{9,8},{10,11... | collective-permute-start | bytes 3932168 | tf_op jit(solution)/shard_map/ppermute | solution.py:355
  66.5 3.7 %collective-permute-start.18 = (bf16[512,1024]{1,0:T(8,128)(2,1)S(1)}, bf16[512,1024]{1,0:T(8,128)(2,1)S(1)}, u32[]{:S(2)}, u32[]{:S(2)}) collective-permute-start(bf16[512,1024]{1,0:T(8,128)(2,1)S(1)} %pack_3.1), channel_id=1, source_target_pairs={{0,1},{1,0},{2,3},{3,2},{4,5},{5,4},{6,7},{7,6},{8,9},{9,8},{10,11... | collective-permute-start | bytes 3145736 | tf_op jit(solution)/shard_map/ppermute | solution.py:355
  66.5 7.0 %collective-permute-start.23 = (f32[256,128]{1,0:T(8,128)S(1)}, f32[256,128]{1,0:T(8,128)S(1)}, u32[]{:S(2)}, u32[]{:S(2)}) collective-permute-start(f32[256,128]{1,0:T(8,128)S(1)} %get-tuple-element.220.refs_0_), channel_id=1, source_target_pairs={{0,2},{1,3},{2,0},{3,1},{4,6},{5,7},{6,4},{7,5},{8,10},{9,11},{10,... | collective-permute-start | bytes 393224 | tf_op jit(solution)/shard_map/ppermute | solution.py:352
  (9 other events, 32.4 us)
